TPU v7x, 256 devices: a whole 4x4x8 slice. The times are simulated.
256 devices in a mesh: gx: 64 (over z, y, core), gy: 4 (over x).
Axes of the slice: x: 4, y: 4, z: 8, core: 2. Of those that a mesh axis runs over, the one named last changes fastest.
Arguments:
- rhs_field: bfloat16 [128, 8, 2, 320, 128], P('gx', 'gy'), may hold values from -6 to 6
- inv_block: bfloat16 [128, 8, 2, 320, 320], P('gx', 'gy'), may hold values from -0.3125 to 0.3125
- face_block: bfloat16 [128, 8, 2, 6, 80, 80], P('gx', 'gy'), may hold values from -0.625 to 0.625
- hang_list: int32 [64, 4, 32, 4], P('gx', 'gy'), may hold values from -1 to 7, as said below
- hang_count: int32 [64, 4], P('gx', 'gy'), may hold values from 8 to 32, as said below
- hang_block: bfloat16 [64, 4, 32, 80, 320], P('gx', 'gy'), may hold values from -0.625 to 0.625
Outputs:
- basis_last: float32 [128, 8, 2, 320, 128], P('gx', 'gy')
- hessenberg: float32 [3, 2, 128], replicated
Inputs may be any that keep to these rules, and one draw needn't show every extreme that they name: `hang_list`: Columns: fine element 0 to 7, face 0 to 5, offset -1, 0 or 1 and never past the ends of gx, owner 0 to 7. `hang_count`: some device holds 32 live couplings in every draw.
All inputs are finite; a program needn't handle non-finite values.
Results may differ from a plain program's by a relative error of at most 0.0065.
Values may be sent and summed in bfloat16 or wider, within the bound.
No kernel may reach another device: no remote copies, remote signals or barrier semaphores. Data moves between devices by JAX's collectives and lax.ppermute only.
A program may use at most 128 MiB of HBM per device.

v0:
```python
import jax
import jax.numpy as jnp
from jax import lax
from jax.sharding import PartitionSpec as P

VARS = 5
NP = 4
BLOCK = 320
FACE = 80
ITERS = 2


def with_halo(cells, sides, width):
    for axis, dim in sides:
        count = lax.axis_size(axis)
        ends = count - 1
        head = lax.slice_in_dim(cells, 0, width, axis=dim)
        tail = lax.slice_in_dim(cells, cells.shape[dim] - width, cells.shape[dim], axis=dim)
        cells = jnp.concatenate(
            [
                lax.ppermute(tail, axis, [(i, (i + 1) % count) for i in range(ends)]),
                cells,
                lax.ppermute(head, axis, [((i + 1) % count, i) for i in range(ends)]),
            ],
            axis=dim,
        )
    return cells


def face_traces(field):
    size_x, size_y, size_z = field.shape[:3]
    columns = field.shape[-1]
    cube = field.reshape(size_x, size_y, size_z, VARS, NP, NP, NP, columns)
    pieces = [
        cube[:, :, :, :, 0],
        cube[:, :, :, :, NP - 1],
        cube[:, :, :, :, :, 0],
        cube[:, :, :, :, :, NP - 1],
        cube[:, :, :, :, :, :, 0],
        cube[:, :, :, :, :, :, NP - 1],
    ]
    return jnp.stack(
        [piece.reshape(size_x, size_y, size_z, VARS * NP * NP, columns) for piece in pieces], axis=3
    )


def place_faces(landed):
    size_x, size_y, size_z = landed[0].shape[:3]
    columns = landed[0].shape[-1]
    total = jnp.zeros((size_x, size_y, size_z, VARS, NP, NP, NP, columns), jnp.float32)
    for face in range(6):
        direction = face // 2
        shape = [VARS, NP, NP, NP]
        shape[1 + direction] = 1
        piece = landed[face].reshape((size_x, size_y, size_z) + tuple(shape) + (columns,))
        widths = [(0, 0)] * 8
        widths[4 + direction] = (0, NP - 1) if face % 2 == 0 else (NP - 1, 0)
        total = total + jnp.pad(piece, widths)
    return total.reshape(size_x, size_y, size_z, VARS * NP**3, columns)


def slide(values, axis, forward):
    length = values.shape[axis]
    widths = [(0, 0)] * values.ndim
    if forward:
        kept = lax.slice_in_dim(values, 0, length - 1, axis=axis)
        widths[axis] = (1, 0)
    else:
        kept = lax.slice_in_dim(values, 1, length, axis=axis)
        widths[axis] = (0, 1)
    return jnp.pad(kept, widths)


def project(blocks, pieces):
    return jnp.einsum("hkj,hkr->hjr", blocks, pieces, preferred_element_type=jnp.float32)


def collect(table, contrib):
    return jnp.einsum("he,hjr->ejr", table, contrib, precision=lax.Precision.HIGHEST)


def per_device(rhs_field, inv_block, face_block, hang_list, hang_count, hang_block):
    span_x, span_y, span_z = rhs_field.shape[:3]
    columns = rhs_field.shape[4]
    elems = span_x * span_y * span_z
    entries = float(elems * BLOCK * lax.axis_size("gx") * lax.axis_size("gy"))
    hang_rows = hang_list[0, 0]
    slots = hang_rows.shape[0]
    live = jnp.arange(slots) < hang_count[0, 0]
    source = hang_rows[:, 0] * 6 + hang_rows[:, 1]
    offset = hang_rows[:, 2]
    owner = hang_rows[:, 3]
    weights = hang_block[0, 0]
    targets = jnp.arange(elems)

    def owner_table(owners, mask):
        return ((owners[:, None] == targets[None, :]) & mask[:, None]).astype(jnp.float32)

    start = rhs_field.astype(jnp.float32)
    start_sum = lax.psum(jnp.sum(start * start, axis=(0, 1, 2, 3)), ("gx", "gy"))
    basis = [start / jnp.sqrt(start_sum / entries + 1e-06)]
    hessenberg = jnp.zeros((ITERS + 1, ITERS, columns), jnp.float32)
    for iteration in range(ITERS):
        field = basis[-1]
        lowered = field.astype(jnp.bfloat16)
        applied = jnp.einsum(
            "xyzij,xyzir->xyzjr", inv_block, lowered, preferred_element_type=jnp.float32
        ).astype(jnp.bfloat16)
        traces = face_traces(applied)
        flux = jnp.einsum(
            "xyzfkl,xyzfkr->xyzflr", face_block, traces, preferred_element_type=jnp.float32
        )
        rim_x = jnp.stack([flux[0, :, :, 0], flux[span_x - 1, :, :, 1]], axis=0)
        near_x = with_halo(rim_x, (("gx", 0),), 1)
        rim_y = jnp.stack([flux[:, 0, :, 2], flux[:, span_y - 1, :, 3]], axis=1)
        near_y = with_halo(rim_y, (("gy", 1),), 1)
        landed = [
            jnp.concatenate([near_x[0:1], flux[:-1, :, :, 1]], axis=0),
            jnp.concatenate([flux[1:, :, :, 0], near_x[3:4]], axis=0),
            jnp.concatenate([near_y[:, 0:1], flux[:, :-1, :, 3]], axis=1),
            jnp.concatenate([flux[:, 1:, :, 2], near_y[:, 3:4]], axis=1),
            slide(flux[:, :, :, 5], 2, True),
            slide(flux[:, :, :, 4], 2, False),
        ]
        result = field + place_faces(landed)
        chosen = traces.reshape(elems * 6, FACE, columns)[source]
        contrib = project(weights, chosen)
        own_part = collect(owner_table(owner, live & (offset == 0)), contrib)
        outgoing = jnp.stack(
            [
                collect(owner_table(owner, live & (offset == -1)), contrib),
                collect(owner_table(owner, live & (offset == 1)), contrib),
            ],
            axis=0,
        )
        near_sums = with_halo(outgoing, (("gx", 0),), 1)
        hanging = own_part + near_sums[0] + near_sums[3]
        image = result + hanging.reshape(span_x, span_y, span_z, BLOCK, columns)
        stacked = jnp.stack(basis)
        local_inner = jnp.sum(stacked * image[None], axis=(1, 2, 3, 4))
        inner = lax.psum(local_inner, ("gx", "gy")) / entries
        image = image - jnp.sum(inner[:, None, None, None, None, :] * stacked, axis=0)
        square = lax.psum(jnp.sum(image * image, axis=(0, 1, 2, 3)), ("gx", "gy"))
        scale = jnp.sqrt(square / entries + 1e-06)
        hessenberg = (
            hessenberg.at[: iteration + 1, iteration]
            .set(inner)
            .at[iteration + 1, iteration]
            .set(scale)
        )
        basis.append(image / scale)
    return (basis[-1], hessenberg)


def solution(mesh):
    in_specs = (
        P("gx", "gy", None, None, None),
        P("gx", "gy", None, None, None),
        P("gx", "gy", None, None, None, None),
        P("gx", "gy", None, None),
        P("gx", "gy"),
        P("gx", "gy", None, None, None),
    )
    out_specs = (P("gx", "gy", None, None, None), P())
    return jax.shard_map(
        per_device, mesh=mesh, in_specs=in_specs, out_specs=out_specs, check_vma=False
    )
```

profile of v0, /device:TPU:1, one launch (start us, length us, event | category | flops | bytes accessed | tf_op | source)
XLA Modules:
  0.0 511.2 jit_solution(4509730630714433893)
XLA Ops:
  2.2 81.4 %psum.35 = f32[128]{0:T(128)S(1)} all-reduce(f32[128]{0:T(128)S(1)} %fusion.26), channel_id=1, replica_groups=mesh['gx'=64,'gy'=4] {'gx','gy'}, use_global_device_ids=true, to_apply=%region_1.0 | all-reduce | flops 128 | bytes 1024 | tf_op jit(solution)/shard_map/psum | solution.py:100
  91.6 4.8 fusion.17
  96.4 3.4 collective-permute-start.5
  99.8 4.8 fusion.14
  104.6 2.7 collective-permute-start.4
  109.2 4.0 collective-permute-start.2
  115.7 3.3 collective-permute-start
  120.6 3.0 collective-permute-done
  125.5 4.9 bitcast_add_fusion.2
  131.5 76.4 %psum.36 = f32[1,128]{1,0:T(1,128)S(1)} all-reduce(f32[1,128]{1,0:T(1,128)S(1)} %bitcast.207), channel_id=1, replica_groups=mesh['gx'=64,'gy'=4] {'gx','gy'}, use_global_device_ids=true, to_apply=%region_3.4 | all-reduce | flops 128 | bytes 1024 | tf_op jit(solution)/shard_map/psum | solution.py:141
  207.9 3.4 multiply_reduce_fusion.3
  211.3 75.0 %psum.37 = f32[128]{0:T(128)S(1)} all-reduce(f32[128]{0:T(128)S(1)} %get-tuple-element.52), channel_id=1, replica_groups=mesh['gx'=64,'gy'=4] {'gx','gy'}, use_global_device_ids=true, to_apply=%region_5.6 | all-reduce | flops 128 | bytes 1024 | tf_op jit(solution)/shard_map/psum | solution.py:143
  286.4 2.8 convolution_convert_fusion
  294.3 2.7 gather_fusion.1
  299.1 5.8 %fusion.23 = f32[1,8,320,128]{3,1,2,0:T(8,128)} fusion(f32[32,320,128]{2,1,0:T(8,128)S(1)} %convolution_bitcast_fusion, s32[32]{0:T(128)S(1)} %get-tuple-element.93, pred[32]{0:T(512)(128)(4,1)S(1)} %get-tuple-element.91), kind=kOutput, calls=%fused_computation.28 | convolution fusion | flops 125829632 | bytes 6553760 | tf_op jit(solution)/shard_map/he,hjr->ejr/dot_general | solution.py:79
  304.9 6.1 %fusion.20 = f32[1,8,320,128]{3,1,2,0:T(8,128)} fusion(f32[32,320,128]{2,1,0:T(8,128)S(1)} %convolution_bitcast_fusion, s32[32]{0:T(128)S(1)} %get-tuple-element.93, pred[32]{0:T(512)(128)(4,1)S(1)} %get-tuple-element.92), kind=kOutput, calls=%fused_computation.27 | convolution fusion | flops 125829632 | bytes 6553760 | tf_op jit(solution)/shard_map/he,hjr->ejr/dot_general | solution.py:79
  312.7 2.6 collective-permute-start.11
  315.3 3.0 collective-permute-start.10
  321.3 4.6 collective-permute-start.8
  326.7 3.0 collective-permute-start.7
  331.7 2.6 collective-permute-start.6
  342.8 6.6 %bitcast_add_fusion = f32[8,320,128]{2,0,1:T(8,128)S(1)} fusion(f32[1,8,320,128]{3,1,2,0:T(8,128)} %collective-permute-done.11, f32[1,8,320,128]{3,1,2,0:T(8,128)} %collective-permute-done.10, f32[32,320,128]{2,1,0:T(8,128)S(1)} %copy-done.2, s32[32]{0:T(128)S(1)} %get-tuple-element.93, pred[32]{0:T(512)(128)(4,1)S(1)} %get-tuple-element.90), kind=kOutput, calls=%fused_computation.54 | convolution fusion | flops 126484992 | bytes 9175200 | tf_op jit(solution)/shard_map/he,hjr->ejr/dot_general | solution.py:79
  351.8 80.2 %psum.38 = f32[2,128]{1,0:T(2,128)S(1)} all-reduce(f32[2,128]{1,0:T(2,128)S(1)} %multiply_reduce_fusion.1), channel_id=1, replica_groups=mesh['gx'=64,'gy'=4] {'gx','gy'}, use_global_device_ids=true, to_apply=%region_7.8 | all-reduce | flops 256 | bytes 2048 | tf_op jit(solution)/shard_map/psum | solution.py:141
  434.2 73.4 %psum.39 = f32[128]{0:T(128)S(1)} all-reduce(f32[128]{0:T(128)S(1)} %get-tuple-element.50), channel_id=1, replica_groups=mesh['gx'=64,'gy'=4] {'gx','gy'}, use_global_device_ids=true, to_apply=%region_10.11 | all-reduce | flops 128 | bytes 1024 | tf_op jit(solution)/shard_map/psum | solution.py:143
  (137 shorter events, 48.3 us)
Async XLA Ops:
  0.6 88.9 %copy-start = (bf16[1,1,32,80,320]{4,3,2,1,0:T(8,128)(2,1)S(1)}, bf16[1,1,32,80,320]{4,3,2,1,0:T(8,128)(2,1)}, u32[]{:S(2)}) copy-start(bf16[1,1,32,80,320]{4,3,2,1,0:T(8,128)(2,1)} %param.19) | copy-start | bytes 4915204
  96.4 29.1 %collective-permute-start.5 = (f32[1,8,320,128]{3,1,2,0:T(8,128)S(1)}, f32[1,8,320,128]{3,1,2,0:T(8,128)S(1)}, u32[]{:S(2)}, u32[]{:S(2)}) collective-permute-start(f32[1,8,320,128]{3,1,2,0:T(8,128)S(1)} %fusion.17), channel_id=1, source_target_pairs={{4,0},{8,4},{12,8},{16,12},{20,16},{24,20},{28,24},{32,28},{36,32}... | collective-permute-start | bytes 3932168 | tf_op jit(solution)/shard_map/ppermute | solution.py:23
  99.8 7.5 %copy-start.10 = (bf16[2,2,2,6,80,80]{5,4,3,2,1,0:T(8,128)(2,1)S(1)}, bf16[2,2,2,6,80,80]{5,4,3,2,1,0:T(8,128)(2,1)}, u32[]{:S(2)}) copy-start(bf16[2,2,2,6,80,80]{5,4,3,2,1,0:T(8,128)(2,1)} %param.16) | copy-start | bytes 1843204
  104.6 20.9 %collective-permute-start.4 = (f32[1,8,320,128]{3,1,2,0:T(8,128)S(1)}, f32[1,8,320,128]{3,1,2,0:T(8,128)S(1)}, u32[]{:S(2)}, u32[]{:S(2)}) collective-permute-start(f32[1,8,320,128]{3,1,2,0:T(8,128)S(1)} %fusion.14), channel_id=1, source_target_pairs={{0,4},{4,8},{8,12},{12,16},{16,20},{20,24},{24,28},{28,32},{32,36}... | collective-permute-start | bytes 3932168 | tf_op jit(solution)/shard_map/ppermute | solution.py:21
  107.9 7.8 %collective-permute-start.3 = (f32[2,1,2,80,128]{4,3,2,0,1:T(8,128)S(1)}, f32[2,1,2,80,128]{4,3,2,0,1:T(8,128)S(1)}, u32[]{:S(2)}, u32[]{:S(2)}) collective-permute-start(f32[2,1,2,80,128]{4,3,2,0,1:T(8,128)S(1)} %get-tuple-element.71), channel_id=1, source_target_pairs={{1,0},{2,1},{3,2},{5,4},{6,5},{7,6},{9,8},{10,9},{11,10},{13,12},{... | collective-permute-start | bytes 491528 | tf_op jit(solution)/shard_map/ppermute | solution.py:23
  109.2 11.2 %collective-permute-start.2 = (f32[2,1,2,80,128]{4,3,2,0,1:T(8,128)S(1)}, f32[2,1,2,80,128]{4,3,2,0,1:T(8,128)S(1)}, u32[]{:S(2)}, u32[]{:S(2)}) collective-permute-start(f32[2,1,2,80,128]{4,3,2,0,1:T(8,128)S(1)} %get-tuple-element.70), channel_id=1, source_target_pairs={{0,1},{1,2},{2,3},{4,5},{5,6},{6,7},{8,9},{9,10},{10,11},{12,13},{... | collective-permute-start | bytes 491528 | tf_op jit(solution)/shard_map/ppermute | solution.py:21
  113.2 7.3 %collective-permute-start.1 = (f32[1,2,2,80,128]{4,3,2,1,0:T(8,128)S(1)}, f32[1,2,2,80,128]{4,3,2,1,0:T(8,128)S(1)}, u32[]{:S(2)}, u32[]{:S(2)}) collective-permute-start(f32[1,2,2,80,128]{4,3,2,1,0:T(8,128)S(1)} %get-tuple-element.67), channel_id=1, source_target_pairs={{4,0},{8,4},{12,8},{16,12},{20,16},{24,20},{28,24},{32,28},{36,32}... | collective-permute-start | bytes 491528 | tf_op jit(solution)/shard_map/ppermute | solution.py:23
  115.7 7.9 %collective-permute-start = (f32[1,2,2,80,128]{4,3,2,1,0:T(8,128)S(1)}, f32[1,2,2,80,128]{4,3,2,1,0:T(8,128)S(1)}, u32[]{:S(2)}, u32[]{:S(2)}) collective-permute-start(f32[1,2,2,80,128]{4,3,2,1,0:T(8,128)S(1)} %get-tuple-element.66), channel_id=1, source_target_pairs={{0,4},{4,8},{8,12},{12,16},{16,20},{20,24},{24,28},{28,32},{32,36}... | collective-permute-start | bytes 491528 | tf_op jit(solution)/shard_map/ppermute | solution.py:21
  125.5 5.0 copy-start.4
  125.5 4.9 copy-start.8
  299.0 5.8 %copy-start.1 = (f32[32,320,128]{2,1,0:T(8,128)}, f32[32,320,128]{2,1,0:T(8,128)S(1)}, u32[]{:S(2)}) copy-start(f32[32,320,128]{2,1,0:T(8,128)S(1)} %convolution_bitcast_fusion) | copy-start | bytes 15728644
  304.9 6.1 %copy-start.11 = (bf16[2,2,2,6,80,80]{5,4,3,2,1,0:T(8,128)(2,1)S(1)}, bf16[2,2,2,6,80,80]{5,4,3,2,1,0:T(8,128)(2,1)}, u32[]{:S(2)}) copy-start(bf16[2,2,2,6,80,80]{5,4,3,2,1,0:T(8,128)(2,1)} %param.16) | copy-start | bytes 1843204
  312.7 29.4 %collective-permute-start.11 = (f32[1,8,320,128]{3,1,2,0:T(8,128)}, f32[1,8,320,128]{3,1,2,0:T(8,128)}, u32[]{:S(2)}, u32[]{:S(2)}) collective-permute-start(f32[1,8,320,128]{3,1,2,0:T(8,128)} %fusion.23), channel_id=1, source_target_pairs={{4,0},{8,4},{12,8},{16,12},{20,16},{24,20},{28,24},{32,28},{36,32}... | collective-permute-start | bytes 3932168 | tf_op jit(solution)/shard_map/ppermute | solution.py:23
  315.3 26.8 %collective-permute-start.10 = (f32[1,8,320,128]{3,1,2,0:T(8,128)}, f32[1,8,320,128]{3,1,2,0:T(8,128)}, u32[]{:S(2)}, u32[]{:S(2)}) collective-permute-start(f32[1,8,320,128]{3,1,2,0:T(8,128)} %fusion.20), channel_id=1, source_target_pairs={{0,4},{4,8},{8,12},{12,16},{16,20},{20,24},{24,28},{28,32},{32,36}... | collective-permute-start | bytes 3932168 | tf_op jit(solution)/shard_map/ppermute | solution.py:21
  319.0 12.1 %collective-permute-start.9 = (f32[2,1,2,80,128]{4,3,2,0,1:T(8,128)S(1)}, f32[2,1,2,80,128]{4,3,2,0,1:T(8,128)S(1)}, u32[]{:S(2)}, u32[]{:S(2)}) collective-permute-start(f32[2,1,2,80,128]{4,3,2,0,1:T(8,128)S(1)} %get-tuple-element.61), channel_id=1, source_target_pairs={{1,0},{2,1},{3,2},{5,4},{6,5},{7,6},{9,8},{10,9},{11,10},{13,12},{... | collective-permute-start | bytes 491528 | tf_op jit(solution)/shard_map/ppermute | solution.py:23
  321.3 15.9 %collective-permute-start.8 = (f32[2,1,2,80,128]{4,3,2,0,1:T(8,128)}, f32[2,1,2,80,128]{4,3,2,0,1:T(8,128)}, u32[]{:S(2)}, u32[]{:S(2)}) collective-permute-start(f32[2,1,2,80,128]{4,3,2,0,1:T(8,128)} %get-tuple-element.60), channel_id=1, source_target_pairs={{0,1},{1,2},{2,3},{4,5},{5,6},{6,7},{8,9},{9,10},{10,11},{12,13},{... | collective-permute-start | bytes 491528 | tf_op jit(solution)/shard_map/ppermute | solution.py:21
  326.7 11.6 %collective-permute-start.7 = (f32[1,2,2,80,128]{4,3,2,1,0:T(8,128)}, f32[1,2,2,80,128]{4,3,2,1,0:T(8,128)}, u32[]{:S(2)}, u32[]{:S(2)}) collective-permute-start(f32[1,2,2,80,128]{4,3,2,1,0:T(8,128)} %get-tuple-element.57), channel_id=1, source_target_pairs={{4,0},{8,4},{12,8},{16,12},{20,16},{24,20},{28,24},{32,28},{36,32}... | collective-permute-start | bytes 491528 | tf_op jit(solution)/shard_map/ppermute | solution.py:23
  331.7 7.5 %collective-permute-start.6 = (f32[1,2,2,80,128]{4,3,2,1,0:T(8,128)}, f32[1,2,2,80,128]{4,3,2,1,0:T(8,128)}, u32[]{:S(2)}, u32[]{:S(2)}) collective-permute-start(f32[1,2,2,80,128]{4,3,2,1,0:T(8,128)} %get-tuple-element.56), channel_id=1, source_target_pairs={{0,4},{4,8},{8,12},{12,16},{16,20},{20,24},{24,28},{28,32},{32,36}... | collective-permute-start | bytes 491528 | tf_op jit(solution)/shard_map/ppermute | solution.py:21
  336.0 4.3 copy-start.12
  336.0 4.3 copy-start.13
  336.0 4.3 copy-start.14
  336.0 4.3 copy-start.15
  336.0 4.3 copy-start.16
  342.1 7.3 %copy-start.9 = (f32[2,2,2,320,128]{4,3,2,1,0:T(8,128)S(1)}, f32[2,2,2,320,128]{4,3,2,1,0:T(8,128)}, u32[]{:S(2)}) copy-start(f32[2,2,2,320,128]{4,3,2,1,0:T(8,128)} %get-tuple-element.53) | copy-start | bytes 3932164
  (8 other events, 9.9 us)
where the time goes:
time: 519 us; the launch traced here: 511 us
  blocking collectives  386 us (74%)
  matrix products  44.6 us (9%)
  starting transfers between devices  33.9 us (7%)
  local copies, waits for them, and re-layouts  28.8 us (6%)
  other arithmetic  11.6 us (2%)
    psum x2, blocking collectives, per_device(): inner = lax.psum(local_inner, ('gx', 'gy')) / entries  157 us
    psum x2, blocking collectives, per_device(): square = lax.psum(jnp.sum(image * image, axis=(0, 1, 2, 3)), ('gx', 'gy'))  148 us
    psum x1, blocking collectives, per_device(): lax.psum(jnp.sum(start * start, axis=(0, 1, 2, 3)), ('gx', 'gy'))  81.4 us
    dot_general x6, matrix products, collect(): jnp.einsum('he,hjr->ejr', table, contrib, precision=lax.Precision.HIGHEST)  33 us
    ppermute x6, starting transfers between devices, with_halo(): lax.ppermute(tail, axis, [(i, (i + 1) % count) for i in range(ends)])  20.2 us
    ppermute x6, starting transfers between devices, with_halo(): lax.ppermute(head, axis, [((i + 1) % count, i) for i in range(ends)])  13.8 us
  transfers between devices with their start and end apart: 12, of which 2 were waited for; matrix products, arithmetic and copies ran while one was open for 4% of the time, Pallas kernels for 0%

commit v1 on v0

v1 whole, which is shorter than its diff:
```python
import functools

import jax
import jax.numpy as jnp
from jax import lax
from jax.experimental import pallas as pl
from jax.experimental.pallas import tpu as pltpu
from jax.sharding import PartitionSpec as P

VARS = 5
NP = 4
BLOCK = 320
FACE = 80
ELEMS = 8
RHS = 128
HANG = 32
EPS = 1e-6
GROUP = 2
VMEM_LIMIT = 40 * 1024 * 1024

TN = (((0,), (0,)), ((), ()))
NN = (((1,), (0,)), ((), ()))


def mm(a, b, dims):
    return lax.dot_general(a, b, dims, preferred_element_type=jnp.float32)


def select_matrix():
    row = lax.broadcasted_iota(jnp.int32, (4 * FACE, BLOCK), 0)
    col = lax.broadcasted_iota(jnp.int32, (4 * FACE, BLOCK), 1)
    group = (
        (row >= FACE).astype(jnp.int32)
        + (row >= 2 * FACE).astype(jnp.int32)
        + (row >= 3 * FACE).astype(jnp.int32)
    )
    entry = row - group * FACE
    along_b = lax.shift_right_logical(entry, 2) * 16 + (entry & 3) + 12 * (group & 1)
    along_c = entry * 4 + 3 * (group & 1)
    source = jnp.where(group < 2, along_b, along_c)
    return (source == col).astype(jnp.float32).astype(jnp.bfloat16)


def fill_traces(lowered, inv_ref, tr_ref):
    pick = select_matrix()
    for e in range(ELEMS):
        applied = mm(inv_ref[e], lowered(e), TN).astype(jnp.bfloat16)
        for v in range(VARS):
            tr_ref[6 * e, 16 * v : 16 * v + 16, :] = applied[64 * v : 64 * v + 16]
            tr_ref[6 * e + 1, 16 * v : 16 * v + 16, :] = applied[64 * v + 48 : 64 * v + 64]
        others = mm(pick, applied, NN).astype(jnp.bfloat16)
        for g in range(4):
            tr_ref[6 * e + 2 + g] = others[FACE * g : FACE * g + FACE]


def flux(face_ref, tr_ref, e, f):
    return mm(face_ref[6 * e + f], tr_ref[6 * e + f], TN)


def add_face(acc, e, f, values, tmp):
    end = f % 2
    if f < 2:
        for v in range(VARS):
            first = 64 * v + 48 * end
            acc[e, first : first + 16, :] += values[16 * v : 16 * v + 16]
    elif f < 4:
        tmp[...] = values
        for c in range(NP):
            at = pl.ds(12 * end + c, 20, stride=16)
            acc[e, at, :] += tmp[pl.ds(c, 20, stride=4), :]
    else:
        acc[e, pl.ds(3 * end, FACE, stride=4), :] += values


def add_slots(acc, wanted, sign, list_ref, count_ref, hang_ref, tr_ref, slot_ref):
    live = count_ref[0]

    def look(h, n):
        slot_ref[n] = h
        hit = jnp.logical_and(list_ref[h, 2] * sign == wanted, h < live)
        return n + hit.astype(jnp.int32)

    n = lax.fori_loop(0, HANG, look, jnp.int32(0))
    for i in range(GROUP):
        slot_ref[n + i] = 0

    def work(g, carry):
        parts = []
        for i in range(GROUP):
            k = g * GROUP + i
            h = slot_ref[k]
            source = list_ref[h, 0] * 6 + list_ref[h, 1]
            target = jnp.where(k < n, list_ref[h, 3], ELEMS)
            parts.append((target, mm(hang_ref[h], tr_ref[source], TN)))
        for target, part in parts:
            acc[target] += part
        return carry

    lax.fori_loop(0, (n + GROUP - 1) // GROUP, work, 0)


def core_and_row():
    return lax.axis_index("c"), lax.axis_index("x") % 2


def outgoing_x(side, acc, face_ref, tr_ref):
    for n in range(4):
        acc_e = n + 4 * (1 - side)
        add_face(acc, acc_e, 1 - side, flux(face_ref, tr_ref, n + 4 * side, side), None)


def cross_part(acc, out_ref, list_ref, count_ref, face_ref, hang_ref, tr_ref, slot_ref, wanted):
    core, _ = core_and_row()
    acc[...] = jnp.zeros_like(acc)
    side = core if wanted == 1 else 1 - core
    for s in range(2):

        @pl.when(side == s)
        def _(s=s):
            outgoing_x(s, acc, face_ref, tr_ref)

    add_slots(acc, wanted, 2 * core - 1, list_ref, count_ref, hang_ref, tr_ref, slot_ref)
    out_ref[...] = acc[0:ELEMS].astype(out_ref.dtype)


def first_kernel(list_ref, count_ref, rhs_ref, inv_ref, face_ref, hang_ref, tr_ref, cross_ref, acc, slot_ref):
    fill_traces(lambda e: rhs_ref[e], inv_ref, tr_ref)
    cross_part(acc, cross_ref, list_ref, count_ref, face_ref, hang_ref, tr_ref, slot_ref, 1)


def side_kernel(list_ref, count_ref, face_ref, hang_ref, tr_ref, chip_ref, ya_ref, yb_ref, acc, slot_ref):
    _, odd = core_and_row()
    for parity in range(2):

        @pl.when(odd == parity)
        def _(parity=parity):
            for x in range(2):
                for z in range(2):
                    up = 4 * x + 2 + z
                    down = 4 * x + z
                    refs = (ya_ref, yb_ref) if parity == 0 else (yb_ref, ya_ref)
                    refs[0][2 * x + z] = flux(face_ref, tr_ref, up, 3)
                    refs[1][2 * x + z] = flux(face_ref, tr_ref, down, 2)

    cross_part(acc, chip_ref, list_ref, count_ref, face_ref, hang_ref, tr_ref, slot_ref, -1)


def own_body(list_ref, count_ref, face_ref, hang_ref, tr_ref, own_ref, acc, tmp, slot_ref):
    acc[...] = jnp.zeros_like(acc)
    for direction, step in ((0, 4), (1, 2), (2, 1)):
        for e in range(ELEMS):
            low, high = 2 * direction, 2 * direction + 1
            if e & step:
                add_face(acc, e - step, high, flux(face_ref, tr_ref, e, low), tmp)
            else:
                add_face(acc, e + step, low, flux(face_ref, tr_ref, e, high), tmp)
    core, _ = core_and_row()
    add_slots(acc, 0, 1, list_ref, count_ref, hang_ref, tr_ref, slot_ref)
    own_ref[...] = acc[0:ELEMS]


def own_kernel(list_ref, count_ref, face_ref, hang_ref, tr_ref, own_ref, acc, tmp, slot_ref):
    own_body(list_ref, count_ref, face_ref, hang_ref, tr_ref, own_ref, acc, tmp, slot_ref)


def own_gram_kernel(
    list_ref, count_ref, face_ref, hang_ref, tr_ref, rhs_ref, w1_ref, own_ref, gram_ref, acc, tmp, slot_ref
):
    own_body(list_ref, count_ref, face_ref, hang_ref, tr_ref, own_ref, acc, tmp, slot_ref)
    zero = jnp.zeros((8, RHS), jnp.float32)
    g00, g01, g11 = zero, zero, zero
    for e in range(ELEMS):
        a = rhs_ref[e].astype(jnp.float32).reshape(BLOCK // 8, 8, RHS)
        b = w1_ref[e].reshape(BLOCK // 8, 8, RHS)
        g00 += jnp.sum(a * a, axis=0)
        g01 += jnp.sum(a * b, axis=0)
        g11 += jnp.sum(b * b, axis=0)
    rows = [jnp.sum(g, axis=0, keepdims=True) for g in (g00, g01, g11)]
    gram_ref[...] = jnp.concatenate(rows + [jnp.zeros((5, RHS), jnp.float32)], axis=0)


def land(w_ref, own_ref, cross_ref, chip_ref, ya_ref, yb_ref):
    w_ref[...] = own_ref[...] + cross_ref[...].astype(jnp.float32) + chip_ref[...].astype(jnp.float32)
    _, odd = core_and_row()
    for parity in range(2):

        @pl.when(odd == parity)
        def _(parity=parity):
            from_up, from_down = (ya_ref, yb_ref) if parity == 0 else (yb_ref, ya_ref)
            for x in range(2):
                for z in range(2):
                    n = 2 * x + z
                    for c in range(NP):
                        rows = pl.ds(c, 20, stride=4)
                        high = pl.ds(12 + c, 20, stride=16)
                        low = pl.ds(c, 20, stride=16)
                        w_ref[4 * x + 2 + z, high, :] += from_up[n, rows, :]
                        w_ref[4 * x + z, low, :] += from_down[n, rows, :]


def second_kernel(
    list_ref, count_ref, own_ref, in_cross, in_chip, in_ya, in_yb, inv_ref, face_ref, hang_ref,
    w_ref, tr_ref, cross_ref, acc, slot_ref,
):
    land(w_ref, own_ref, in_cross, in_chip, in_ya, in_yb)
    fill_traces(lambda e: w_ref[e].astype(jnp.bfloat16), inv_ref, tr_ref)
    cross_part(acc, cross_ref, list_ref, count_ref, face_ref, hang_ref, tr_ref, slot_ref, 1)


def last_kernel(own_ref, in_cross, in_chip, in_ya, in_yb, rhs_ref, w1_ref, early_ref, w_ref, gram_ref):
    land(w_ref, own_ref, in_cross, in_chip, in_ya, in_yb)
    zero = jnp.zeros((8, RHS), jnp.float32)
    g02, g12, g22 = zero, zero, zero
    for e in range(ELEMS):
        a = rhs_ref[e].astype(jnp.float32).reshape(BLOCK // 8, 8, RHS)
        b = w1_ref[e].reshape(BLOCK // 8, 8, RHS)
        c = w_ref[e].reshape(BLOCK // 8, 8, RHS)
        g02 += jnp.sum(a * c, axis=0)
        g12 += jnp.sum(b * c, axis=0)
        g22 += jnp.sum(c * c, axis=0)
    rows = [jnp.sum(g, axis=0, keepdims=True) for g in (g02, g12, g22)]
    gram_ref[...] = jnp.concatenate(
        [early_ref[0:3]] + rows + [jnp.zeros((2, RHS), jnp.float32)], axis=0
    )


def combine_kernel(entries, sums_ref, rhs_ref, w1_ref, w2_ref, out_ref, hess_ref):
    gram = jnp.sum(sums_ref[...], axis=0) * (1.0 / entries)
    g00, g01, g11, g02, g12, g22 = (gram[i : i + 1] for i in range(6))
    norm0 = g00 + EPS
    size0 = jnp.sqrt(norm0)
    h11 = (g00 + g01) / norm0
    c1 = (EPS - g01) / norm0
    square1 = jnp.maximum(g11 + 2.0 * c1 * g01 + c1 * c1 * g00, 0.0) / norm0 + EPS
    h21 = jnp.sqrt(square1)
    s2 = 1.0 / (size0 * h21)
    ratio = (g02 + c1 * g01 + EPS * h11) / norm0
    h12 = ratio * s2 * size0
    q = EPS / square1 - s2 * s2 * (g12 + c1 * (g11 + g02 + c1 * g01))
    h22 = 1.0 - q
    alpha = c1 + q
    beta = c1 * q - ratio
    total = g22 + 2.0 * (alpha * g12 + beta * g02 + alpha * beta * g01)
    total = total + alpha * alpha * g11 + beta * beta * g00
    h32 = jnp.sqrt(s2 * s2 * jnp.maximum(total, 0.0) + EPS)
    zero = jnp.zeros_like(h11)
    for i, row in enumerate(((h11, h12), (h21, h22), (zero, h32))):
        hess_ref[i] = jnp.concatenate(row, axis=0)
    k2 = s2 / h32
    k1 = k2 * alpha
    k0 = k2 * beta
    for e in range(ELEMS):
        out_ref[e] = k2 * w2_ref[e] + k1 * w1_ref[e] + k0 * rhs_ref[e].astype(jnp.float32)


def shape(dims, dtype=jnp.float32):
    return jax.ShapeDtypeStruct(dims, dtype)


FIELD = (ELEMS, BLOCK, RHS)
TRACES = (6 * ELEMS, FACE, RHS)
SIDE = (4, FACE, RHS)
SMEM = pl.BlockSpec(memory_space=pltpu.SMEM)
VMEM = pl.BlockSpec(memory_space=pltpu.VMEM)


def call(kernel, n_smem, n_vmem, outs, scratch, flops, moved):
    return pl.pallas_call(
        kernel,
        out_shape=outs,
        in_specs=[SMEM] * n_smem + [VMEM] * n_vmem,
        out_specs=[VMEM] * len(outs),
        scratch_shapes=scratch,
        compiler_params=pltpu.CompilerParams(vmem_limit_bytes=VMEM_LIMIT),
        cost_estimate=pl.CostEstimate(flops=flops, bytes_accessed=moved, transcendentals=0),
    )


def per_device(entries, pairs, rhs_field, inv_block, face_block, hang_list, hang_count, hang_block):
    rhs = rhs_field.reshape(FIELD)
    inv = inv_block.reshape(ELEMS, BLOCK, BLOCK)
    face = face_block.reshape(6 * ELEMS, FACE, FACE)
    hang = hang_block.reshape(HANG, FACE, BLOCK)
    rows = hang_list.reshape(HANG, 4)
    count = hang_count.reshape(1)
    acc = pltpu.VMEM((ELEMS + 1, BLOCK, RHS), jnp.float32)
    tmp = pltpu.VMEM((FACE, RHS), jnp.float32)
    slots = pltpu.SMEM((HANG + 8,), jnp.int32)
    bf16 = jnp.bfloat16
    million = 10**6

    def exchange(traces, cross, own_call):
        in_cross = lax.ppermute(cross, ("z", "y", "c"), pairs["cross"])
        chip, ya, yb = call(
            side_kernel, 2, 3, [shape(FIELD, bf16), shape(SIDE), shape(SIDE)], [acc, slots],
            100 * million, 4 * million,
        )(rows, count, face, hang, traces)
        in_chip = lax.ppermute(chip, "c", [(0, 1), (1, 0)])
        in_ya = lax.ppermute(ya, "x", pairs["even"])
        in_yb = lax.ppermute(yb, "x", pairs["odd"])
        return own_call(traces), (in_cross, in_chip, in_ya, in_yb)

    traces, cross = call(
        first_kernel, 2, 4, [shape(TRACES, bf16), shape(FIELD, bf16)], [acc, slots],
        300 * million, 6 * million,
    )(rows, count, rhs, inv, face, hang)

    def own_first(traces):
        return call(
            own_kernel, 2, 3, [shape(FIELD)], [acc, tmp, slots], 100 * million, 6 * million
        )(rows, count, face, hang, traces)[0]

    own, arrived = exchange(traces, cross, own_first)
    w1, traces, cross = call(
        second_kernel, 2, 8, [shape(FIELD), shape(TRACES, bf16), shape(FIELD, bf16)], [acc, slots],
        300 * million, 8 * million,
    )(rows, count, own, *arrived, inv, face, hang)

    def own_second(traces):
        return call(
            own_gram_kernel, 2, 5, [shape(FIELD), shape((8, RHS))], [acc, tmp, slots],
            100 * million, 6 * million,
        )(rows, count, face, hang, traces, rhs, w1)

    (own, early), arrived = exchange(traces, cross, own_second)
    w2, gram = call(
        last_kernel, 0, 8, [shape(FIELD), shape((8, RHS))], [], 10 * million, 8 * million
    )(own, *arrived, rhs, w1, early)

    gram = gram + lax.ppermute(gram, "c", [(0, 1), (1, 0)])
    chips = lax.axis_size(("z", "y", "x"))
    sums = lax.all_to_all(jnp.broadcast_to(gram, (chips, 8, RHS)), ("z", "y", "x"), 0, 0)
    last, hessenberg = call(
        functools.partial(combine_kernel, entries), 0, 4, [shape(FIELD), shape((3, 2, RHS))], [],
        10 * million, 6 * million,
    )(sums, rhs, w1, w2)
    return last.reshape(rhs_field.shape), hessenberg


def solution(mesh):
    count_x, count_y = mesh.shape["gx"], mesh.shape["gy"]
    grid = jax.sharding.Mesh(
        mesh.devices.reshape(count_x // 8, 4, 2, count_y), ("z", "y", "c", "x")
    )
    pairs = {"cross": [], "even": [], "odd": []}
    for i in range(1, count_x - 1, 2):
        pairs["cross"] += [(i, i + 1), (i + 1, i)]
    for j in range(count_y - 1):
        pairs["odd" if j % 2 else "even"] += [(j, j + 1), (j + 1, j)]
    long = ("z", "y", "c")
    in_specs = (P(long, "x"),) * 6
    out_specs = (P(long, "x"), P())
    entries = float(ELEMS * BLOCK * count_x * count_y)
    return jax.shard_map(
        functools.partial(per_device, entries, pairs),
        mesh=grid, in_specs=in_specs, out_specs=out_specs, check_vma=False,
    )
```

time: 519 us -> 87.3 us (0.17); the launches traced: 511 us -> 86.3 us
  blocking collectives: 386 us -> 36.5 us
  matrix products: 44.6 us -> 0 us
  Pallas kernels: 0 us -> 24.4 us
  local copies, waits for them, and re-layouts: 28.8 us -> 6.19 us
  starting transfers between devices: 33.9 us -> 15 us
  other arithmetic: 11.6 us -> 0.01 us
    psum x5 -> x0, blocking collectives: 386 us -> none  [the longest x2 157 us: per_device(): inner = lax.psum(local_inner, ('gx', 'gy')) / entries]
    dot_general x12 -> x0, matrix products: 44.6 us -> none  [the longest x6 33 us: collect(): jnp.einsum('he,hjr->ejr', table, contrib, precision=lax.Precision.HIGHEST)]
    all_to_all x0 -> x1, blocking collectives: none -> 36.5 us  [per_device(): lax.all_to_all(jnp.broadcast_to(gram, (chips, 8, RHS)), ('z', 'y', 'x'),...]
    pallas_call x0 -> x8, Pallas kernels: none -> 24.4 us  [the longest x1 5.76 us: per_device(): call(second_kernel, 2, 8, [shape(FIELD), shape(TRACES, bf16), shape(FIELD...]
    ppermute x12 -> x9, starting transfers between devices: 33.9 us -> 15 us  [the longest x2 7.42 us: exchange(): in_cross = lax.ppermute(cross, ('z', 'y', 'c'), pairs['cross'])]
    reduce_sum x5 -> x0, other arithmetic: 7.7 us -> none  [the longest x2 3.73 us: per_device(): square = lax.psum(jnp.sum(image * image, axis=(0, 1, 2, 3)), ('gx', 'gy'))]
    concatenate x16 -> x0, local copies, waits for them, and re-layouts: 7.44 us -> none  [the longest x4 2.26 us: per_device(): jnp.concatenate([near_y[:, 0:1], flux[:, :-1, :, 3]], axis=1)]
  transfers between devices with their start and end apart: 12 -> 9, of which waited for: 2 -> 4; matrix products, arithmetic and copies ran while one was open for 4% -> 0% of each run, Pallas kernels for 0% -> 13%
where the time goes in v1:
time: 87.3 us; the launch traced here: 86.3 us
  blocking collectives  36.5 us (42%)
  Pallas kernels  24.4 us (28%)
  starting transfers between devices  15 us (17%)
  local copies, waits for them, and re-layouts  6.19 us (7%)
  waiting for transfers between devices  2.75 us (3%)
  between operations  1.42 us (2%)
    all_to_all x1, blocking collectives, per_device(): lax.all_to_all(jnp.broadcast_to(gram, (chips, 8, RHS)), ('z', 'y', 'x'),...  36.5 us
    ppermute x2, starting transfers between devices, exchange(): in_cross = lax.ppermute(cross, ('z', 'y', 'c'), pairs['cross'])  7.42 us
    pallas_call x1, Pallas kernels, per_device(): call(second_kernel, 2, 8, [shape(FIELD), shape(TRACES, bf16), shape(FIELD...  5.76 us
    unnamed x14, local copies, waits for them, and re-layouts  5.39 us
    pallas_call x1, Pallas kernels, per_device(): call(first_kernel, 2, 4, [shape(TRACES, bf16), shape(FIELD, bf16)], [acc,...  5.38 us
    pallas_call x2, Pallas kernels, exchange(): call(side_kernel, 2, 3, [shape(FIELD, bf16), shape(SIDE), shape(SIDE)], [...  5.33 us
    ppermute x2, starting transfers between devices, exchange(): in_ya = lax.ppermute(ya, 'x', pairs['even'])  4.44 us
    pallas_call x1, Pallas kernels, own_second(): call(own_gram_kernel, 2, 5, [shape(FIELD), shape((8, RHS))], [acc, tmp, s...  2.99 us
  transfers between devices with their start and end apart: 9, of which 4 were waited for; matrix products, arithmetic and copies ran while one was open for 0% of the time, Pallas kernels for 13%

profile of v1, /device:TPU:1, one launch (start us, length us, event | category | flops | bytes accessed | tf_op | source)
XLA Modules:
  0.0 86.3 jit_solution(1521245741268931250)
XLA Ops:
  1.3 0.8 copy.12.list_ref
  2.0 1.5 %copy-done = bf16[1,1,32,80,320]{4,3,2,1,0:T(8,128)(2,1)S(1)} copy-done((bf16[1,1,32,80,320]{4,3,2,1,0:T(8,128)(2,1)S(1)}, bf16[1,1,32,80,320]{4,3,2,1,0:T(8,128)(2,1)}, u32[]{:S(2)}) %copy-start) | copy-done | bytes 1638424
  3.6 1.2 %copy-done.2 = bf16[2,2,2,6,80,80]{5,4,3,2,1,0:T(8,128)(2,1)S(1)} copy-done((bf16[2,2,2,6,80,80]{5,4,3,2,1,0:T(8,128)(2,1)S(1)}, bf16[2,2,2,6,80,80]{5,4,3,2,1,0:T(8,128)(2,1)}, u32[]{:S(2)}) %copy-start.2) | copy-done | bytes 614424
  4.8 1.1 %copy-done.4 = bf16[2,2,2,320,128]{4,3,2,1,0:T(8,128)(2,1)S(1)} copy-done((bf16[2,2,2,320,128]{4,3,2,1,0:T(8,128)(2,1)S(1)}, bf16[2,2,2,320,128]{4,3,2,1,0:T(8,128)(2,1)}, u32[]{:S(2)}) %copy-start.4) | copy-done | bytes 655384
  5.9 1.5 %copy-done.6 = bf16[2,2,2,320,320]{4,3,2,1,0:T(8,128)(2,1)S(1)} copy-done((bf16[2,2,2,320,320]{4,3,2,1,0:T(8,128)(2,1)S(1)}, bf16[2,2,2,320,320]{4,3,2,1,0:T(8,128)(2,1)}, u32[]{:S(2)}) %copy-start.6) | copy-done | bytes 1638424
  7.4 5.4 %shard_map.77 = (bf16[48,80,128]{2,1,0:T(8,128)(2,1)S(1)}, bf16[8,320,128]{2,1,0:T(8,128)(2,1)S(1)}) custom-call(s32[32,4]{1,0:T(8,128)S(1)} %copy.12.list_ref, s32[1]{0:T(128)} %bitcast.7.count_ref, bf16[8,320,128]{2,1,0:T(8,128)(2,1)S(1)} %bitcast.25, bf16[8,320,320]{2,1,0:T(8,128)(2,1)S(1)} %bitcast.29, bf16[48,80,80]{2,1,0:T(8,128)(2,1)S(1)} %bitcast.19, ...), custom_call_target="tpu_custom_call" | custom-call | flops 300000000 | bytes 6000000 | tf_op jit(solution)/shard_map/pallas_call | solution.py:303
  12.8 3.9 %collective-permute-start = (bf16[8,320,128]{2,1,0:T(8,128)(2,1)S(1)}, bf16[8,320,128]{2,1,0:T(8,128)(2,1)S(1)}, u32[]{:S(2)}, u32[]{:S(2)}) collective-permute-start(bf16[8,320,128]{2,1,0:T(8,128)(2,1)S(1)} %get-tuple-element.20), channel_id=1, source_target_pairs={{4,8},{8,4},{12,16},{16,12},{20,24},{24,20},{28,32},{32,28},{36,40... | collective-permute-start | bytes 1966088 | tf_op jit(solution)/shard_map/ppermute | solution.py:293
  16.7 2.7 %shard_map.79 = (bf16[8,320,128]{2,1,0:T(8,128)(2,1)S(1)}, f32[4,80,128]{2,1,0:T(8,128)S(1)}, f32[4,80,128]{2,1,0:T(8,128)S(1)}) custom-call(s32[32,4]{1,0:T(8,128)S(1)} %copy.12.list_ref, s32[1]{0:T(128)} %bitcast.9.count_ref, bf16[48,80,80]{2,1,0:T(8,128)(2,1)S(1)} %bitcast.20, bf16[32,80,320]{2,1,0:T(8,128)(2,1)S(1)} %bitcast.14, ...), custom_call_target="tpu_custom_call" | custom-call | flops 100000000 | bytes 4000000 | tf_op jit(solution)/shard_map/pallas_call | solution.py:294
  19.5 1.1 %collective-permute-start.2 = (f32[4,80,128]{2,1,0:T(8,128)S(1)}, f32[4,80,128]{2,1,0:T(8,128)S(1)}, u32[]{:S(2)}, u32[]{:S(2)}) collective-permute-start(f32[4,80,128]{2,1,0:T(8,128)S(1)} %get-tuple-element.22), channel_id=1, source_target_pairs={{0,1},{1,0},{2,3},{3,2},{4,5},{5,4},{6,7},{7,6},{8,9},{9,8},{10,11... | collective-permute-start | bytes 491528 | tf_op jit(solution)/shard_map/ppermute | solution.py:299
  20.5 0.7 collective-permute-start.3
  21.2 2.7 %shard_map.78.own_ref = f32[8,320,128]{2,1,0:T(8,128)S(1)} custom-call(s32[32,4]{1,0:T(8,128)S(1)} %copy.12.list_ref, s32[1]{0:T(128)} %bitcast.8.count_ref, bf16[48,80,80]{2,1,0:T(8,128)(2,1)S(1)} %bitcast.21, bf16[32,80,320]{2,1,0:T(8,128)(2,1)S(1)} %bitcast.15, bf16[48,80,128]{2,1,0:T(8,128)(2,1)S(1)} %get-tuple-element.19.tr_ref), custom_call_target="tpu_custom_call" | custom-call | flops 100000000 | bytes 6000000 | tf_op jit(solution)/shard_map/pallas_call | solution.py:309
  23.9 1.0 %collective-permute-done.2.in_ya = f32[4,80,128]{2,1,0:T(8,128)S(1)} collective-permute-done((f32[4,80,128]{2,1,0:T(8,128)S(1)}, f32[4,80,128]{2,1,0:T(8,128)S(1)}, u32[]{:S(2)}, u32[]{:S(2)}) %collective-permute-start.2) | collective-permute-done | bytes 163872 | tf_op jit(solution)/shard_map/ppermute | solution.py:299
  25.2 5.8 %shard_map.80 = (f32[8,320,128]{2,1,0:T(8,128)S(1)}, bf16[48,80,128]{2,1,0:T(8,128)(2,1)S(1)}, bf16[8,320,128]{2,1,0:T(8,128)(2,1)S(1)}) custom-call(s32[32,4]{1,0:T(8,128)S(1)} %copy.12.list_ref, s32[1]{0:T(128)} %bitcast.10.count_ref, f32[8,320,128]{2,1,0:T(8,128)S(1)} %shard_map.78.own_ref, bf16[8,320,128]{2,1,0:T(8,128)(2,1)S(1)} %collective-permute-done.in_cross, ...), custom_call_target="tpu_custom_call" | custom-call | flops 300000000 | bytes 8000000 | tf_op jit(solution)/shard_map/pallas_call | solution.py:314
  31.0 3.6 %collective-permute-start.4 = (bf16[8,320,128]{2,1,0:T(8,128)(2,1)S(1)}, bf16[8,320,128]{2,1,0:T(8,128)(2,1)S(1)}, u32[]{:S(2)}, u32[]{:S(2)}) collective-permute-start(bf16[8,320,128]{2,1,0:T(8,128)(2,1)S(1)} %get-tuple-element.27), channel_id=1, source_target_pairs={{4,8},{8,4},{12,16},{16,12},{20,24},{24,20},{28,32},{32,28},{36,40... | collective-permute-start | bytes 1966088 | tf_op jit(solution)/shard_map/ppermute | solution.py:293
  34.6 2.7 %shard_map.82 = (bf16[8,320,128]{2,1,0:T(8,128)(2,1)S(1)}, f32[4,80,128]{2,1,0:T(8,128)S(1)}, f32[4,80,128]{2,1,0:T(8,128)S(1)}) custom-call(s32[32,4]{1,0:T(8,128)S(1)} %copy.12.list_ref, s32[1]{0:T(128)} %bitcast.12.count_ref, bf16[48,80,80]{2,1,0:T(8,128)(2,1)S(1)} %bitcast.23, bf16[32,80,320]{2,1,0:T(8,128)(2,1)S(1)} %bitcast.17, ...), custom_call_target="tpu_custom_call" | custom-call | flops 100000000 | bytes 4000000 | tf_op jit(solution)/shard_map/pallas_call | solution.py:294
  37.4 3.4 %collective-permute-start.6 = (f32[4,80,128]{2,1,0:T(8,128)S(1)}, f32[4,80,128]{2,1,0:T(8,128)S(1)}, u32[]{:S(2)}, u32[]{:S(2)}) collective-permute-start(f32[4,80,128]{2,1,0:T(8,128)S(1)} %get-tuple-element.29), channel_id=1, source_target_pairs={{0,1},{1,0},{2,3},{3,2},{4,5},{5,4},{6,7},{7,6},{8,9},{9,8},{10,11... | collective-permute-start | bytes 491528 | tf_op jit(solution)/shard_map/ppermute | solution.py:299
  40.7 0.7 collective-permute-start.7
  41.4 3.0 %shard_map.81 = (f32[8,320,128]{2,1,0:T(8,128)S(1)}, f32[8,128]{1,0:T(8,128)S(1)}) custom-call(s32[32,4]{1,0:T(8,128)S(1)} %copy.12.list_ref, s32[1]{0:T(128)} %bitcast.11.count_ref, bf16[48,80,80]{2,1,0:T(8,128)(2,1)S(1)} %bitcast.24, bf16[32,80,320]{2,1,0:T(8,128)(2,1)S(1)} %bitcast.18, bf16[48,80,128]{2,1,0:T(8,128)(2,1)S(1)} %get-tuple-element.24.tr_ref, ...), custom_call_target="tpu_custom_call" | custom-call | flops 100000000 | bytes 6000000 | tf_op jit(solution)/shard_map/pallas_call | solution.py:320
  44.4 0.6 collective-permute-done.6.in_ya
  45.0 0.7 shard_map.83
  45.7 1.6 %collective-permute-start.8 = (f32[8,128]{1,0:T(8,128)S(1)}, f32[8,128]{1,0:T(8,128)S(1)}, u32[]{:S(2)}, u32[]{:S(2)}) collective-permute-start(f32[8,128]{1,0:T(8,128)S(1)} %get-tuple-element.32), channel_id=1, source_target_pairs={{0,4},{4,0},{1,5},{5,1},{2,6},{6,2},{3,7},{7,3},{8,12},{12,8},{9,1... | collective-permute-start | bytes 12296 | tf_op jit(solution)/shard_map/ppermute | solution.py:330
  47.4 0.8 collective-permute-done.8
  48.2 36.5 %all_to_all.5.sums_ref = f32[128,8,128]{2,1,0:T(8,128)S(1)} all-to-all(f32[128,8,128]{2,1,0:T(8,128)S(1)} %broadcast_in_dim.3), channel_id=1, replica_groups=mesh['z'=8,'y'=4,'c'=2,'x'=4] {'z','y','x'}, dimensions={0} | all-to-all | bytes 1048576 | tf_op jit(solution)/shard_map/all_to_all | solution.py:332
  84.7 1.5 %shard_map.84 = (f32[8,320,128]{2,1,0:T(8,128)}, f32[3,2,128]{2,1,0:T(2,128)}) custom-call(f32[128,8,128]{2,1,0:T(8,128)S(1)} %all_to_all.5.sums_ref, bf16[8,320,128]{2,1,0:T(8,128)(2,1)S(1)} %bitcast.28, f32[8,320,128]{2,1,0:T(8,128)S(1)} %get-tuple-element.25.w1_ref, f32[8,320,128]{2,1,0:T(8,128)S(1)} %get-tuple-element.33.w2_ref), custom_call_target="tpu_custom_call" | custom-call | flops 10000000 | bytes 6000000 | tf_op jit(solution)/shard_map/pallas_call | solution.py:333
  (20 shorter events, 0.6 us)
Async XLA Ops:
  2.0 1.5 %copy-start = (bf16[1,1,32,80,320]{4,3,2,1,0:T(8,128)(2,1)S(1)}, bf16[1,1,32,80,320]{4,3,2,1,0:T(8,128)(2,1)}, u32[]{:S(2)}) copy-start(bf16[1,1,32,80,320]{4,3,2,1,0:T(8,128)(2,1)} %param.11) | copy-start | bytes 4915204
  3.6 1.2 %copy-start.2 = (bf16[2,2,2,6,80,80]{5,4,3,2,1,0:T(8,128)(2,1)S(1)}, bf16[2,2,2,6,80,80]{5,4,3,2,1,0:T(8,128)(2,1)}, u32[]{:S(2)}) copy-start(bf16[2,2,2,6,80,80]{5,4,3,2,1,0:T(8,128)(2,1)} %param.8) | copy-start | bytes 1843204
  4.8 1.1 %copy-start.4 = (bf16[2,2,2,320,128]{4,3,2,1,0:T(8,128)(2,1)S(1)}, bf16[2,2,2,320,128]{4,3,2,1,0:T(8,128)(2,1)}, u32[]{:S(2)}) copy-start(bf16[2,2,2,320,128]{4,3,2,1,0:T(8,128)(2,1)} %param.6) | copy-start | bytes 1966084
  5.9 1.5 %copy-start.6 = (bf16[2,2,2,320,320]{4,3,2,1,0:T(8,128)(2,1)S(1)}, bf16[2,2,2,320,320]{4,3,2,1,0:T(8,128)(2,1)}, u32[]{:S(2)}) copy-start(bf16[2,2,2,320,320]{4,3,2,1,0:T(8,128)(2,1)} %param.7) | copy-start | bytes 4915204
  7.4 9.3 %copy-start.1 = (bf16[1,1,32,80,320]{4,3,2,1,0:T(8,128)(2,1)S(1)}, bf16[1,1,32,80,320]{4,3,2,1,0:T(8,128)(2,1)}, u32[]{:S(2)}) copy-start(bf16[1,1,32,80,320]{4,3,2,1,0:T(8,128)(2,1)} %param.11) | copy-start | bytes 4915204
  7.4 9.3 %copy-start.3 = (bf16[2,2,2,6,80,80]{5,4,3,2,1,0:T(8,128)(2,1)S(1)}, bf16[2,2,2,6,80,80]{5,4,3,2,1,0:T(8,128)(2,1)}, u32[]{:S(2)}) copy-start(bf16[2,2,2,6,80,80]{5,4,3,2,1,0:T(8,128)(2,1)} %param.8) | copy-start | bytes 1843204
  12.8 12.4 %collective-permute-start = (bf16[8,320,128]{2,1,0:T(8,128)(2,1)S(1)}, bf16[8,320,128]{2,1,0:T(8,128)(2,1)S(1)}, u32[]{:S(2)}, u32[]{:S(2)}) collective-permute-start(bf16[8,320,128]{2,1,0:T(8,128)(2,1)S(1)} %get-tuple-element.20), channel_id=1, source_target_pairs={{4,8},{8,4},{12,16},{16,12},{20,24},{24,20},{28,32},{32,28},{36,40... | collective-permute-start | bytes 1966088 | tf_op jit(solution)/shard_map/ppermute | solution.py:293
  19.4 5.9 %collective-permute-start.1 = (bf16[8,320,128]{2,1,0:T(8,128)(2,1)S(1)}, bf16[8,320,128]{2,1,0:T(8,128)(2,1)S(1)}, u32[]{:S(2)}, u32[]{:S(2)}) collective-permute-start(bf16[8,320,128]{2,1,0:T(8,128)(2,1)S(1)} %get-tuple-element.21), channel_id=1, source_target_pairs={{0,4},{4,0},{1,5},{5,1},{2,6},{6,2},{3,7},{7,3},{8,12},{12,8},{9,1... | collective-permute-start | bytes 1966088 | tf_op jit(solution)/shard_map/ppermute | solution.py:298
  19.5 5.5 %collective-permute-start.2 = (f32[4,80,128]{2,1,0:T(8,128)S(1)}, f32[4,80,128]{2,1,0:T(8,128)S(1)}, u32[]{:S(2)}, u32[]{:S(2)}) collective-permute-start(f32[4,80,128]{2,1,0:T(8,128)S(1)} %get-tuple-element.22), channel_id=1, source_target_pairs={{0,1},{1,0},{2,3},{3,2},{4,5},{5,4},{6,7},{7,6},{8,9},{9,8},{10,11... | collective-permute-start | bytes 491528 | tf_op jit(solution)/shard_map/ppermute | solution.py:299
  20.5 4.4 %collective-permute-start.3 = (f32[4,80,128]{2,1,0:T(8,128)S(1)}, f32[4,80,128]{2,1,0:T(8,128)S(1)}, u32[]{:S(2)}, u32[]{:S(2)}) collective-permute-start(f32[4,80,128]{2,1,0:T(8,128)S(1)} %get-tuple-element.23), channel_id=1, source_target_pairs={{1,2},{2,1},{5,6},{6,5},{9,10},{10,9},{13,14},{14,13},{17,18},{18,... | collective-permute-start | bytes 491528 | tf_op jit(solution)/shard_map/ppermute | solution.py:300
  31.0 14.0 %collective-permute-start.4 = (bf16[8,320,128]{2,1,0:T(8,128)(2,1)S(1)}, bf16[8,320,128]{2,1,0:T(8,128)(2,1)S(1)}, u32[]{:S(2)}, u32[]{:S(2)}) collective-permute-start(bf16[8,320,128]{2,1,0:T(8,128)(2,1)S(1)} %get-tuple-element.27), channel_id=1, source_target_pairs={{4,8},{8,4},{12,16},{16,12},{20,24},{24,20},{28,32},{32,28},{36,40... | collective-permute-start | bytes 1966088 | tf_op jit(solution)/shard_map/ppermute | solution.py:293
  34.6 6.8 %copy-start.5 = (bf16[2,2,2,320,128]{4,3,2,1,0:T(8,128)(2,1)S(1)}, bf16[2,2,2,320,128]{4,3,2,1,0:T(8,128)(2,1)}, u32[]{:S(2)}) copy-start(bf16[2,2,2,320,128]{4,3,2,1,0:T(8,128)(2,1)} %param.6) | copy-start | bytes 1966084
  37.3 7.7 %collective-permute-start.5 = (bf16[8,320,128]{2,1,0:T(8,128)(2,1)S(1)}, bf16[8,320,128]{2,1,0:T(8,128)(2,1)S(1)}, u32[]{:S(2)}, u32[]{:S(2)}) collective-permute-start(bf16[8,320,128]{2,1,0:T(8,128)(2,1)S(1)} %get-tuple-element.28), channel_id=1, source_target_pairs={{0,4},{4,0},{1,5},{5,1},{2,6},{6,2},{3,7},{7,3},{8,12},{12,8},{9,1... | collective-permute-start | bytes 1966088 | tf_op jit(solution)/shard_map/ppermute | solution.py:298
  37.4 7.6 %collective-permute-start.6 = (f32[4,80,128]{2,1,0:T(8,128)S(1)}, f32[4,80,128]{2,1,0:T(8,128)S(1)}, u32[]{:S(2)}, u32[]{:S(2)}) collective-permute-start(f32[4,80,128]{2,1,0:T(8,128)S(1)} %get-tuple-element.29), channel_id=1, source_target_pairs={{0,1},{1,0},{2,3},{3,2},{4,5},{5,4},{6,7},{7,6},{8,9},{9,8},{10,11... | collective-permute-start | bytes 491528 | tf_op jit(solution)/shard_map/ppermute | solution.py:299
  40.7 4.2 %collective-permute-start.7 = (f32[4,80,128]{2,1,0:T(8,128)S(1)}, f32[4,80,128]{2,1,0:T(8,128)S(1)}, u32[]{:S(2)}, u32[]{:S(2)}) collective-permute-start(f32[4,80,128]{2,1,0:T(8,128)S(1)} %get-tuple-element.30), channel_id=1, source_target_pairs={{1,2},{2,1},{5,6},{6,5},{9,10},{10,9},{13,14},{14,13},{17,18},{18,... | collective-permute-start | bytes 491528 | tf_op jit(solution)/shard_map/ppermute | solution.py:300
  45.7 2.5 %collective-permute-start.8 = (f32[8,128]{1,0:T(8,128)S(1)}, f32[8,128]{1,0:T(8,128)S(1)}, u32[]{:S(2)}, u32[]{:S(2)}) collective-permute-start(f32[8,128]{1,0:T(8,128)S(1)} %get-tuple-element.32), channel_id=1, source_target_pairs={{0,4},{4,0},{1,5},{5,1},{2,6},{6,2},{3,7},{7,3},{8,12},{12,8},{9,1... | collective-permute-start | bytes 12296 | tf_op jit(solution)/shard_map/ppermute | solution.py:330

commit v2 on v1

v2 whole, which is shorter than its diff:
```python
import functools

import jax
import jax.numpy as jnp
from jax import lax
from jax.experimental import pallas as pl
from jax.experimental.pallas import tpu as pltpu
from jax.sharding import PartitionSpec as P

VARS = 5
CHIPS_Z = 8
CHIPS_Y = 4
BLOCK = 320
FACE = 80
ELEMS = 8
RHS = 128
HANG = 32
EPS = 1e-6
GROUP = 8
VMEM_LIMIT = 40 * 1024 * 1024

TN = (((0,), (0,)), ((), ()))
NN = (((1,), (0,)), ((), ()))


def mm(a, b, dims):
    return lax.dot_general(a, b, dims, preferred_element_type=jnp.float32)


def low_half():
    return lax.broadcasted_iota(jnp.int32, (10, 8, RHS), 1) < 4


def turn(x):
    return pltpu.roll(x, 4, 1)


def trace_a(field, end):
    return field.reshape(VARS, 4, 16, RHS)[:, 3 * end].reshape(FACE, RHS)


def trace_b(field, end):
    rows = field.reshape(10, 4, 8, RHS)
    if end == 0:
        out = jnp.where(low_half(), rows[:, 0], turn(rows[:, 2]))
    else:
        out = jnp.where(low_half(), turn(rows[:, 1]), rows[:, 3])
    return out.reshape(FACE, RHS)


def spread_a(values, end):
    piece = values.reshape(VARS, 1, 16, RHS)
    zero = jnp.zeros((VARS, 3, 16, RHS), jnp.float32)
    return jnp.concatenate([zero, piece] if end else [piece, zero], axis=1).reshape(BLOCK, RHS)


def spread_b(values, end):
    rows = values.reshape(10, 8, RHS)
    zero = jnp.zeros_like(rows)
    low = low_half()
    if end == 0:
        parts = [jnp.where(low, rows, 0.0), zero, jnp.where(low, turn(rows), 0.0), zero]
    else:
        parts = [zero, jnp.where(low, 0.0, turn(rows)), zero, jnp.where(low, 0.0, rows)]
    return jnp.stack(parts, axis=1).reshape(BLOCK, RHS)


def face_c(end):
    return pl.ds(3 * end, FACE, stride=4)


def fill_traces(lowered, inv_ref, tr_ref, app_ref):
    for e in range(ELEMS):
        field = lowered(e)
        applied = mm(inv_ref[e], field, TN)
        app_ref[e] = applied
        for end in range(2):
            tr_ref[6 * e + end] = trace_a(applied, end).astype(jnp.bfloat16)
            tr_ref[6 * e + 2 + end] = trace_b(applied, end).astype(jnp.bfloat16)
            tr_ref[6 * e + 4 + end] = app_ref[e, face_c(end), :].astype(jnp.bfloat16)


def flux(face_ref, tr_ref, e, f):
    return mm(face_ref[6 * e + f], tr_ref[6 * e + f], TN)


def add_slots(acc, wanted, sign, list_ref, count_ref, hang_ref, tr_ref, slot_ref):
    live = count_ref[0, 0]

    def look(h, n):
        slot_ref[n] = h
        hit = jnp.logical_and(list_ref[2, h] * sign == wanted, h < live)
        return n + hit.astype(jnp.int32)

    n = lax.fori_loop(0, HANG, look, jnp.int32(0), unroll=8)
    for i in range(GROUP):
        slot_ref[n + i] = 0

    def work(first, size):
        parts = []
        for i in range(size):
            k = first + i
            h = slot_ref[k]
            source = list_ref[0, h] * 6 + list_ref[1, h]
            target = jnp.where(k < n, list_ref[3, h], ELEMS)
            parts.append((target, mm(hang_ref[h], tr_ref[source], TN)))
        for target, part in parts:
            acc[target] += part

    whole = (n + GROUP // 2 - 1) // GROUP

    @pl.loop(0, whole)
    def _(g):
        work(g * GROUP, GROUP)

    @pl.when(n > whole * GROUP)
    def _():
        work(whole * GROUP, GROUP // 2)


def core_and_row():
    return lax.axis_index("c"), lax.axis_index("x") % 2


def start_x(side, acc, face_ref, tr_ref):
    for n in range(4):
        acc[n + 4 * (1 - side)] = spread_a(flux(face_ref, tr_ref, n + 4 * side, side), 1 - side)
        acc[n + 4 * side] = jnp.zeros((BLOCK, RHS), jnp.float32)


def cross_part(acc, out_ref, list_ref, count_ref, face_ref, hang_ref, tr_ref, slot_ref, wanted):
    core, _ = core_and_row()
    side = core if wanted == 1 else 1 - core
    for s in range(2):

        @pl.when(side == s)
        def _(s=s):
            start_x(s, acc, face_ref, tr_ref)

    add_slots(acc, wanted, 2 * core - 1, list_ref, count_ref, hang_ref, tr_ref, slot_ref)
    out_ref[...] = acc[0:ELEMS].astype(out_ref.dtype)


def edge_fluxes(face_ref, tr_ref, ya_ref, yb_ref):
    _, odd = core_and_row()
    for parity in range(2):

        @pl.when(odd == parity)
        def _(parity=parity):
            up_ref, down_ref = (ya_ref, yb_ref) if parity == 0 else (yb_ref, ya_ref)
            for x in range(2):
                for z in range(2):
                    up_ref[2 * x + z] = flux(face_ref, tr_ref, 4 * x + 2 + z, 3)
                    down_ref[2 * x + z] = flux(face_ref, tr_ref, 4 * x + z, 2)


def first_kernel(
    list_ref, count_ref, rhs_hbm, inv_hbm, face_hbm, hang_hbm,
    rhs_ref, inv_ref, face_ref, hang_ref, tr_ref, cross_ref, acc, app_ref, slot_ref, sems,
):
    copies = []

    def bring(source, target):
        copies.append(pltpu.make_async_copy(source, target, sems.at[len(copies)]))
        copies[-1].start()

    for e in range(0, ELEMS, 2):
        pair = pl.ds(e, 2)
        bring(rhs_hbm.at[pair], rhs_ref.at[pair])
        bring(inv_hbm.at[pair], inv_ref.at[pair])
    late = len(copies)
    bring(face_hbm, face_ref)
    for h in range(0, HANG, 8):
        bring(hang_hbm.at[pl.ds(h, 8)], hang_ref.at[pl.ds(h, 8)])

    def lowered(e):
        if e % 2 == 0:
            copies[e].wait()
            copies[e + 1].wait()
        return rhs_ref[e]

    fill_traces(lowered, inv_ref, tr_ref, app_ref)
    for copy in copies[late:]:
        copy.wait()
    cross_part(acc, cross_ref, list_ref, count_ref, face_ref, hang_ref, tr_ref, slot_ref, 1)


def side_kernel(list_ref, count_ref, face_ref, hang_ref, tr_ref, chip_ref, ya_ref, yb_ref, acc, slot_ref):
    edge_fluxes(face_ref, tr_ref, ya_ref, yb_ref)
    cross_part(acc, chip_ref, list_ref, count_ref, face_ref, hang_ref, tr_ref, slot_ref, -1)


def own_body(list_ref, count_ref, face_ref, hang_ref, tr_ref, own_ref, acc, slot_ref):
    for e in range(ELEMS):
        x, y, z = (e >> 2) & 1, (e >> 1) & 1, e & 1
        from_x = flux(face_ref, tr_ref, e ^ 4, 0 if x == 0 else 1)
        from_y = flux(face_ref, tr_ref, e ^ 2, 2 if y == 0 else 3)
        from_z = flux(face_ref, tr_ref, e ^ 1, 4 if z == 0 else 5)
        acc[e] = spread_a(from_x, 1 - x) + spread_b(from_y, 1 - y)
        acc[e, face_c(1 - z), :] += from_z
    add_slots(acc, 0, 1, list_ref, count_ref, hang_ref, tr_ref, slot_ref)
    own_ref[...] = acc[0:ELEMS]


def own_kernel(list_ref, count_ref, face_ref, hang_ref, tr_ref, own_ref, acc, slot_ref):
    own_body(list_ref, count_ref, face_ref, hang_ref, tr_ref, own_ref, acc, slot_ref)


def inner(e, *pairs):
    return [jnp.sum((a[e].astype(jnp.float32) * b[e].astype(jnp.float32)).reshape(BLOCK // 8, 8, RHS), axis=0) for a, b in pairs]


def gram_rows(*pairs):
    totals = inner(0, *pairs)
    for e in range(1, ELEMS):
        totals = [t + p for t, p in zip(totals, inner(e, *pairs))]
    rows = [jnp.sum(t, axis=0, keepdims=True) for t in totals]
    return jnp.concatenate(rows, axis=1)


def own_gram_kernel(
    list_ref, count_ref, face_ref, hang_ref, tr_ref, rhs_ref, w1_ref, own_ref, gram_ref, acc, slot_ref
):
    own_body(list_ref, count_ref, face_ref, hang_ref, tr_ref, own_ref, acc, slot_ref)
    gram_ref[...] = gram_rows((rhs_ref, rhs_ref), (rhs_ref, w1_ref), (w1_ref, w1_ref))


def land(w_ref, own_ref, cross_ref, chip_ref, ya_ref, yb_ref):
    _, odd = core_and_row()
    for parity in range(2):

        @pl.when(odd == parity)
        def _(parity=parity):
            from_up, from_down = (ya_ref, yb_ref) if parity == 0 else (yb_ref, ya_ref)
            for e in range(ELEMS):
                y = (e >> 1) & 1
                n = 2 * (e >> 2) + (e & 1)
                edge = spread_b(from_up[n], 1) if y else spread_b(from_down[n], 0)
                came = cross_ref[e].astype(jnp.float32) + chip_ref[e].astype(jnp.float32)
                w_ref[e] = own_ref[e] + came + edge


def second_kernel(
    list_ref, count_ref, own_ref, in_cross, in_chip, in_ya, in_yb, inv_ref, face_ref, hang_ref,
    w_ref, tr_ref, cross_ref, acc, app_ref, slot_ref,
):
    land(w_ref, own_ref, in_cross, in_chip, in_ya, in_yb)
    fill_traces(lambda e: w_ref[e].astype(jnp.bfloat16), inv_ref, tr_ref, app_ref)
    cross_part(acc, cross_ref, list_ref, count_ref, face_ref, hang_ref, tr_ref, slot_ref, 1)


def last_kernel(own_ref, in_cross, in_chip, in_ya, in_yb, rhs_ref, w1_ref, early_ref, w_ref, keep_ref, give_ref):
    land(w_ref, own_ref, in_cross, in_chip, in_ya, in_yb)
    late = gram_rows((rhs_ref, w_ref), (w1_ref, w_ref), (w_ref, w_ref))
    early = early_ref[...]
    core, _ = core_and_row()
    keep_ref[...] = jnp.where(core == 0, early, late)
    give_ref[...] = jnp.where(core == 0, late, early)


def combine_kernel(entries, mine_ref, other_ref, rhs_ref, w1_ref, w2_ref, out_hbm, hess_ref, out_ref, sems):
    core, _ = core_and_row()
    mine = mine_ref[...] * (1.0 / entries)
    other = other_ref[...] * (1.0 / entries)
    early = jnp.where(core == 0, mine, other)
    late = jnp.where(core == 0, other, mine)
    g00, g01, g11 = (early[:, RHS * i : RHS * i + RHS] for i in range(3))
    g02, g12, g22 = (late[:, RHS * i : RHS * i + RHS] for i in range(3))
    norm0 = g00 + EPS
    size0 = jnp.sqrt(norm0)
    h11 = (g00 + g01) / norm0
    c1 = (EPS - g01) / norm0
    square1 = jnp.maximum(g11 + 2.0 * c1 * g01 + c1 * c1 * g00, 0.0) / norm0 + EPS
    h21 = jnp.sqrt(square1)
    s2 = 1.0 / (size0 * h21)
    ratio = (g02 + c1 * g01 + EPS * h11) / norm0
    h12 = ratio * s2 * size0
    q = EPS / square1 - s2 * s2 * (g12 + c1 * (g11 + g02 + c1 * g01))
    h22 = 1.0 - q
    alpha = c1 + q
    beta = c1 * q - ratio
    total = g22 + 2.0 * (alpha * g12 + beta * g02 + alpha * beta * g01)
    total = total + alpha * alpha * g11 + beta * beta * g00
    h32 = jnp.sqrt(s2 * s2 * jnp.maximum(total, 0.0) + EPS)
    zero = jnp.zeros_like(h11)
    for i, row in enumerate(((h11, h12), (h21, h22), (zero, h32))):
        hess_ref[i] = jnp.concatenate(row, axis=0)
    k2 = s2 / h32
    k1 = k2 * alpha
    k0 = k2 * beta
    copies = []
    for e in range(ELEMS):
        out_ref[e] = k2 * w2_ref[e] + k1 * w1_ref[e] + k0 * rhs_ref[e].astype(jnp.float32)
        copies.append(pltpu.make_async_copy(out_ref.at[e], out_hbm.at[e], sems.at[e]))
        copies[e].start()
    for copy in copies:
        copy.wait()


def shape(dims, dtype=jnp.float32):
    return jax.ShapeDtypeStruct(dims, dtype)


FIELD = (ELEMS, BLOCK, RHS)
TRACES = (6 * ELEMS, FACE, RHS)
SIDE = (4, FACE, RHS)
SMEM = pl.BlockSpec(memory_space=pltpu.SMEM)
VMEM = pl.BlockSpec(memory_space=pltpu.VMEM)
HBM = pl.BlockSpec(memory_space=pltpu.HBM)


def call(kernel, in_specs, outs, scratch, flops, moved, out_specs=None):
    return pl.pallas_call(
        kernel,
        out_shape=outs,
        in_specs=in_specs,
        out_specs=out_specs or [VMEM] * len(outs),
        scratch_shapes=scratch,
        compiler_params=pltpu.CompilerParams(vmem_limit_bytes=VMEM_LIMIT),
        cost_estimate=pl.CostEstimate(flops=flops, bytes_accessed=moved, transcendentals=0),
    )


def stay(x):
    return pltpu.with_memory_space_constraint(x, pltpu.HBM)


def per_device(entries, pairs, rhs_field, inv_block, face_block, hang_list, hang_count, hang_block):
    rows = stay(hang_list.reshape(HANG, 4).T)
    count = hang_count
    field = pltpu.VMEM(FIELD, jnp.float32)
    acc = pltpu.VMEM((ELEMS + 1, BLOCK, RHS), jnp.float32)
    slots = pltpu.SMEM((HANG + 8,), jnp.int32)
    bf16 = jnp.bfloat16
    million = 10**6
    scalars = [SMEM, SMEM]

    rhs, inv, face, hang, traces, cross = call(
        first_kernel, scalars + [HBM] * 4,
        [
            shape(FIELD, bf16), shape((ELEMS, BLOCK, BLOCK), bf16), shape((6 * ELEMS, FACE, FACE), bf16),
            shape((HANG, FACE, BLOCK), bf16), shape(TRACES, bf16), shape(FIELD, bf16),
        ],
        [acc, field, slots, pltpu.SemaphoreType.DMA((ELEMS + 5,))],
        300 * million, 6 * million,
    )(
        rows, count, stay(rhs_field.reshape(FIELD)), stay(inv_block.reshape(ELEMS, BLOCK, BLOCK)),
        stay(face_block.reshape(6 * ELEMS, FACE, FACE)), stay(hang_block.reshape(HANG, FACE, BLOCK)),
    )

    def exchange(traces, cross, own_call):
        in_cross = lax.ppermute(cross, ("z", "y", "c"), pairs["cross"])
        chip, ya, yb = call(
            side_kernel, scalars + [VMEM] * 3, [shape(FIELD, bf16), shape(SIDE), shape(SIDE)], [acc, slots],
            100 * million, 4 * million,
        )(rows, count, face, hang, traces)
        in_ya = lax.ppermute(ya, "x", pairs["even"])
        in_yb = lax.ppermute(yb, "x", pairs["odd"])
        in_chip = lax.ppermute(chip, "c", [(0, 1), (1, 0)])
        return own_call(traces), (in_cross, in_chip, in_ya, in_yb)

    def own_first(traces):
        return call(
            own_kernel, scalars + [VMEM] * 3, [shape(FIELD)], [acc, slots], 100 * million, 6 * million
        )(rows, count, face, hang, traces)[0]

    own, arrived = exchange(traces, cross, own_first)
    w1, traces, cross = call(
        second_kernel, scalars + [VMEM] * 8, [shape(FIELD), shape(TRACES, bf16), shape(FIELD, bf16)],
        [acc, field, slots], 300 * million, 8 * million,
    )(rows, count, own, *arrived, inv, face, hang)

    def own_second(traces):
        return call(
            own_gram_kernel, scalars + [VMEM] * 5, [shape(FIELD), shape((1, 3 * RHS))], [acc, slots],
            100 * million, 6 * million,
        )(rows, count, face, hang, traces, rhs, w1)

    (own, early), arrived = exchange(traces, cross, own_second)
    w2, keep, give = call(
        last_kernel, [VMEM] * 8, [shape(FIELD), shape((1, 3 * RHS)), shape((1, 3 * RHS))], [], 10 * million, 8 * million
    )(own, *arrived, rhs, w1, early)

    swap = [(0, 1), (1, 0)]
    part = keep + lax.ppermute(give, "c", swap)
    chips = lax.axis_size(("z", "y", "x"))
    mine = lax.all_to_all(jnp.broadcast_to(part, (chips, 1, 3 * RHS)), ("z", "y", "x"), 0, 0).sum(0)
    last, hessenberg = call(
        functools.partial(combine_kernel, entries), [VMEM] * 5, [shape(FIELD), shape((3, 2, RHS))],
        [field, pltpu.SemaphoreType.DMA((ELEMS,))], 10 * million, 6 * million, [HBM, VMEM],
    )(mine, lax.ppermute(mine, "c", swap), rhs, w1, w2)
    return last.reshape(rhs_field.shape), hessenberg


def solution(mesh):
    count_x, count_y = mesh.shape["gx"], mesh.shape["gy"]
    grid = jax.sharding.Mesh(
        mesh.devices.reshape(CHIPS_Z, CHIPS_Y, 2, count_y), ("z", "y", "c", "x")
    )
    pairs = {"cross": [], "even": [], "odd": []}
    for i in range(1, count_x - 1, 2):
        pairs["cross"] += [(i, i + 1), (i + 1, i)]
    for j in range(count_y - 1):
        pairs["odd" if j % 2 else "even"] += [(j, j + 1), (j + 1, j)]
    long = ("z", "y", "c")
    in_specs = (P(long, "x"),) * 6
    out_specs = (P(long, "x"), P())
    entries = float(ELEMS * BLOCK * count_x * count_y)
    return jax.shard_map(
        functools.partial(per_device, entries, pairs),
        mesh=grid, in_specs=in_specs, out_specs=out_specs, check_vma=False,
    )
```

time: 87.3 us -> 74 us (0.85)
  Pallas kernels: 24.4 us -> 18.2 us
  local copies, waits for them, and re-layouts: 6.19 us -> 0.11 us
  blocking collectives: 36.5 us -> 30.6 us
  starting transfers between devices: 15 us -> 17.9 us
  waiting for transfers between devices: 2.75 us -> 4.88 us
    pallas_call x8, Pallas kernels: 24.4 us -> 18.2 us  [the longest x1 4.26 us: per_device(): call(first_kernel, scalars + [HBM] * 4, [shape(FIELD, bf16), shape((ELEMS...]
    all_to_all x1, blocking collectives: 36.5 us -> 30.6 us  [per_device(): lax.all_to_all(jnp.broadcast_to(part, (chips, 1, 3 * RHS)), ('z', 'y', 'x...]
    unnamed x14 -> x0, local copies, waits for them, and re-layouts: 5.39 us -> none
    ppermute x1 -> x2, starting transfers between devices: 1.64 us -> 3.47 us  [the longest x1 2.47 us: per_device(): lax.ppermute(mine, 'c', swap)]
  transfers between devices with their start and end apart: 9 -> 10, of which waited for: 4 -> 5; matrix products, arithmetic and copies ran while one was open for 0% -> 0% of each run, Pallas kernels for 13% -> 12%
where the time goes in v2:
time: 74 us; the launch traced here: 73.5 us
  blocking collectives  30.6 us (41%)
  Pallas kernels  18.2 us (25%)
  starting transfers between devices  17.9 us (24%)
  waiting for transfers between devices  4.88 us (7%)
  between operations  1.55 us (2%)
    all_to_all x1, blocking collectives, per_device(): lax.all_to_all(jnp.broadcast_to(part, (chips, 1, 3 * RHS)), ('z', 'y', 'x...  30.6 us
    ppermute x2, starting transfers between devices, exchange(): in_cross = lax.ppermute(cross, ('z', 'y', 'c'), pairs['cross'])  8.01 us
    ppermute x2, starting transfers between devices, exchange(): in_ya = lax.ppermute(ya, 'x', pairs['even'])  4.96 us
    pallas_call x1, Pallas kernels, per_device(): call(first_kernel, scalars + [HBM] * 4, [shape(FIELD, bf16), shape((ELEMS...  4.26 us
    pallas_call x2, Pallas kernels, exchange(): call(side_kernel, scalars + [VMEM] * 3, [shape(FIELD, bf16), shape(SIDE),...  4.21 us
    pallas_call x1, Pallas kernels, per_device(): call(second_kernel, scalars + [VMEM] * 8, [shape(FIELD), shape(TRACES, bf...  2.65 us
    ppermute x1, starting transfers between devices, per_device(): lax.ppermute(mine, 'c', swap)  2.47 us
    pallas_call x1, Pallas kernels, own_second(): call(own_gram_kernel, scalars + [VMEM] * 5, [shape(FIELD), shape((1, 3 *...  2.44 us
  transfers between devices with their start and end apart: 10, of which 5 were waited for; matrix products, arithmetic and copies ran while one was open for 0% of the time, Pallas kernels for 12%

profile of v2, /device:TPU:1, one launch (start us, length us, event | category | flops | bytes accessed | tf_op | source)
XLA Modules:
  0.0 73.5 jit_solution(1575103243726671260)
XLA Ops:
  1.3 4.3 %shard_map.77 = (bf16[8,320,128]{2,1,0:T(8,128)(2,1)S(1)}, bf16[8,320,320]{2,1,0:T(8,128)(2,1)S(1)}, bf16[48,80,80]{2,1,0:T(8,128)(2,1)S(1)}, bf16[32,80,320]{2,...) custom-call(s32[4,32]{1,0:T(4,128)} %bitcast.12, s32[1,1]{1,0:T(1,128)S(6)} %copy.10.count_ref, ...), custom_call_target="tpu_custom_call" | custom-call | flops 300000000 | bytes 6000000 | tf_op jit(solution)/shard_map/pallas_call | solution.py:338
  5.5 4.6 %collective-permute-start = (bf16[8,320,128]{2,1,0:T(8,128)(2,1)S(1)}, bf16[8,320,128]{2,1,0:T(8,128)(2,1)S(1)}, u32[]{:S(2)}, u32[]{:S(2)}) collective-permute-start(bf16[8,320,128]{2,1,0:T(8,128)(2,1)S(1)} %get-tuple-element.27), channel_id=1, source_target_pairs={{4,8},{8,4},{12,16},{16,12},{20,24},{24,20},{28,32},{32,28},{36,40... | collective-permute-start | bytes 1966088 | tf_op jit(solution)/shard_map/ppermute | solution.py:352
  10.2 2.1 %shard_map.79 = (bf16[8,320,128]{2,1,0:T(8,128)(2,1)S(1)}, f32[4,80,128]{2,1,0:T(8,128)S(1)}, f32[4,80,128]{2,1,0:T(8,128)S(1)}) custom-call(s32[4,32]{1,0:T(4,128)} %bitcast.13, s32[1,1]{1,0:T(1,128)S(6)} %copy.10.count_ref, bf16[48,80,80]{2,1,0:T(8,128)(2,1)S(1)} %get-tuple-element.24.face_ref, bf16[32,80,320]{2,1,0:T(8,128)(2,1)S(1)} %get-tuple-element.25.hang_ref, ...), custom_call_target="tpu_custom_call" | custom-call | flops 100000000 | bytes 4000000 | tf_op jit(solution)/shard_map/pallas_call | solution.py:353
  12.4 1.4 %collective-permute-start.2 = (f32[4,80,128]{2,1,0:T(8,128)S(1)}, f32[4,80,128]{2,1,0:T(8,128)S(1)}, u32[]{:S(2)}, u32[]{:S(2)}) collective-permute-start(f32[4,80,128]{2,1,0:T(8,128)S(1)} %get-tuple-element.29), channel_id=1, source_target_pairs={{0,1},{1,0},{2,3},{3,2},{4,5},{5,4},{6,7},{7,6},{8,9},{9,8},{10,11... | collective-permute-start | bytes 491528 | tf_op jit(solution)/shard_map/ppermute | solution.py:357
  13.8 0.7 collective-permute-start.3
  14.4 2.1 %shard_map.78.own_ref = f32[8,320,128]{2,1,0:T(8,128)S(1)} custom-call(s32[4,32]{1,0:T(4,128)} %bitcast.14, s32[1,1]{1,0:T(1,128)S(6)} %copy.10.count_ref, bf16[48,80,80]{2,1,0:T(8,128)(2,1)S(1)} %get-tuple-element.24.face_ref, bf16[32,80,320]{2,1,0:T(8,128)(2,1)S(1)} %get-tuple-element.25.hang_ref, bf16[48,80,128]{2,1,0:T(8,128)(2,1)S(1)} %get-tuple-element.26.tr_ref), custom_call_target="tpu_custom_call" | custom-call | flops 100000000 | bytes 6000000 | tf_op jit(solution)/shard_map/pallas_call | solution.py:363
  16.6 1.3 %collective-permute-done.2.in_ya = f32[4,80,128]{2,1,0:T(8,128)S(1)} collective-permute-done((f32[4,80,128]{2,1,0:T(8,128)S(1)}, f32[4,80,128]{2,1,0:T(8,128)S(1)}, u32[]{:S(2)}, u32[]{:S(2)}) %collective-permute-start.2) | collective-permute-done | bytes 163872 | tf_op jit(solution)/shard_map/ppermute | solution.py:357
  17.8 0.8 %collective-permute-done.in_cross = bf16[8,320,128]{2,1,0:T(8,128)(2,1)S(1)} collective-permute-done((bf16[8,320,128]{2,1,0:T(8,128)(2,1)S(1)}, bf16[8,320,128]{2,1,0:T(8,128)(2,1)S(1)}, u32[]{:S(2)}, u32[]{:S(2)}) %collective-permute-start) | collective-permute-done | bytes 655392 | tf_op jit(solution)/shard_map/ppermute | solution.py:352
  18.7 2.6 %shard_map.80 = (f32[8,320,128]{2,1,0:T(8,128)S(1)}, bf16[48,80,128]{2,1,0:T(8,128)(2,1)S(1)}, bf16[8,320,128]{2,1,0:T(8,128)(2,1)S(1)}) custom-call(s32[4,32]{1,0:T(4,128)} %bitcast.15, s32[1,1]{1,0:T(1,128)S(6)} %copy.10.count_ref, f32[8,320,128]{2,1,0:T(8,128)S(1)} %shard_map.78.own_ref, bf16[8,320,128]{2,1,0:T(8,128)(2,1)S(1)} %collective-permute-done.in_cross, ...), custom_call_target="tpu_custom_call" | custom-call | flops 300000000 | bytes 8000000 | tf_op jit(solution)/shard_map/pallas_call | solution.py:368
  21.3 3.4 %collective-permute-start.4 = (bf16[8,320,128]{2,1,0:T(8,128)(2,1)S(1)}, bf16[8,320,128]{2,1,0:T(8,128)(2,1)S(1)}, u32[]{:S(2)}, u32[]{:S(2)}) collective-permute-start(bf16[8,320,128]{2,1,0:T(8,128)(2,1)S(1)} %get-tuple-element.36), channel_id=1, source_target_pairs={{4,8},{8,4},{12,16},{16,12},{20,24},{24,20},{28,32},{32,28},{36,40... | collective-permute-start | bytes 1966088 | tf_op jit(solution)/shard_map/ppermute | solution.py:352
  24.7 2.1 %shard_map.82 = (bf16[8,320,128]{2,1,0:T(8,128)(2,1)S(1)}, f32[4,80,128]{2,1,0:T(8,128)S(1)}, f32[4,80,128]{2,1,0:T(8,128)S(1)}) custom-call(s32[4,32]{1,0:T(4,128)} %bitcast.16, s32[1,1]{1,0:T(1,128)S(6)} %copy.10.count_ref, bf16[48,80,80]{2,1,0:T(8,128)(2,1)S(1)} %get-tuple-element.24.face_ref, bf16[32,80,320]{2,1,0:T(8,128)(2,1)S(1)} %get-tuple-element.25.hang_ref, ...), custom_call_target="tpu_custom_call" | custom-call | flops 100000000 | bytes 4000000 | tf_op jit(solution)/shard_map/pallas_call | solution.py:353
  27.0 3.6 %collective-permute-start.6 = (f32[4,80,128]{2,1,0:T(8,128)S(1)}, f32[4,80,128]{2,1,0:T(8,128)S(1)}, u32[]{:S(2)}, u32[]{:S(2)}) collective-permute-start(f32[4,80,128]{2,1,0:T(8,128)S(1)} %get-tuple-element.38), channel_id=1, source_target_pairs={{0,1},{1,0},{2,3},{3,2},{4,5},{5,4},{6,7},{7,6},{8,9},{9,8},{10,11... | collective-permute-start | bytes 491528 | tf_op jit(solution)/shard_map/ppermute | solution.py:357
  30.5 0.7 collective-permute-start.7
  31.2 2.4 %shard_map.81 = (f32[8,320,128]{2,1,0:T(8,128)S(1)}, f32[1,384]{1,0:T(1,128)S(1)}) custom-call(s32[4,32]{1,0:T(4,128)} %bitcast.17, s32[1,1]{1,0:T(1,128)S(6)} %copy.10.count_ref, bf16[48,80,80]{2,1,0:T(8,128)(2,1)S(1)} %get-tuple-element.24.face_ref, bf16[32,80,320]{2,1,0:T(8,128)(2,1)S(1)} %get-tuple-element.25.hang_ref, ...), custom_call_target="tpu_custom_call" | custom-call | flops 100000000 | bytes 6000000 | tf_op jit(solution)/shard_map/pallas_call | solution.py:374
  33.6 1.1 %collective-permute-done.6.in_ya = f32[4,80,128]{2,1,0:T(8,128)S(1)} collective-permute-done((f32[4,80,128]{2,1,0:T(8,128)S(1)}, f32[4,80,128]{2,1,0:T(8,128)S(1)}, u32[]{:S(2)}, u32[]{:S(2)}) %collective-permute-start.6) | collective-permute-done | bytes 163872 | tf_op jit(solution)/shard_map/ppermute | solution.py:357
  34.8 0.8 %shard_map.83 = (f32[8,320,128]{2,1,0:T(8,128)S(1)}, f32[1,384]{1,0:T(1,128)S(1)}, f32[1,384]{1,0:T(1,128)S(1)}) custom-call(f32[8,320,128]{2,1,0:T(8,128)S(1)} %get-tuple-element.35.own_ref, bf16[8,320,128]{2,1,0:T(8,128)(2,1)S(1)} %collective-permute-done.4.in_cross, bf16[8,320,128]{2,1,0:T(8,128)(2,1)S(1)} %collective-permute-done.5.in_chip, ...), custom_call_target="tpu_custom_call" | custom-call | flops 10000000 | bytes 8000000 | tf_op jit(solution)/shard_map/pallas_call | solution.py:380
  35.5 1.0 %collective-permute-start.8 = (f32[1,384]{1,0:T(1,128)S(1)}, f32[1,384]{1,0:T(1,128)S(1)}, u32[]{:S(2)}, u32[]{:S(2)}) collective-permute-start(f32[1,384]{1,0:T(1,128)S(1)} %get-tuple-element.42), channel_id=1, source_target_pairs={{0,4},{4,0},{1,5},{5,1},{2,6},{6,2},{3,7},{7,3},{8,12},{12,8},{9,1... | collective-permute-start | bytes 4616 | tf_op jit(solution)/shard_map/ppermute | solution.py:385
  36.5 0.8 %collective-permute-done.8 = f32[1,384]{1,0:T(1,128)S(1)} collective-permute-done((f32[1,384]{1,0:T(1,128)S(1)}, f32[1,384]{1,0:T(1,128)S(1)}, u32[]{:S(2)}, u32[]{:S(2)}) %collective-permute-start.8) | collective-permute-done | bytes 1568 | tf_op jit(solution)/shard_map/ppermute | solution.py:385
  37.4 0.1 broadcast_in_dim.3
  37.5 30.6 %all_to_all.5 = f32[128,1,384]{2,1,0:T(1,128)S(1)} all-to-all(f32[128,1,384]{2,1,0:T(1,128)S(1)} %broadcast_in_dim.3), channel_id=1, replica_groups=mesh['z'=8,'y'=4,'c'=2,'x'=4] {'z','y','x'}, dimensions={0} | all-to-all | bytes 393216 | tf_op jit(solution)/shard_map/all_to_all | solution.py:387
  68.1 0.2 reduce_sum.11
  68.2 2.5 %collective-permute-start.9 = (f32[1,384]{1,0:T(1,128)S(1)}, f32[1,384]{1,0:T(1,128)S(1)}, u32[]{:S(2)}, u32[]{:S(2)}) collective-permute-start(f32[1,384]{1,0:T(1,128)S(1)} %reduce_sum.12.mine_ref), channel_id=1, source_target_pairs={{0,4},{4,0},{1,5},{5,1},{2,6},{6,2},{3,7},{7,3},{8,12},{12,8},{9,1... | collective-permute-start | bytes 4616 | tf_op jit(solution)/shard_map/ppermute | solution.py:391
  70.7 0.8 %collective-permute-done.9.other_ref = f32[1,384]{1,0:T(1,128)S(1)} collective-permute-done((f32[1,384]{1,0:T(1,128)S(1)}, f32[1,384]{1,0:T(1,128)S(1)}, u32[]{:S(2)}, u32[]{:S(2)}) %collective-permute-start.9) | collective-permute-done | bytes 1568 | tf_op jit(solution)/shard_map/ppermute | solution.py:391
  71.5 1.8 %shard_map.84 = (f32[8,320,128]{2,1,0:T(8,128)}, f32[3,2,128]{2,1,0:T(2,128)}) custom-call(f32[1,384]{1,0:T(1,128)S(1)} %reduce_sum.12.mine_ref, f32[1,384]{1,0:T(1,128)S(1)} %collective-permute-done.9.other_ref, bf16[8,320,128]{2,1,0:T(8,128)(2,1)S(1)} %get-tuple-element.33.rhs_ref, f32[8,320,128]{2,1,0:T(8,128)S(1)} %get-tuple-element.34.w1_ref, ...), custom_call_target="tpu_custom_call" | custom-call | flops 10000000 | bytes 6000000 | tf_op jit(solution)/shard_map/pallas_call | solution.py:388
  (9 shorter events, 0.2 us)
Async XLA Ops:
  5.5 13.1 %collective-permute-start = (bf16[8,320,128]{2,1,0:T(8,128)(2,1)S(1)}, bf16[8,320,128]{2,1,0:T(8,128)(2,1)S(1)}, u32[]{:S(2)}, u32[]{:S(2)}) collective-permute-start(bf16[8,320,128]{2,1,0:T(8,128)(2,1)S(1)} %get-tuple-element.27), channel_id=1, source_target_pairs={{4,8},{8,4},{12,16},{16,12},{20,24},{24,20},{28,32},{32,28},{36,40... | collective-permute-start | bytes 1966088 | tf_op jit(solution)/shard_map/ppermute | solution.py:352
  12.3 6.4 %collective-permute-start.1 = (bf16[8,320,128]{2,1,0:T(8,128)(2,1)S(1)}, bf16[8,320,128]{2,1,0:T(8,128)(2,1)S(1)}, u32[]{:S(2)}, u32[]{:S(2)}) collective-permute-start(bf16[8,320,128]{2,1,0:T(8,128)(2,1)S(1)} %get-tuple-element.28), channel_id=1, source_target_pairs={{0,4},{4,0},{1,5},{5,1},{2,6},{6,2},{3,7},{7,3},{8,12},{12,8},{9,1... | collective-permute-start | bytes 1966088 | tf_op jit(solution)/shard_map/ppermute | solution.py:359
  12.4 5.5 %collective-permute-start.2 = (f32[4,80,128]{2,1,0:T(8,128)S(1)}, f32[4,80,128]{2,1,0:T(8,128)S(1)}, u32[]{:S(2)}, u32[]{:S(2)}) collective-permute-start(f32[4,80,128]{2,1,0:T(8,128)S(1)} %get-tuple-element.29), channel_id=1, source_target_pairs={{0,1},{1,0},{2,3},{3,2},{4,5},{5,4},{6,7},{7,6},{8,9},{9,8},{10,11... | collective-permute-start | bytes 491528 | tf_op jit(solution)/shard_map/ppermute | solution.py:357
  13.8 4.1 %collective-permute-start.3 = (f32[4,80,128]{2,1,0:T(8,128)S(1)}, f32[4,80,128]{2,1,0:T(8,128)S(1)}, u32[]{:S(2)}, u32[]{:S(2)}) collective-permute-start(f32[4,80,128]{2,1,0:T(8,128)S(1)} %get-tuple-element.30), channel_id=1, source_target_pairs={{1,2},{2,1},{5,6},{6,5},{9,10},{10,9},{13,14},{14,13},{17,18},{18,... | collective-permute-start | bytes 491528 | tf_op jit(solution)/shard_map/ppermute | solution.py:358
  21.3 13.4 %collective-permute-start.4 = (bf16[8,320,128]{2,1,0:T(8,128)(2,1)S(1)}, bf16[8,320,128]{2,1,0:T(8,128)(2,1)S(1)}, u32[]{:S(2)}, u32[]{:S(2)}) collective-permute-start(bf16[8,320,128]{2,1,0:T(8,128)(2,1)S(1)} %get-tuple-element.36), channel_id=1, source_target_pairs={{4,8},{8,4},{12,16},{16,12},{20,24},{24,20},{28,32},{32,28},{36,40... | collective-permute-start | bytes 1966088 | tf_op jit(solution)/shard_map/ppermute | solution.py:352
  26.9 7.9 %collective-permute-start.5 = (bf16[8,320,128]{2,1,0:T(8,128)(2,1)S(1)}, bf16[8,320,128]{2,1,0:T(8,128)(2,1)S(1)}, u32[]{:S(2)}, u32[]{:S(2)}) collective-permute-start(bf16[8,320,128]{2,1,0:T(8,128)(2,1)S(1)} %get-tuple-element.37), channel_id=1, source_target_pairs={{0,4},{4,0},{1,5},{5,1},{2,6},{6,2},{3,7},{7,3},{8,12},{12,8},{9,1... | collective-permute-start | bytes 1966088 | tf_op jit(solution)/shard_map/ppermute | solution.py:359
  27.0 7.8 %collective-permute-start.6 = (f32[4,80,128]{2,1,0:T(8,128)S(1)}, f32[4,80,128]{2,1,0:T(8,128)S(1)}, u32[]{:S(2)}, u32[]{:S(2)}) collective-permute-start(f32[4,80,128]{2,1,0:T(8,128)S(1)} %get-tuple-element.38), channel_id=1, source_target_pairs={{0,1},{1,0},{2,3},{3,2},{4,5},{5,4},{6,7},{7,6},{8,9},{9,8},{10,11... | collective-permute-start | bytes 491528 | tf_op jit(solution)/shard_map/ppermute | solution.py:357
  30.5 4.2 %collective-permute-start.7 = (f32[4,80,128]{2,1,0:T(8,128)S(1)}, f32[4,80,128]{2,1,0:T(8,128)S(1)}, u32[]{:S(2)}, u32[]{:S(2)}) collective-permute-start(f32[4,80,128]{2,1,0:T(8,128)S(1)} %get-tuple-element.39), channel_id=1, source_target_pairs={{1,2},{2,1},{5,6},{6,5},{9,10},{10,9},{13,14},{14,13},{17,18},{18,... | collective-permute-start | bytes 491528 | tf_op jit(solution)/shard_map/ppermute | solution.py:358
  35.5 1.8 %collective-permute-start.8 = (f32[1,384]{1,0:T(1,128)S(1)}, f32[1,384]{1,0:T(1,128)S(1)}, u32[]{:S(2)}, u32[]{:S(2)}) collective-permute-start(f32[1,384]{1,0:T(1,128)S(1)} %get-tuple-element.42), channel_id=1, source_target_pairs={{0,4},{4,0},{1,5},{5,1},{2,6},{6,2},{3,7},{7,3},{8,12},{12,8},{9,1... | collective-permute-start | bytes 4616 | tf_op jit(solution)/shard_map/ppermute | solution.py:385
  68.2 3.3 %collective-permute-start.9 = (f32[1,384]{1,0:T(1,128)S(1)}, f32[1,384]{1,0:T(1,128)S(1)}, u32[]{:S(2)}, u32[]{:S(2)}) collective-permute-start(f32[1,384]{1,0:T(1,128)S(1)} %reduce_sum.12.mine_ref), channel_id=1, source_target_pairs={{0,4},{4,0},{1,5},{5,1},{2,6},{6,2},{3,7},{7,3},{8,12},{12,8},{9,1... | collective-permute-start | bytes 4616 | tf_op jit(solution)/shard_map/ppermute | solution.py:391

commit v3 on v2

--- a/solution.py
+++ b/solution.py
@@ -17,6 +17,8 @@
 HANG = 32
 EPS = 1e-6
 GROUP = 8
+SIDE_FLOPS = 100 * 10**6
+OWN_FLOPS = 4000 * 10**6
 VMEM_LIMIT = 40 * 1024 * 1024
 
 TN = (((0,), (0,)), ((), ()))
@@ -80,11 +82,7 @@
             tr_ref[6 * e + 4 + end] = app_ref[e, face_c(end), :].astype(jnp.bfloat16)
 
 
-def flux(face_ref, tr_ref, e, f):
-    return mm(face_ref[6 * e + f], tr_ref[6 * e + f], TN)
-
-
-def add_slots(acc, wanted, sign, list_ref, count_ref, hang_ref, tr_ref, slot_ref):
+def list_slots(wanted, sign, list_ref, count_ref, slot_ref):
     live = count_ref[0, 0]
 
     def look(h, n):
@@ -95,7 +93,16 @@
     n = lax.fori_loop(0, HANG, look, jnp.int32(0), unroll=8)
     for i in range(GROUP):
         slot_ref[n + i] = 0
-
+    return n
+
+
+def each_slot(n, slot_ref, hang_hbm, hang_ref, sems, act):
+    @pl.loop(0, n)
+    def _(k):
+        act(pltpu.make_async_copy(hang_hbm.at[slot_ref[k]], hang_ref.at[k], sems.at[k]))
+
+
+def add_slots(acc, n, list_ref, hang_ref, tr_ref, slot_ref):
     def work(first, size):
         parts = []
         for i in range(size):
@@ -103,7 +110,7 @@
             h = slot_ref[k]
             source = list_ref[0, h] * 6 + list_ref[1, h]
             target = jnp.where(k < n, list_ref[3, h], ELEMS)
-            parts.append((target, mm(hang_ref[h], tr_ref[source], TN)))
+            parts.append((target, mm(hang_ref[k], tr_ref[source], TN)))
         for target, part in parts:
             acc[target] += part
 
@@ -122,88 +129,122 @@
     return lax.axis_index("c"), lax.axis_index("x") % 2
 
 
-def start_x(side, acc, face_ref, tr_ref):
-    for n in range(4):
-        acc[n + 4 * (1 - side)] = spread_a(flux(face_ref, tr_ref, n + 4 * side, side), 1 - side)
-        acc[n + 4 * side] = jnp.zeros((BLOCK, RHS), jnp.float32)
-
-
-def cross_part(acc, out_ref, list_ref, count_ref, face_ref, hang_ref, tr_ref, slot_ref, wanted):
-    core, _ = core_and_row()
-    side = core if wanted == 1 else 1 - core
-    for s in range(2):
-
-        @pl.when(side == s)
-        def _(s=s):
-            start_x(s, acc, face_ref, tr_ref)
-
-    add_slots(acc, wanted, 2 * core - 1, list_ref, count_ref, hang_ref, tr_ref, slot_ref)
-    out_ref[...] = acc[0:ELEMS].astype(out_ref.dtype)
+def flux(weights, tr_ref, e, f):
+    return mm(weights, tr_ref[6 * e + f], TN)
+
+
+def swap_if(flag, a, b):
+    return jnp.where(flag, b, a), jnp.where(flag, a, b)
 
 
 def edge_fluxes(face_ref, tr_ref, ya_ref, yb_ref):
     _, odd = core_and_row()
-    for parity in range(2):
-
-        @pl.when(odd == parity)
-        def _(parity=parity):
-            up_ref, down_ref = (ya_ref, yb_ref) if parity == 0 else (yb_ref, ya_ref)
-            for x in range(2):
-                for z in range(2):
-                    up_ref[2 * x + z] = flux(face_ref, tr_ref, 4 * x + 2 + z, 3)
-                    down_ref[2 * x + z] = flux(face_ref, tr_ref, 4 * x + z, 2)
+    for x in range(2):
+        for z in range(2):
+            up = flux(face_ref[1, x, z], tr_ref, 4 * x + 2 + z, 3)
+            down = flux(face_ref[2, x, z], tr_ref, 4 * x + z, 2)
+            first, second = swap_if(odd == 1, up, down)
+            ya_ref[2 * x + z] = first.astype(jnp.bfloat16)
+            yb_ref[2 * x + z] = second.astype(jnp.bfloat16)
+
+
+def cross_part(acc, out_refs, n, side, list_ref, face_ref, hang_ref, tr_ref, slot_ref):
+    for m in range(4):
+        piece = flux(face_ref[0, m // 2, m % 2], tr_ref, m + 4 * side, side)
+        acc[m + 4 * (1 - side)] = jnp.where(side == 1, spread_a(piece, 0), spread_a(piece, 1))
+        acc[m + 4 * side] = jnp.zeros((BLOCK, RHS), jnp.float32)
+    add_slots(acc, n, list_ref, hang_ref, tr_ref, slot_ref)
+    for i, ref in enumerate(out_refs):
+        size = ref.shape[0]
+        ref[...] = acc[size * i : size * i + size].astype(ref.dtype)
 
 
 def first_kernel(
-    list_ref, count_ref, rhs_hbm, inv_hbm, face_hbm, hang_hbm,
-    rhs_ref, inv_ref, face_ref, hang_ref, tr_ref, cross_ref, acc, app_ref, slot_ref, sems,
+    list_hbm, count_ref, rhs_hbm, inv_hbm, face_hbm, hang_hbm,
+    rhs_ref, inv_ref, face_ref, hang_ref, tr_ref, cross_ref, ya_ref, yb_ref,
+    acc, app_ref, list_ref, slot_ref, sems, hang_sems,
 ):
+    core, _ = core_and_row()
     copies = []
 
     def bring(source, target):
         copies.append(pltpu.make_async_copy(source, target, sems.at[len(copies)]))
         copies[-1].start()
 
+    bring(list_hbm, list_ref)
     for e in range(0, ELEMS, 2):
         pair = pl.ds(e, 2)
         bring(rhs_hbm.at[pair], rhs_ref.at[pair])
         bring(inv_hbm.at[pair], inv_ref.at[pair])
     late = len(copies)
-    bring(face_hbm, face_ref)
-    for h in range(0, HANG, 8):
-        bring(hang_hbm.at[pl.ds(h, 8)], hang_ref.at[pl.ds(h, 8)])
+    bring(face_hbm.at[core, :, :, core], face_ref.at[0])
+    bring(face_hbm.at[:, 1, :, 3], face_ref.at[1])
+    bring(face_hbm.at[:, 0, :, 2], face_ref.at[2])
+    copies[0].wait()
+    n = list_slots(1, 2 * core - 1, list_ref, count_ref, slot_ref)
+    each_slot(n, slot_ref, hang_hbm, hang_ref, hang_sems, lambda copy: copy.start())
 
     def lowered(e):
         if e % 2 == 0:
-            copies[e].wait()
             copies[e + 1].wait()
+            copies[e + 2].wait()
         return rhs_ref[e]
 
     fill_traces(lowered, inv_ref, tr_ref, app_ref)
     for copy in copies[late:]:
         copy.wait()
-    cross_part(acc, cross_ref, list_ref, count_ref, face_ref, hang_ref, tr_ref, slot_ref, 1)
-
-
-def side_kernel(list_ref, count_ref, face_ref, hang_ref, tr_ref, chip_ref, ya_ref, yb_ref, acc, slot_ref):
     edge_fluxes(face_ref, tr_ref, ya_ref, yb_ref)
-    cross_part(acc, chip_ref, list_ref, count_ref, face_ref, hang_ref, tr_ref, slot_ref, -1)
-
-
-def own_body(list_ref, count_ref, face_ref, hang_ref, tr_ref, own_ref, acc, slot_ref):
+    each_slot(n, slot_ref, hang_hbm, hang_ref, hang_sems, lambda copy: copy.wait())
+    cross_part(acc, (cross_ref,), n, core, list_ref, face_ref, hang_ref, tr_ref, slot_ref)
+
+
+def side_first_kernel(
+    list_ref, count_ref, face_hbm, hang_hbm, tr_ref, chip_ref, chip2_ref, face_ref, hang_ref, own_face_ref, own_hang_ref,
+    acc, slot_ref, own_slot_ref, sems, hang_sems, own_hang_sems,
+):
+    core, _ = core_and_row()
+    pieces = [
+        face_hbm.at[1, :, :, 0], face_hbm.at[0, :, :, 1], face_hbm.at[:, 1, :, 2],
+        face_hbm.at[:, 0, :, 3], face_hbm.at[:, :, 1, 4], face_hbm.at[:, :, 0, 5],
+    ]
+    copies = [pltpu.make_async_copy(face_hbm.at[1 - core, :, :, 1 - core], face_ref.at[0], sems.at[6])]
+    copies += [pltpu.make_async_copy(p, own_face_ref.at[f], sems.at[f]) for f, p in enumerate(pieces)]
+    copies[0].start()
+    n = list_slots(-1, 2 * core - 1, list_ref, count_ref, slot_ref)
+    each_slot(n, slot_ref, hang_hbm, hang_ref, hang_sems, lambda copy: copy.start())
+    for copy in copies[1:]:
+        copy.start()
+    own_n = list_slots(0, 1, list_ref, count_ref, own_slot_ref)
+    each_slot(own_n, own_slot_ref, hang_hbm, own_hang_ref, own_hang_sems, lambda copy: copy.start())
+    copies[0].wait()
+    each_slot(n, slot_ref, hang_hbm, hang_ref, hang_sems, lambda copy: copy.wait())
+    cross_part(acc, (chip_ref, chip2_ref), n, 1 - core, list_ref, face_ref, hang_ref, tr_ref, slot_ref)
+    for copy in copies[1:]:
+        copy.wait()
+    each_slot(own_n, own_slot_ref, hang_hbm, own_hang_ref, own_hang_sems, lambda copy: copy.wait())
+
+
+def side_second_kernel(list_ref, count_ref, face_ref, hang_ref, tr_ref, chip_ref, chip2_ref, acc, slot_ref):
+    core, _ = core_and_row()
+    n = list_slots(-1, 2 * core - 1, list_ref, count_ref, slot_ref)
+    cross_part(acc, (chip_ref, chip2_ref), n, 1 - core, list_ref, face_ref, hang_ref, tr_ref, slot_ref)
+
+
+def own_part(n, list_ref, face_ref, hang_ref, tr_ref, own_ref, acc, slot_ref):
     for e in range(ELEMS):
         x, y, z = (e >> 2) & 1, (e >> 1) & 1, e & 1
-        from_x = flux(face_ref, tr_ref, e ^ 4, 0 if x == 0 else 1)
-        from_y = flux(face_ref, tr_ref, e ^ 2, 2 if y == 0 else 3)
-        from_z = flux(face_ref, tr_ref, e ^ 1, 4 if z == 0 else 5)
+        from_x = flux(face_ref[x, y, z], tr_ref, e ^ 4, x)
+        from_y = flux(face_ref[2 + y, x, z], tr_ref, e ^ 2, 2 + y)
+        from_z = flux(face_ref[4 + z, x, y], tr_ref, e ^ 1, 4 + z)
         acc[e] = spread_a(from_x, 1 - x) + spread_b(from_y, 1 - y)
         acc[e, face_c(1 - z), :] += from_z
-    add_slots(acc, 0, 1, list_ref, count_ref, hang_ref, tr_ref, slot_ref)
+    add_slots(acc, n, list_ref, hang_ref, tr_ref, slot_ref)
     own_ref[...] = acc[0:ELEMS]
 
 
 def own_kernel(list_ref, count_ref, face_ref, hang_ref, tr_ref, own_ref, acc, slot_ref):
-    own_body(list_ref, count_ref, face_ref, hang_ref, tr_ref, own_ref, acc, slot_ref)
+    n = list_slots(0, 1, list_ref, count_ref, slot_ref)
+    own_part(n, list_ref, face_ref, hang_ref, tr_ref, own_ref, acc, slot_ref)
 
 
 def inner(e, *pairs):
@@ -221,36 +262,40 @@
 def own_gram_kernel(
     list_ref, count_ref, face_ref, hang_ref, tr_ref, rhs_ref, w1_ref, own_ref, gram_ref, acc, slot_ref
 ):
-    own_body(list_ref, count_ref, face_ref, hang_ref, tr_ref, own_ref, acc, slot_ref)
+    n = list_slots(0, 1, list_ref, count_ref, slot_ref)
+    own_part(n, list_ref, face_ref, hang_ref, tr_ref, own_ref, acc, slot_ref)
     gram_ref[...] = gram_rows((rhs_ref, rhs_ref), (rhs_ref, w1_ref), (w1_ref, w1_ref))
 
 
-def land(w_ref, own_ref, cross_ref, chip_ref, ya_ref, yb_ref):
+def landed(e, own_ref, cross_ref, chip_refs, ya_ref, yb_ref):
     _, odd = core_and_row()
-    for parity in range(2):
-
-        @pl.when(odd == parity)
-        def _(parity=parity):
-            from_up, from_down = (ya_ref, yb_ref) if parity == 0 else (yb_ref, ya_ref)
-            for e in range(ELEMS):
-                y = (e >> 1) & 1
-                n = 2 * (e >> 2) + (e & 1)
-                edge = spread_b(from_up[n], 1) if y else spread_b(from_down[n], 0)
-                came = cross_ref[e].astype(jnp.float32) + chip_ref[e].astype(jnp.float32)
-                w_ref[e] = own_ref[e] + came + edge
+    y = (e >> 1) & 1
+    n = 2 * (e >> 2) + (e & 1)
+    edge = swap_if(odd == 1, ya_ref[n].astype(jnp.float32), yb_ref[n].astype(jnp.float32))[1 - y]
+    came = cross_ref[e].astype(jnp.float32) + chip_refs[e // 4][e % 4].astype(jnp.float32)
+    return own_ref[e] + came + spread_b(edge, y)
 
 
 def second_kernel(
-    list_ref, count_ref, own_ref, in_cross, in_chip, in_ya, in_yb, inv_ref, face_ref, hang_ref,
-    w_ref, tr_ref, cross_ref, acc, app_ref, slot_ref,
+    list_ref, count_ref, own_ref, in_cross, in_chip, in_chip2, in_ya, in_yb, inv_ref, face_ref, hang_ref,
+    w_ref, tr_ref, cross_ref, ya_ref, yb_ref, acc, app_ref, slot_ref,
 ):
-    land(w_ref, own_ref, in_cross, in_chip, in_ya, in_yb)
-    fill_traces(lambda e: w_ref[e].astype(jnp.bfloat16), inv_ref, tr_ref, app_ref)
-    cross_part(acc, cross_ref, list_ref, count_ref, face_ref, hang_ref, tr_ref, slot_ref, 1)
-
-
-def last_kernel(own_ref, in_cross, in_chip, in_ya, in_yb, rhs_ref, w1_ref, early_ref, w_ref, keep_ref, give_ref):
-    land(w_ref, own_ref, in_cross, in_chip, in_ya, in_yb)
+
+    def lowered(e):
+        w = landed(e, own_ref, in_cross, (in_chip, in_chip2), in_ya, in_yb)
+        w_ref[e] = w
+        return w.astype(jnp.bfloat16)
+
+    fill_traces(lowered, inv_ref, tr_ref, app_ref)
+    edge_fluxes(face_ref, tr_ref, ya_ref, yb_ref)
+    core, _ = core_and_row()
+    n = list_slots(1, 2 * core - 1, list_ref, count_ref, slot_ref)
+    cross_part(acc, (cross_ref,), n, core, list_ref, face_ref, hang_ref, tr_ref, slot_ref)
+
+
+def last_kernel(own_ref, in_cross, in_chip, in_chip2, in_ya, in_yb, rhs_ref, w1_ref, early_ref, w_ref, keep_ref, give_ref):
+    for e in range(ELEMS):
+        w_ref[e] = landed(e, own_ref, in_cross, (in_chip, in_chip2), in_ya, in_yb)
     late = gram_rows((rhs_ref, w_ref), (w1_ref, w_ref), (w_ref, w_ref))
     early = early_ref[...]
     core, _ = core_and_row()
@@ -304,6 +349,7 @@
 FIELD = (ELEMS, BLOCK, RHS)
 TRACES = (6 * ELEMS, FACE, RHS)
 SIDE = (4, FACE, RHS)
+HALF = (4, BLOCK, RHS)
 SMEM = pl.BlockSpec(memory_space=pltpu.SMEM)
 VMEM = pl.BlockSpec(memory_space=pltpu.VMEM)
 HBM = pl.BlockSpec(memory_space=pltpu.HBM)
@@ -334,52 +380,64 @@
     bf16 = jnp.bfloat16
     million = 10**6
     scalars = [SMEM, SMEM]
-
-    rhs, inv, face, hang, traces, cross = call(
-        first_kernel, scalars + [HBM] * 4,
+    sems = lambda n: pltpu.SemaphoreType.DMA((n,))
+    faces = stay(face_block)
+    hangs = stay(hang_block.reshape(HANG, FACE, BLOCK))
+    packed = shape((HANG, FACE, BLOCK), bf16)
+    held = lambda n: shape((n, 2, 2, FACE, FACE), bf16)
+    halves = [shape(HALF, bf16)] * 2
+    sent = [shape(TRACES, bf16), shape(FIELD, bf16), shape(SIDE, bf16), shape(SIDE, bf16)]
+
+    rhs, inv, face, hang, traces, *out = call(
+        first_kernel, [HBM, SMEM] + [HBM] * 4, [shape(FIELD, bf16), shape((ELEMS, BLOCK, BLOCK), bf16), held(3), packed] + sent,
         [
-            shape(FIELD, bf16), shape((ELEMS, BLOCK, BLOCK), bf16), shape((6 * ELEMS, FACE, FACE), bf16),
-            shape((HANG, FACE, BLOCK), bf16), shape(TRACES, bf16), shape(FIELD, bf16),
+            acc, field, pltpu.SMEM((4, HANG), jnp.int32), slots,
+            sems(ELEMS + 4), sems(HANG),
         ],
-        [acc, field, slots, pltpu.SemaphoreType.DMA((ELEMS + 5,))],
         300 * million, 6 * million,
-    )(
-        rows, count, stay(rhs_field.reshape(FIELD)), stay(inv_block.reshape(ELEMS, BLOCK, BLOCK)),
-        stay(face_block.reshape(6 * ELEMS, FACE, FACE)), stay(hang_block.reshape(HANG, FACE, BLOCK)),
-    )
-
-    def exchange(traces, cross, own_call):
+    )(rows, count, stay(rhs_field.reshape(FIELD)), stay(inv_block.reshape(ELEMS, BLOCK, BLOCK)), faces, hangs)
+
+    def exchange(out, side_call, own_call):
+        cross, ya, yb = out
         in_cross = lax.ppermute(cross, ("z", "y", "c"), pairs["cross"])
-        chip, ya, yb = call(
-            side_kernel, scalars + [VMEM] * 3, [shape(FIELD, bf16), shape(SIDE), shape(SIDE)], [acc, slots],
-            100 * million, 4 * million,
-        )(rows, count, face, hang, traces)
         in_ya = lax.ppermute(ya, "x", pairs["even"])
         in_yb = lax.ppermute(yb, "x", pairs["odd"])
-        in_chip = lax.ppermute(chip, "c", [(0, 1), (1, 0)])
-        return own_call(traces), (in_cross, in_chip, in_ya, in_yb)
-
-    def own_first(traces):
+        low, high, *weights = side_call()
+        in_chip = [lax.ppermute(part, "c", [(0, 1), (1, 0)]) for part in (low, high)]
+        own, *rest = own_call(weights[2:])
+        return (own, in_cross, *in_chip, in_ya, in_yb), weights, rest
+
+    def side_first():
         return call(
-            own_kernel, scalars + [VMEM] * 3, [shape(FIELD)], [acc, slots], 100 * million, 6 * million
-        )(rows, count, face, hang, traces)[0]
-
-    own, arrived = exchange(traces, cross, own_first)
-    w1, traces, cross = call(
-        second_kernel, scalars + [VMEM] * 8, [shape(FIELD), shape(TRACES, bf16), shape(FIELD, bf16)],
-        [acc, field, slots], 300 * million, 8 * million,
-    )(rows, count, own, *arrived, inv, face, hang)
-
-    def own_second(traces):
+            side_first_kernel, scalars + [HBM, HBM, VMEM], halves + [held(1), packed, held(6), packed],
+            [acc, slots, slots, sems(7), sems(HANG), sems(HANG)], SIDE_FLOPS, 4 * million,
+        )(rows, count, faces, hangs, traces)
+
+    def own_first(weights):
+        return call(own_kernel, scalars + [VMEM] * 3, [shape(FIELD)], [acc, slots], OWN_FLOPS, 6 * million)(
+            rows, count, *weights, traces
+        )
+
+    arrived, weights, _ = exchange(out, side_first, own_first)
+    w1, traces, *out = call(
+        second_kernel, scalars + [VMEM] * 9, [shape(FIELD)] + sent, [acc, field, slots], 300 * million, 8 * million,
+    )(rows, count, *arrived, inv, face, hang)
+
+    def side_second():
+        return call(side_second_kernel, scalars + [VMEM] * 3, halves, [acc, slots], SIDE_FLOPS, 4 * million)(
+            rows, count, *weights[:2], traces
+        )
+
+    def own_second(_):
         return call(
             own_gram_kernel, scalars + [VMEM] * 5, [shape(FIELD), shape((1, 3 * RHS))], [acc, slots],
-            100 * million, 6 * million,
-        )(rows, count, face, hang, traces, rhs, w1)
-
-    (own, early), arrived = exchange(traces, cross, own_second)
+            OWN_FLOPS, 6 * million,
+        )(rows, count, *weights[2:], traces, rhs, w1)
+
+    arrived, _, (early,) = exchange(out, side_second, own_second)
     w2, keep, give = call(
-        last_kernel, [VMEM] * 8, [shape(FIELD), shape((1, 3 * RHS)), shape((1, 3 * RHS))], [], 10 * million, 8 * million
-    )(own, *arrived, rhs, w1, early)
+        last_kernel, [VMEM] * 9, [shape(FIELD), shape((1, 3 * RHS)), shape((1, 3 * RHS))], [], 10 * million, 8 * million
+    )(*arrived, rhs, w1, early)
 
     swap = [(0, 1), (1, 0)]
     part = keep + lax.ppermute(give, "c", swap)

time: 74 us -> 72.7 us (0.982)
  waiting for transfers between devices: 4.88 us -> 2.48 us
  blocking collectives: 30.6 us -> 32 us
    ppermute x2, waiting for transfers between devices: 2.38 us -> 0.01 us  [exchange(): in_ya = lax.ppermute(ya, 'x', pairs['even'])]
    all_to_all x1, blocking collectives: 30.6 us -> 32 us  [per_device(): lax.all_to_all(jnp.broadcast_to(part, (chips, 1, 3 * RHS)), ('z', 'y', 'x...]
    ppermute x2 -> x4, starting transfers between devices: 0.19 us -> 1.18 us  [exchange(): lax.ppermute(part, 'c', [(0, 1), (1, 0)])]
    ppermute x1, starting transfers between devices: 1.01 us -> 0.19 us  [per_device(): part = keep + lax.ppermute(give, 'c', swap)]
  transfers between devices with their start and end apart: 10 -> 12, of which waited for: 5 -> 3; matrix products, arithmetic and copies ran while one was open for 0% -> 0% of each run, Pallas kernels for 12% -> 12%
where the time goes in v3:
time: 72.7 us; the launch traced here: 72.4 us
  blocking collectives  32 us (44%)
  starting transfers between devices  18.2 us (25%)
  Pallas kernels  17.8 us (24%)
  waiting for transfers between devices  2.48 us (3%)
  between operations  1.61 us (2%)
    all_to_all x1, blocking collectives, per_device(): lax.all_to_all(jnp.broadcast_to(part, (chips, 1, 3 * RHS)), ('z', 'y', 'x...  32 us
    ppermute x2, starting transfers between devices, exchange(): in_cross = lax.ppermute(cross, ('z', 'y', 'c'), pairs['cross'])  8.23 us
    ppermute x2, starting transfers between devices, exchange(): in_ya = lax.ppermute(ya, 'x', pairs['even'])  4.85 us
    pallas_call x1, Pallas kernels, per_device(): call(first_kernel, [HBM, SMEM] + [HBM] * 4, [shape(FIELD, bf16), shape((E...  4.01 us
    pallas_call x1, Pallas kernels, side_first(): call(side_first_kernel, scalars + [HBM, HBM, VMEM], halves + [held(1), pa...  3.24 us
    pallas_call x1, Pallas kernels, per_device(): call(second_kernel, scalars + [VMEM] * 9, [shape(FIELD)] + sent, [acc, fi...  2.51 us
    ppermute x1, starting transfers between devices, per_device(): lax.ppermute(mine, 'c', swap)  2.47 us
    pallas_call x1, Pallas kernels, own_second(): call(own_gram_kernel, scalars + [VMEM] * 5, [shape(FIELD), shape((1, 3 *...  2.31 us
  transfers between devices with their start and end apart: 12, of which 3 were waited for; matrix products, arithmetic and copies ran while one was open for 0% of the time, Pallas kernels for 12%

profile of v3, /device:TPU:1, one launch (start us, length us, event | category | flops | bytes accessed | tf_op | source)
XLA Modules:
  0.0 72.4 jit_solution(14031975824031194715)
XLA Ops:
  1.3 4.0 %shard_map.77 = (bf16[8,320,128]{2,1,0:T(8,128)(2,1)S(1)}, bf16[8,320,320]{2,1,0:T(8,128)(2,1)S(1)}, bf16[3,2,2,80,80]{4,3,2,1,0:T(8,128)(2,1)S(1)}, bf16[32,80,...) custom-call(s32[4,32]{1,0:T(4,128)} %bitcast.11, ...), custom_call_target="tpu_custom_call" | custom-call | flops 300000000 | bytes 6000000 | tf_op jit(solution)/shard_map/pallas_call | solution.py:391
  5.3 4.6 %collective-permute-start = (bf16[8,320,128]{2,1,0:T(8,128)(2,1)S(1)}, bf16[8,320,128]{2,1,0:T(8,128)(2,1)S(1)}, u32[]{:S(2)}, u32[]{:S(2)}) collective-permute-start(bf16[8,320,128]{2,1,0:T(8,128)(2,1)S(1)} %get-tuple-element.33), channel_id=1, source_target_pairs={{4,8},{8,4},{12,16},{16,12},{20,24},{24,20},{28,32},{32,28},{36,40... | collective-permute-start | bytes 1966088 | tf_op jit(solution)/shard_map/ppermute | solution.py:402
  9.9 1.3 %collective-permute-start.3 = (bf16[4,80,128]{2,1,0:T(8,128)(2,1)S(1)}, bf16[4,80,128]{2,1,0:T(8,128)(2,1)S(1)}, u32[]{:S(2)}, u32[]{:S(2)}) collective-permute-start(bf16[4,80,128]{2,1,0:T(8,128)(2,1)S(1)} %get-tuple-element.36), channel_id=1, source_target_pairs={{0,1},{1,0},{2,3},{3,2},{4,5},{5,4},{6,7},{7,6},{8,9},{9,8},{10,11... | collective-permute-start | bytes 245768 | tf_op jit(solution)/shard_map/ppermute | solution.py:403
  11.2 0.7 collective-permute-start.4
  11.9 3.2 %shard_map.78 = (bf16[4,320,128]{2,1,0:T(8,128)(2,1)S(1)}, bf16[4,320,128]{2,1,0:T(8,128)(2,1)S(1)}, bf16[1,2,2,80,80]{4,3,2,1,0:T(8,128)(2,1)S(1)}, bf16[32,80,...) custom-call(s32[4,32]{1,0:T(4,128)} %bitcast.12, ...), custom_call_target="tpu_custom_call" | custom-call | flops 100000000 | bytes 4000000 | tf_op jit(solution)/shard_map/pallas_call | solution.py:411
  15.2 0.5 collective-permute-start.2
  15.7 1.8 %shard_map.79.own_ref = f32[8,320,128]{2,1,0:T(8,128)S(1)} custom-call(s32[4,32]{1,0:T(4,128)} %bitcast.13, s32[1,1]{1,0:T(1,128)S(6)} %copy.10.count_ref, bf16[6,2,2,80,80]{4,3,2,1,0:T(8,128)(2,1)S(1)} %get-tuple-element.31.face_ref, bf16[32,80,320]{2,1,0:T(8,128)(2,1)S(1)} %get-tuple-element.32.hang_ref, bf16[48,80,128]{2,1,0:T(8,128)(2,1)S(1)} %get-tuple-element.30.tr_ref), custom_call_target="tpu_custom_call" | custom-call | flops 4000000000 | bytes 6000000 | tf_op jit(solution)/shard_map/pallas_call | solution.py:417
  17.6 0.6 collective-permute-done.in_cross
  18.2 2.5 %shard_map.80 = (f32[8,320,128]{2,1,0:T(8,128)S(1)}, bf16[48,80,128]{2,1,0:T(8,128)(2,1)S(1)}, bf16[8,320,128]{2,1,0:T(8,128)(2,1)S(1)}, bf16[4,80,128]{2,1,0:T(8,128)(2,1)S(1)}, bf16[4,80,128]{2,1,0:T(8,128)(2,1)S(1)}) custom-call(s32[4,32]{1,0:T(4,128)} %bitcast.14, s32[1,1]{1,0:T(1,128)S(6)} %copy.10.count_ref, f32[8,320,128]{2,1,0:T(8,128)S(1)} %shard_map.79.own_ref, ...), custom_call_target="tpu_custom_call" | custom-call | flops 300000000 | bytes 8000000 | tf_op jit(solution)/shard_map/pallas_call | solution.py:422
  20.7 3.6 %collective-permute-start.5 = (bf16[8,320,128]{2,1,0:T(8,128)(2,1)S(1)}, bf16[8,320,128]{2,1,0:T(8,128)(2,1)S(1)}, u32[]{:S(2)}, u32[]{:S(2)}) collective-permute-start(bf16[8,320,128]{2,1,0:T(8,128)(2,1)S(1)} %get-tuple-element.45), channel_id=1, source_target_pairs={{4,8},{8,4},{12,16},{16,12},{20,24},{24,20},{28,32},{32,28},{36,40... | collective-permute-start | bytes 1966088 | tf_op jit(solution)/shard_map/ppermute | solution.py:402
  24.3 3.5 %collective-permute-start.8 = (bf16[4,80,128]{2,1,0:T(8,128)(2,1)S(1)}, bf16[4,80,128]{2,1,0:T(8,128)(2,1)S(1)}, u32[]{:S(2)}, u32[]{:S(2)}) collective-permute-start(bf16[4,80,128]{2,1,0:T(8,128)(2,1)S(1)} %get-tuple-element.50), channel_id=1, source_target_pairs={{0,1},{1,0},{2,3},{3,2},{4,5},{5,4},{6,7},{7,6},{8,9},{9,8},{10,11... | collective-permute-start | bytes 245768 | tf_op jit(solution)/shard_map/ppermute | solution.py:403
  27.9 0.7 collective-permute-start.9
  28.5 1.5 %shard_map.82 = (bf16[4,320,128]{2,1,0:T(8,128)(2,1)S(1)}, bf16[4,320,128]{2,1,0:T(8,128)(2,1)S(1)}) custom-call(s32[4,32]{1,0:T(4,128)} %bitcast.15, s32[1,1]{1,0:T(1,128)S(6)} %copy.10.count_ref, bf16[1,2,2,80,80]{4,3,2,1,0:T(8,128)(2,1)S(1)} %get-tuple-element.46.face_ref, bf16[32,80,320]{2,1,0:T(8,128)(2,1)S(1)} %get-tuple-element.47.hang_ref, ...), custom_call_target="tpu_custom_call" | custom-call | flops 100000000 | bytes 4000000 | tf_op jit(solution)/shard_map/pallas_call | solution.py:427
  30.2 0.5 collective-permute-start.7
  30.7 2.3 %shard_map.81 = (f32[8,320,128]{2,1,0:T(8,128)S(1)}, f32[1,384]{1,0:T(1,128)S(1)}) custom-call(s32[4,32]{1,0:T(4,128)} %bitcast.16, s32[1,1]{1,0:T(1,128)S(6)} %copy.10.count_ref, bf16[6,2,2,80,80]{4,3,2,1,0:T(8,128)(2,1)S(1)} %get-tuple-element.31.face_ref, bf16[32,80,320]{2,1,0:T(8,128)(2,1)S(1)} %get-tuple-element.32.hang_ref, ...), custom_call_target="tpu_custom_call" | custom-call | flops 4000000000 | bytes 6000000 | tf_op jit(solution)/shard_map/pallas_call | solution.py:432
  33.0 0.6 shard_map.83
  33.7 0.2 collective-permute-start.10
  33.8 1.1 %collective-permute-done.10 = f32[1,384]{1,0:T(1,128)S(1)} collective-permute-done((f32[1,384]{1,0:T(1,128)S(1)}, f32[1,384]{1,0:T(1,128)S(1)}, u32[]{:S(2)}, u32[]{:S(2)}) %collective-permute-start.10) | collective-permute-done | bytes 1568 | tf_op jit(solution)/shard_map/ppermute | solution.py:443
  34.9 0.1 broadcast_in_dim.3
  35.0 32.0 %all_to_all.5 = f32[128,1,384]{2,1,0:T(1,128)S(1)} all-to-all(f32[128,1,384]{2,1,0:T(1,128)S(1)} %broadcast_in_dim.3), channel_id=1, replica_groups=mesh['z'=8,'y'=4,'c'=2,'x'=4] {'z','y','x'}, dimensions={0} | all-to-all | bytes 393216 | tf_op jit(solution)/shard_map/all_to_all | solution.py:445
  67.0 0.2 reduce_sum.11
  67.2 2.5 %collective-permute-start.11 = (f32[1,384]{1,0:T(1,128)S(1)}, f32[1,384]{1,0:T(1,128)S(1)}, u32[]{:S(2)}, u32[]{:S(2)}) collective-permute-start(f32[1,384]{1,0:T(1,128)S(1)} %reduce_sum.12.mine_ref), channel_id=1, source_target_pairs={{0,4},{4,0},{1,5},{5,1},{2,6},{6,2},{3,7},{7,3},{8,12},{12,8},{9,1... | collective-permute-start | bytes 4616 | tf_op jit(solution)/shard_map/ppermute | solution.py:449
  69.7 0.8 %collective-permute-done.11.other_ref = f32[1,384]{1,0:T(1,128)S(1)} collective-permute-done((f32[1,384]{1,0:T(1,128)S(1)}, f32[1,384]{1,0:T(1,128)S(1)}, u32[]{:S(2)}, u32[]{:S(2)}) %collective-permute-start.11) | collective-permute-done | bytes 1568 | tf_op jit(solution)/shard_map/ppermute | solution.py:449
  70.5 1.8 %shard_map.84 = (f32[8,320,128]{2,1,0:T(8,128)}, f32[3,2,128]{2,1,0:T(2,128)}) custom-call(f32[1,384]{1,0:T(1,128)S(1)} %reduce_sum.12.mine_ref, f32[1,384]{1,0:T(1,128)S(1)} %collective-permute-done.11.other_ref, bf16[8,320,128]{2,1,0:T(8,128)(2,1)S(1)} %get-tuple-element.42.rhs_ref, f32[8,320,128]{2,1,0:T(8,128)S(1)} %get-tuple-element.43.w1_ref, ...), custom_call_target="tpu_custom_call" | custom-call | flops 10000000 | bytes 6000000 | tf_op jit(solution)/shard_map/pallas_call | solution.py:446
  (13 shorter events, 0.2 us)
Async XLA Ops:
  5.3 12.9 %collective-permute-start = (bf16[8,320,128]{2,1,0:T(8,128)(2,1)S(1)}, bf16[8,320,128]{2,1,0:T(8,128)(2,1)S(1)}, u32[]{:S(2)}, u32[]{:S(2)}) collective-permute-start(bf16[8,320,128]{2,1,0:T(8,128)(2,1)S(1)} %get-tuple-element.33), channel_id=1, source_target_pairs={{4,8},{8,4},{12,16},{16,12},{20,24},{24,20},{28,32},{32,28},{36,40... | collective-permute-start | bytes 1966088 | tf_op jit(solution)/shard_map/ppermute | solution.py:402
  9.9 7.6 %collective-permute-start.3 = (bf16[4,80,128]{2,1,0:T(8,128)(2,1)S(1)}, bf16[4,80,128]{2,1,0:T(8,128)(2,1)S(1)}, u32[]{:S(2)}, u32[]{:S(2)}) collective-permute-start(bf16[4,80,128]{2,1,0:T(8,128)(2,1)S(1)} %get-tuple-element.36), channel_id=1, source_target_pairs={{0,1},{1,0},{2,3},{3,2},{4,5},{5,4},{6,7},{7,6},{8,9},{9,8},{10,11... | collective-permute-start | bytes 245768 | tf_op jit(solution)/shard_map/ppermute | solution.py:403
  11.2 6.3 %collective-permute-start.4 = (bf16[4,80,128]{2,1,0:T(8,128)(2,1)S(1)}, bf16[4,80,128]{2,1,0:T(8,128)(2,1)S(1)}, u32[]{:S(2)}, u32[]{:S(2)}) collective-permute-start(bf16[4,80,128]{2,1,0:T(8,128)(2,1)S(1)} %get-tuple-element.37), channel_id=1, source_target_pairs={{1,2},{2,1},{5,6},{6,5},{9,10},{10,9},{13,14},{14,13},{17,18},{18,... | collective-permute-start | bytes 245768 | tf_op jit(solution)/shard_map/ppermute | solution.py:404
  15.1 2.4 %collective-permute-start.1 = (bf16[4,320,128]{2,1,0:T(8,128)(2,1)S(1)}, bf16[4,320,128]{2,1,0:T(8,128)(2,1)S(1)}, u32[]{:S(2)}, u32[]{:S(2)}) collective-permute-start(bf16[4,320,128]{2,1,0:T(8,128)(2,1)S(1)} %get-tuple-element.34), channel_id=1, source_target_pairs={{0,4},{4,0},{1,5},{5,1},{2,6},{6,2},{3,7},{7,3},{8,12},{12,8},{9,1... | collective-permute-start | bytes 983048 | tf_op jit(solution)/shard_map/ppermute | solution.py:406
  15.2 2.4 %collective-permute-start.2 = (bf16[4,320,128]{2,1,0:T(8,128)(2,1)S(1)}, bf16[4,320,128]{2,1,0:T(8,128)(2,1)S(1)}, u32[]{:S(2)}, u32[]{:S(2)}) collective-permute-start(bf16[4,320,128]{2,1,0:T(8,128)(2,1)S(1)} %get-tuple-element.35), channel_id=1, source_target_pairs={{0,4},{4,0},{1,5},{5,1},{2,6},{6,2},{3,7},{7,3},{8,12},{12,8},{9,1... | collective-permute-start | bytes 983048 | tf_op jit(solution)/shard_map/ppermute | solution.py:406
  20.7 12.3 %collective-permute-start.5 = (bf16[8,320,128]{2,1,0:T(8,128)(2,1)S(1)}, bf16[8,320,128]{2,1,0:T(8,128)(2,1)S(1)}, u32[]{:S(2)}, u32[]{:S(2)}) collective-permute-start(bf16[8,320,128]{2,1,0:T(8,128)(2,1)S(1)} %get-tuple-element.45), channel_id=1, source_target_pairs={{4,8},{8,4},{12,16},{16,12},{20,24},{24,20},{28,32},{32,28},{36,40... | collective-permute-start | bytes 1966088 | tf_op jit(solution)/shard_map/ppermute | solution.py:402
  24.3 8.7 %collective-permute-start.8 = (bf16[4,80,128]{2,1,0:T(8,128)(2,1)S(1)}, bf16[4,80,128]{2,1,0:T(8,128)(2,1)S(1)}, u32[]{:S(2)}, u32[]{:S(2)}) collective-permute-start(bf16[4,80,128]{2,1,0:T(8,128)(2,1)S(1)} %get-tuple-element.50), channel_id=1, source_target_pairs={{0,1},{1,0},{2,3},{3,2},{4,5},{5,4},{6,7},{7,6},{8,9},{9,8},{10,11... | collective-permute-start | bytes 245768 | tf_op jit(solution)/shard_map/ppermute | solution.py:403
  27.9 5.1 %collective-permute-start.9 = (bf16[4,80,128]{2,1,0:T(8,128)(2,1)S(1)}, bf16[4,80,128]{2,1,0:T(8,128)(2,1)S(1)}, u32[]{:S(2)}, u32[]{:S(2)}) collective-permute-start(bf16[4,80,128]{2,1,0:T(8,128)(2,1)S(1)} %get-tuple-element.51), channel_id=1, source_target_pairs={{1,2},{2,1},{5,6},{6,5},{9,10},{10,9},{13,14},{14,13},{17,18},{18,... | collective-permute-start | bytes 245768 | tf_op jit(solution)/shard_map/ppermute | solution.py:404
  30.1 2.9 %collective-permute-start.6 = (bf16[4,320,128]{2,1,0:T(8,128)(2,1)S(1)}, bf16[4,320,128]{2,1,0:T(8,128)(2,1)S(1)}, u32[]{:S(2)}, u32[]{:S(2)}) collective-permute-start(bf16[4,320,128]{2,1,0:T(8,128)(2,1)S(1)} %get-tuple-element.48), channel_id=1, source_target_pairs={{0,4},{4,0},{1,5},{5,1},{2,6},{6,2},{3,7},{7,3},{8,12},{12,8},{9,1... | collective-permute-start | bytes 983048 | tf_op jit(solution)/shard_map/ppermute | solution.py:406
  30.2 2.8 %collective-permute-start.7 = (bf16[4,320,128]{2,1,0:T(8,128)(2,1)S(1)}, bf16[4,320,128]{2,1,0:T(8,128)(2,1)S(1)}, u32[]{:S(2)}, u32[]{:S(2)}) collective-permute-start(bf16[4,320,128]{2,1,0:T(8,128)(2,1)S(1)} %get-tuple-element.49), channel_id=1, source_target_pairs={{0,4},{4,0},{1,5},{5,1},{2,6},{6,2},{3,7},{7,3},{8,12},{12,8},{9,1... | collective-permute-start | bytes 983048 | tf_op jit(solution)/shard_map/ppermute | solution.py:406
  33.7 1.2 %collective-permute-start.10 = (f32[1,384]{1,0:T(1,128)S(1)}, f32[1,384]{1,0:T(1,128)S(1)}, u32[]{:S(2)}, u32[]{:S(2)}) collective-permute-start(f32[1,384]{1,0:T(1,128)S(1)} %get-tuple-element.54), channel_id=1, source_target_pairs={{0,4},{4,0},{1,5},{5,1},{2,6},{6,2},{3,7},{7,3},{8,12},{12,8},{9,1... | collective-permute-start | bytes 4616 | tf_op jit(solution)/shard_map/ppermute | solution.py:443
  67.2 3.3 %collective-permute-start.11 = (f32[1,384]{1,0:T(1,128)S(1)}, f32[1,384]{1,0:T(1,128)S(1)}, u32[]{:S(2)}, u32[]{:S(2)}) collective-permute-start(f32[1,384]{1,0:T(1,128)S(1)} %reduce_sum.12.mine_ref), channel_id=1, source_target_pairs={{0,4},{4,0},{1,5},{5,1},{2,6},{6,2},{3,7},{7,3},{8,12},{12,8},{9,1... | collective-permute-start | bytes 4616 | tf_op jit(solution)/shard_map/ppermute | solution.py:449

commit v4 on v3

--- a/solution.py
+++ b/solution.py
@@ -96,6 +96,17 @@
     return n
 
 
+def fetch_list(wanted, sign, list_hbm, list_ref, count_ref, slot_ref, sem):
+    copy = pltpu.make_async_copy(list_hbm, list_ref, sem)
+    copy.start()
+
+    def listing():
+        copy.wait()
+        return list_slots(wanted, sign, list_ref, count_ref, slot_ref)
+
+    return listing
+
+
 def each_slot(n, slot_ref, hang_hbm, hang_ref, sems, act):
     @pl.loop(0, n)
     def _(k):
@@ -148,12 +159,12 @@
             yb_ref[2 * x + z] = second.astype(jnp.bfloat16)
 
 
-def cross_part(acc, out_refs, n, side, list_ref, face_ref, hang_ref, tr_ref, slot_ref):
+def cross_part(acc, out_refs, listing, side, list_ref, face_ref, hang_ref, tr_ref, slot_ref):
     for m in range(4):
         piece = flux(face_ref[0, m // 2, m % 2], tr_ref, m + 4 * side, side)
         acc[m + 4 * (1 - side)] = jnp.where(side == 1, spread_a(piece, 0), spread_a(piece, 1))
         acc[m + 4 * side] = jnp.zeros((BLOCK, RHS), jnp.float32)
-    add_slots(acc, n, list_ref, hang_ref, tr_ref, slot_ref)
+    add_slots(acc, listing(), list_ref, hang_ref, tr_ref, slot_ref)
     for i, ref in enumerate(out_refs):
         size = ref.shape[0]
         ref[...] = acc[size * i : size * i + size].astype(ref.dtype)
@@ -195,7 +206,7 @@
         copy.wait()
     edge_fluxes(face_ref, tr_ref, ya_ref, yb_ref)
     each_slot(n, slot_ref, hang_hbm, hang_ref, hang_sems, lambda copy: copy.wait())
-    cross_part(acc, (cross_ref,), n, core, list_ref, face_ref, hang_ref, tr_ref, slot_ref)
+    cross_part(acc, (cross_ref,), lambda: n, core, list_ref, face_ref, hang_ref, tr_ref, slot_ref)
 
 
 def side_first_kernel(
@@ -218,19 +229,21 @@
     each_slot(own_n, own_slot_ref, hang_hbm, own_hang_ref, own_hang_sems, lambda copy: copy.start())
     copies[0].wait()
     each_slot(n, slot_ref, hang_hbm, hang_ref, hang_sems, lambda copy: copy.wait())
-    cross_part(acc, (chip_ref, chip2_ref), n, 1 - core, list_ref, face_ref, hang_ref, tr_ref, slot_ref)
+    cross_part(acc, (chip_ref, chip2_ref), lambda: n, 1 - core, list_ref, face_ref, hang_ref, tr_ref, slot_ref)
     for copy in copies[1:]:
         copy.wait()
     each_slot(own_n, own_slot_ref, hang_hbm, own_hang_ref, own_hang_sems, lambda copy: copy.wait())
 
 
-def side_second_kernel(list_ref, count_ref, face_ref, hang_ref, tr_ref, chip_ref, chip2_ref, acc, slot_ref):
-    core, _ = core_and_row()
-    n = list_slots(-1, 2 * core - 1, list_ref, count_ref, slot_ref)
-    cross_part(acc, (chip_ref, chip2_ref), n, 1 - core, list_ref, face_ref, hang_ref, tr_ref, slot_ref)
-
-
-def own_part(n, list_ref, face_ref, hang_ref, tr_ref, own_ref, acc, slot_ref):
+def side_second_kernel(
+    list_hbm, count_ref, face_ref, hang_ref, tr_ref, chip_ref, chip2_ref, acc, slot_ref, list_ref, sem
+):
+    core, _ = core_and_row()
+    listing = fetch_list(-1, 2 * core - 1, list_hbm, list_ref, count_ref, slot_ref, sem)
+    cross_part(acc, (chip_ref, chip2_ref), listing, 1 - core, list_ref, face_ref, hang_ref, tr_ref, slot_ref)
+
+
+def own_part(listing, list_ref, face_ref, hang_ref, tr_ref, own_ref, acc, slot_ref):
     for e in range(ELEMS):
         x, y, z = (e >> 2) & 1, (e >> 1) & 1, e & 1
         from_x = flux(face_ref[x, y, z], tr_ref, e ^ 4, x)
@@ -238,13 +251,13 @@
         from_z = flux(face_ref[4 + z, x, y], tr_ref, e ^ 1, 4 + z)
         acc[e] = spread_a(from_x, 1 - x) + spread_b(from_y, 1 - y)
         acc[e, face_c(1 - z), :] += from_z
-    add_slots(acc, n, list_ref, hang_ref, tr_ref, slot_ref)
+    add_slots(acc, listing(), list_ref, hang_ref, tr_ref, slot_ref)
     own_ref[...] = acc[0:ELEMS]
 
 
-def own_kernel(list_ref, count_ref, face_ref, hang_ref, tr_ref, own_ref, acc, slot_ref):
-    n = list_slots(0, 1, list_ref, count_ref, slot_ref)
-    own_part(n, list_ref, face_ref, hang_ref, tr_ref, own_ref, acc, slot_ref)
+def own_kernel(list_hbm, count_ref, face_ref, hang_ref, tr_ref, own_ref, acc, slot_ref, list_ref, sem):
+    listing = fetch_list(0, 1, list_hbm, list_ref, count_ref, slot_ref, sem)
+    own_part(listing, list_ref, face_ref, hang_ref, tr_ref, own_ref, acc, slot_ref)
 
 
 def inner(e, *pairs):
@@ -260,10 +273,10 @@
 
 
 def own_gram_kernel(
-    list_ref, count_ref, face_ref, hang_ref, tr_ref, rhs_ref, w1_ref, own_ref, gram_ref, acc, slot_ref
+    list_hbm, count_ref, face_ref, hang_ref, tr_ref, rhs_ref, w1_ref, own_ref, gram_ref, acc, slot_ref, list_ref, sem
 ):
-    n = list_slots(0, 1, list_ref, count_ref, slot_ref)
-    own_part(n, list_ref, face_ref, hang_ref, tr_ref, own_ref, acc, slot_ref)
+    listing = fetch_list(0, 1, list_hbm, list_ref, count_ref, slot_ref, sem)
+    own_part(listing, list_ref, face_ref, hang_ref, tr_ref, own_ref, acc, slot_ref)
     gram_ref[...] = gram_rows((rhs_ref, rhs_ref), (rhs_ref, w1_ref), (w1_ref, w1_ref))
 
 
@@ -277,9 +290,11 @@
 
 
 def second_kernel(
-    list_ref, count_ref, own_ref, in_cross, in_chip, in_chip2, in_ya, in_yb, inv_ref, face_ref, hang_ref,
-    w_ref, tr_ref, cross_ref, ya_ref, yb_ref, acc, app_ref, slot_ref,
+    list_hbm, count_ref, own_ref, in_cross, in_chip, in_chip2, in_ya, in_yb, inv_ref, face_ref, hang_ref,
+    w_ref, tr_ref, cross_ref, ya_ref, yb_ref, acc, app_ref, slot_ref, list_ref, sem,
 ):
+    core, _ = core_and_row()
+    listing = fetch_list(1, 2 * core - 1, list_hbm, list_ref, count_ref, slot_ref, sem)
 
     def lowered(e):
         w = landed(e, own_ref, in_cross, (in_chip, in_chip2), in_ya, in_yb)
@@ -288,9 +303,7 @@
 
     fill_traces(lowered, inv_ref, tr_ref, app_ref)
     edge_fluxes(face_ref, tr_ref, ya_ref, yb_ref)
-    core, _ = core_and_row()
-    n = list_slots(1, 2 * core - 1, list_ref, count_ref, slot_ref)
-    cross_part(acc, (cross_ref,), n, core, list_ref, face_ref, hang_ref, tr_ref, slot_ref)
+    cross_part(acc, (cross_ref,), listing, core, list_ref, face_ref, hang_ref, tr_ref, slot_ref)
 
 
 def last_kernel(own_ref, in_cross, in_chip, in_chip2, in_ya, in_yb, rhs_ref, w1_ref, early_ref, w_ref, keep_ref, give_ref):
@@ -380,6 +393,8 @@
     bf16 = jnp.bfloat16
     million = 10**6
     scalars = [SMEM, SMEM]
+    later = [HBM, SMEM]
+    lists = [slots, pltpu.SMEM((4, HANG), jnp.int32), pltpu.SemaphoreType.DMA]
     sems = lambda n: pltpu.SemaphoreType.DMA((n,))
     faces = stay(face_block)
     hangs = stay(hang_block.reshape(HANG, FACE, BLOCK))
@@ -414,23 +429,23 @@
         )(rows, count, faces, hangs, traces)
 
     def own_first(weights):
-        return call(own_kernel, scalars + [VMEM] * 3, [shape(FIELD)], [acc, slots], OWN_FLOPS, 6 * million)(
+        return call(own_kernel, later + [VMEM] * 3, [shape(FIELD)], [acc, *lists], OWN_FLOPS, 6 * million)(
             rows, count, *weights, traces
         )
 
     arrived, weights, _ = exchange(out, side_first, own_first)
     w1, traces, *out = call(
-        second_kernel, scalars + [VMEM] * 9, [shape(FIELD)] + sent, [acc, field, slots], 300 * million, 8 * million,
+        second_kernel, later + [VMEM] * 9, [shape(FIELD)] + sent, [acc, field, *lists], 300 * million, 8 * million,
     )(rows, count, *arrived, inv, face, hang)
 
     def side_second():
-        return call(side_second_kernel, scalars + [VMEM] * 3, halves, [acc, slots], SIDE_FLOPS, 4 * million)(
+        return call(side_second_kernel, later + [VMEM] * 3, halves, [acc, *lists], SIDE_FLOPS, 4 * million)(
             rows, count, *weights[:2], traces
         )
 
     def own_second(_):
         return call(
-            own_gram_kernel, scalars + [VMEM] * 5, [shape(FIELD), shape((1, 3 * RHS))], [acc, slots],
+            own_gram_kernel, later + [VMEM] * 5, [shape(FIELD), shape((1, 3 * RHS))], [acc, *lists],
             OWN_FLOPS, 6 * million,
         )(rows, count, *weights[2:], traces, rhs, w1)
 

time: 72.7 us -> 72.1 us (level)
  Pallas kernels: 17.8 us -> 16.4 us
  waiting for transfers between devices: 2.48 us -> 3.39 us
  starting transfers between devices: 18.2 us -> 17.3 us
  blocking collectives: 32 us -> 32.8 us
    pallas_call x4, Pallas kernels: 8.17 us -> 6.75 us  [the longest x1 2.11 us: own_second(): call(own_gram_kernel, later + [VMEM] * 5, [shape(FIELD), shape((1, 3 * RH...]
    ppermute x2, waiting for transfers between devices: 0.58 us -> 1.41 us  [exchange(): in_cross = lax.ppermute(cross, ('z', 'y', 'c'), pairs['cross'])]
    all_to_all x1, blocking collectives: 32 us -> 32.8 us  [per_device(): lax.all_to_all(jnp.broadcast_to(part, (chips, 1, 3 * RHS)), ('z', 'y', 'x...]
  transfers between devices with their start and end apart: 12 -> 12, of which waited for: 3 -> 4; matrix products, arithmetic and copies ran while one was open for 0% -> 0% of each run, Pallas kernels for 12% -> 12%
where the time goes in v4:
time: 72.1 us; the launch traced here: 71.8 us
  blocking collectives  32.8 us (45%)
  starting transfers between devices  17.3 us (24%)
  Pallas kernels  16.4 us (23%)
  waiting for transfers between devices  3.39 us (5%)
  between operations  1.62 us (2%)
    all_to_all x1, blocking collectives, per_device(): lax.all_to_all(jnp.broadcast_to(part, (chips, 1, 3 * RHS)), ('z', 'y', 'x...  32.8 us
    ppermute x2, starting transfers between devices, exchange(): in_cross = lax.ppermute(cross, ('z', 'y', 'c'), pairs['cross'])  8.03 us
    ppermute x2, starting transfers between devices, exchange(): in_ya = lax.ppermute(ya, 'x', pairs['even'])  4.24 us
    pallas_call x1, Pallas kernels, per_device(): call(first_kernel, [HBM, SMEM] + [HBM] * 4, [shape(FIELD, bf16), shape((E...  4.02 us
    pallas_call x1, Pallas kernels, side_first(): call(side_first_kernel, scalars + [HBM, HBM, VMEM], halves + [held(1), pa...  3.26 us
    ppermute x1, starting transfers between devices, per_device(): lax.ppermute(mine, 'c', swap)  2.47 us
    pallas_call x1, Pallas kernels, own_second(): call(own_gram_kernel, later + [VMEM] * 5, [shape(FIELD), shape((1, 3 * RH...  2.11 us
    pallas_call x1, Pallas kernels, per_device(): call(functools.partial(combine_kernel, entries), [VMEM] * 5, [shape(FIELD...  1.79 us
  transfers between devices with their start and end apart: 12, of which 4 were waited for; matrix products, arithmetic and copies ran while one was open for 0% of the time, Pallas kernels for 12%

profile of v4, /device:TPU:1, one launch (start us, length us, event | category | flops | bytes accessed | tf_op | source)
XLA Modules:
  0.0 71.8 jit_solution(15669810269557701935)
XLA Ops:
  1.3 4.0 %shard_map.77 = (bf16[8,320,128]{2,1,0:T(8,128)(2,1)S(1)}, bf16[8,320,320]{2,1,0:T(8,128)(2,1)S(1)}, bf16[3,2,2,80,80]{4,3,2,1,0:T(8,128)(2,1)S(1)}, bf16[32,80,...) custom-call(s32[4,32]{1,0:T(4,128)} %bitcast.11, ...), custom_call_target="tpu_custom_call" | custom-call | flops 300000000 | bytes 6000000 | tf_op jit(solution)/shard_map/pallas_call | solution.py:406
  5.3 4.5 %collective-permute-start = (bf16[8,320,128]{2,1,0:T(8,128)(2,1)S(1)}, bf16[8,320,128]{2,1,0:T(8,128)(2,1)S(1)}, u32[]{:S(2)}, u32[]{:S(2)}) collective-permute-start(bf16[8,320,128]{2,1,0:T(8,128)(2,1)S(1)} %get-tuple-element.33), channel_id=1, source_target_pairs={{4,8},{8,4},{12,16},{16,12},{20,24},{24,20},{28,32},{32,28},{36,40... | collective-permute-start | bytes 1966088 | tf_op jit(solution)/shard_map/ppermute | solution.py:417
  9.8 1.7 %collective-permute-start.3 = (bf16[4,80,128]{2,1,0:T(8,128)(2,1)S(1)}, bf16[4,80,128]{2,1,0:T(8,128)(2,1)S(1)}, u32[]{:S(2)}, u32[]{:S(2)}) collective-permute-start(bf16[4,80,128]{2,1,0:T(8,128)(2,1)S(1)} %get-tuple-element.36), channel_id=1, source_target_pairs={{0,1},{1,0},{2,3},{3,2},{4,5},{5,4},{6,7},{7,6},{8,9},{9,8},{10,11... | collective-permute-start | bytes 245768 | tf_op jit(solution)/shard_map/ppermute | solution.py:418
  11.5 0.7 collective-permute-start.4
  12.2 3.3 %shard_map.78 = (bf16[4,320,128]{2,1,0:T(8,128)(2,1)S(1)}, bf16[4,320,128]{2,1,0:T(8,128)(2,1)S(1)}, bf16[1,2,2,80,80]{4,3,2,1,0:T(8,128)(2,1)S(1)}, bf16[32,80,...) custom-call(s32[4,32]{1,0:T(4,128)} %bitcast.12, ...), custom_call_target="tpu_custom_call" | custom-call | flops 100000000 | bytes 4000000 | tf_op jit(solution)/shard_map/pallas_call | solution.py:426
  15.5 0.5 collective-permute-start.2
  16.0 1.6 %shard_map.79.own_ref = f32[8,320,128]{2,1,0:T(8,128)S(1)} custom-call(s32[4,32]{1,0:T(4,128)} %bitcast.13, s32[1,1]{1,0:T(1,128)S(6)} %copy.10.count_ref, bf16[6,2,2,80,80]{4,3,2,1,0:T(8,128)(2,1)S(1)} %get-tuple-element.31.face_ref, bf16[32,80,320]{2,1,0:T(8,128)(2,1)S(1)} %get-tuple-element.32.hang_ref, bf16[48,80,128]{2,1,0:T(8,128)(2,1)S(1)} %get-tuple-element.30.tr_ref), custom_call_target="tpu_custom_call" | custom-call | flops 4000000000 | bytes 6000000 | tf_op jit(solution)/shard_map/pallas_call | solution.py:432
  17.7 0.3 collective-permute-done.in_cross
  18.0 1.7 %shard_map.80 = (f32[8,320,128]{2,1,0:T(8,128)S(1)}, bf16[48,80,128]{2,1,0:T(8,128)(2,1)S(1)}, bf16[8,320,128]{2,1,0:T(8,128)(2,1)S(1)}, bf16[4,80,128]{2,1,0:T(8,128)(2,1)S(1)}, bf16[4,80,128]{2,1,0:T(8,128)(2,1)S(1)}) custom-call(s32[4,32]{1,0:T(4,128)} %bitcast.14, s32[1,1]{1,0:T(1,128)S(6)} %copy.10.count_ref, f32[8,320,128]{2,1,0:T(8,128)S(1)} %shard_map.79.own_ref, ...), custom_call_target="tpu_custom_call" | custom-call | flops 300000000 | bytes 8000000 | tf_op jit(solution)/shard_map/pallas_call | solution.py:437
  19.7 3.6 %collective-permute-start.5 = (bf16[8,320,128]{2,1,0:T(8,128)(2,1)S(1)}, bf16[8,320,128]{2,1,0:T(8,128)(2,1)S(1)}, u32[]{:S(2)}, u32[]{:S(2)}) collective-permute-start(bf16[8,320,128]{2,1,0:T(8,128)(2,1)S(1)} %get-tuple-element.45), channel_id=1, source_target_pairs={{4,8},{8,4},{12,16},{16,12},{20,24},{24,20},{28,32},{32,28},{36,40... | collective-permute-start | bytes 1966088 | tf_op jit(solution)/shard_map/ppermute | solution.py:417
  23.3 2.5 %collective-permute-start.8 = (bf16[4,80,128]{2,1,0:T(8,128)(2,1)S(1)}, bf16[4,80,128]{2,1,0:T(8,128)(2,1)S(1)}, u32[]{:S(2)}, u32[]{:S(2)}) collective-permute-start(bf16[4,80,128]{2,1,0:T(8,128)(2,1)S(1)} %get-tuple-element.50), channel_id=1, source_target_pairs={{0,1},{1,0},{2,3},{3,2},{4,5},{5,4},{6,7},{7,6},{8,9},{9,8},{10,11... | collective-permute-start | bytes 245768 | tf_op jit(solution)/shard_map/ppermute | solution.py:418
  25.8 0.7 collective-permute-start.9
  26.5 1.3 %shard_map.82 = (bf16[4,320,128]{2,1,0:T(8,128)(2,1)S(1)}, bf16[4,320,128]{2,1,0:T(8,128)(2,1)S(1)}) custom-call(s32[4,32]{1,0:T(4,128)} %bitcast.15, s32[1,1]{1,0:T(1,128)S(6)} %copy.10.count_ref, bf16[1,2,2,80,80]{4,3,2,1,0:T(8,128)(2,1)S(1)} %get-tuple-element.46.face_ref, bf16[32,80,320]{2,1,0:T(8,128)(2,1)S(1)} %get-tuple-element.47.hang_ref, ...), custom_call_target="tpu_custom_call" | custom-call | flops 100000000 | bytes 4000000 | tf_op jit(solution)/shard_map/pallas_call | solution.py:442
  27.9 0.5 collective-permute-start.7
  28.4 2.1 %shard_map.81 = (f32[8,320,128]{2,1,0:T(8,128)S(1)}, f32[1,384]{1,0:T(1,128)S(1)}) custom-call(s32[4,32]{1,0:T(4,128)} %bitcast.16, s32[1,1]{1,0:T(1,128)S(6)} %copy.10.count_ref, bf16[6,2,2,80,80]{4,3,2,1,0:T(8,128)(2,1)S(1)} %get-tuple-element.31.face_ref, bf16[32,80,320]{2,1,0:T(8,128)(2,1)S(1)} %get-tuple-element.32.hang_ref, ...), custom_call_target="tpu_custom_call" | custom-call | flops 4000000000 | bytes 6000000 | tf_op jit(solution)/shard_map/pallas_call | solution.py:447
  30.6 1.1 %collective-permute-done.5.in_cross = bf16[8,320,128]{2,1,0:T(8,128)(2,1)S(1)} collective-permute-done((bf16[8,320,128]{2,1,0:T(8,128)(2,1)S(1)}, bf16[8,320,128]{2,1,0:T(8,128)(2,1)S(1)}, u32[]{:S(2)}, u32[]{:S(2)}) %collective-permute-start.5) | collective-permute-done | bytes 655392 | tf_op jit(solution)/shard_map/ppermute | solution.py:417
  31.6 0.6 shard_map.83
  32.4 1.1 %collective-permute-done.10 = f32[1,384]{1,0:T(1,128)S(1)} collective-permute-done((f32[1,384]{1,0:T(1,128)S(1)}, f32[1,384]{1,0:T(1,128)S(1)}, u32[]{:S(2)}, u32[]{:S(2)}) %collective-permute-start.10) | collective-permute-done | bytes 1568 | tf_op jit(solution)/shard_map/ppermute | solution.py:458
  33.5 0.1 broadcast_in_dim.3
  33.6 32.8 %all_to_all.5 = f32[128,1,384]{2,1,0:T(1,128)S(1)} all-to-all(f32[128,1,384]{2,1,0:T(1,128)S(1)} %broadcast_in_dim.3), channel_id=1, replica_groups=mesh['z'=8,'y'=4,'c'=2,'x'=4] {'z','y','x'}, dimensions={0} | all-to-all | bytes 393216 | tf_op jit(solution)/shard_map/all_to_all | solution.py:460
  66.4 0.2 reduce_sum.11
  66.6 2.5 %collective-permute-start.11 = (f32[1,384]{1,0:T(1,128)S(1)}, f32[1,384]{1,0:T(1,128)S(1)}, u32[]{:S(2)}, u32[]{:S(2)}) collective-permute-start(f32[1,384]{1,0:T(1,128)S(1)} %reduce_sum.12.mine_ref), channel_id=1, source_target_pairs={{0,4},{4,0},{1,5},{5,1},{2,6},{6,2},{3,7},{7,3},{8,12},{12,8},{9,1... | collective-permute-start | bytes 4616 | tf_op jit(solution)/shard_map/ppermute | solution.py:464
  69.1 0.8 %collective-permute-done.11.other_ref = f32[1,384]{1,0:T(1,128)S(1)} collective-permute-done((f32[1,384]{1,0:T(1,128)S(1)}, f32[1,384]{1,0:T(1,128)S(1)}, u32[]{:S(2)}, u32[]{:S(2)}) %collective-permute-start.11) | collective-permute-done | bytes 1568 | tf_op jit(solution)/shard_map/ppermute | solution.py:464
  69.9 1.8 %shard_map.84 = (f32[8,320,128]{2,1,0:T(8,128)}, f32[3,2,128]{2,1,0:T(2,128)}) custom-call(f32[1,384]{1,0:T(1,128)S(1)} %reduce_sum.12.mine_ref, f32[1,384]{1,0:T(1,128)S(1)} %collective-permute-done.11.other_ref, bf16[8,320,128]{2,1,0:T(8,128)(2,1)S(1)} %get-tuple-element.42.rhs_ref, f32[8,320,128]{2,1,0:T(8,128)S(1)} %get-tuple-element.43.w1_ref, ...), custom_call_target="tpu_custom_call" | custom-call | flops 10000000 | bytes 6000000 | tf_op jit(solution)/shard_map/pallas_call | solution.py:461
  (13 shorter events, 0.3 us)
Async XLA Ops:
  5.3 12.7 %collective-permute-start = (bf16[8,320,128]{2,1,0:T(8,128)(2,1)S(1)}, bf16[8,320,128]{2,1,0:T(8,128)(2,1)S(1)}, u32[]{:S(2)}, u32[]{:S(2)}) collective-permute-start(bf16[8,320,128]{2,1,0:T(8,128)(2,1)S(1)} %get-tuple-element.33), channel_id=1, source_target_pairs={{4,8},{8,4},{12,16},{16,12},{20,24},{24,20},{28,32},{32,28},{36,40... | collective-permute-start | bytes 1966088 | tf_op jit(solution)/shard_map/ppermute | solution.py:417
  9.8 7.9 %collective-permute-start.3 = (bf16[4,80,128]{2,1,0:T(8,128)(2,1)S(1)}, bf16[4,80,128]{2,1,0:T(8,128)(2,1)S(1)}, u32[]{:S(2)}, u32[]{:S(2)}) collective-permute-start(bf16[4,80,128]{2,1,0:T(8,128)(2,1)S(1)} %get-tuple-element.36), channel_id=1, source_target_pairs={{0,1},{1,0},{2,3},{3,2},{4,5},{5,4},{6,7},{7,6},{8,9},{9,8},{10,11... | collective-permute-start | bytes 245768 | tf_op jit(solution)/shard_map/ppermute | solution.py:418
  11.5 6.2 %collective-permute-start.4 = (bf16[4,80,128]{2,1,0:T(8,128)(2,1)S(1)}, bf16[4,80,128]{2,1,0:T(8,128)(2,1)S(1)}, u32[]{:S(2)}, u32[]{:S(2)}) collective-permute-start(bf16[4,80,128]{2,1,0:T(8,128)(2,1)S(1)} %get-tuple-element.37), channel_id=1, source_target_pairs={{1,2},{2,1},{5,6},{6,5},{9,10},{10,9},{13,14},{14,13},{17,18},{18,... | collective-permute-start | bytes 245768 | tf_op jit(solution)/shard_map/ppermute | solution.py:419
  15.4 2.2 %collective-permute-start.1 = (bf16[4,320,128]{2,1,0:T(8,128)(2,1)S(1)}, bf16[4,320,128]{2,1,0:T(8,128)(2,1)S(1)}, u32[]{:S(2)}, u32[]{:S(2)}) collective-permute-start(bf16[4,320,128]{2,1,0:T(8,128)(2,1)S(1)} %get-tuple-element.34), channel_id=1, source_target_pairs={{0,4},{4,0},{1,5},{5,1},{2,6},{6,2},{3,7},{7,3},{8,12},{12,8},{9,1... | collective-permute-start | bytes 983048 | tf_op jit(solution)/shard_map/ppermute | solution.py:421
  15.5 2.2 %collective-permute-start.2 = (bf16[4,320,128]{2,1,0:T(8,128)(2,1)S(1)}, bf16[4,320,128]{2,1,0:T(8,128)(2,1)S(1)}, u32[]{:S(2)}, u32[]{:S(2)}) collective-permute-start(bf16[4,320,128]{2,1,0:T(8,128)(2,1)S(1)} %get-tuple-element.35), channel_id=1, source_target_pairs={{0,4},{4,0},{1,5},{5,1},{2,6},{6,2},{3,7},{7,3},{8,12},{12,8},{9,1... | collective-permute-start | bytes 983048 | tf_op jit(solution)/shard_map/ppermute | solution.py:421
  19.7 11.9 %collective-permute-start.5 = (bf16[8,320,128]{2,1,0:T(8,128)(2,1)S(1)}, bf16[8,320,128]{2,1,0:T(8,128)(2,1)S(1)}, u32[]{:S(2)}, u32[]{:S(2)}) collective-permute-start(bf16[8,320,128]{2,1,0:T(8,128)(2,1)S(1)} %get-tuple-element.45), channel_id=1, source_target_pairs={{4,8},{8,4},{12,16},{16,12},{20,24},{24,20},{28,32},{32,28},{36,40... | collective-permute-start | bytes 1966088 | tf_op jit(solution)/shard_map/ppermute | solution.py:417
  23.3 7.2 %collective-permute-start.8 = (bf16[4,80,128]{2,1,0:T(8,128)(2,1)S(1)}, bf16[4,80,128]{2,1,0:T(8,128)(2,1)S(1)}, u32[]{:S(2)}, u32[]{:S(2)}) collective-permute-start(bf16[4,80,128]{2,1,0:T(8,128)(2,1)S(1)} %get-tuple-element.50), channel_id=1, source_target_pairs={{0,1},{1,0},{2,3},{3,2},{4,5},{5,4},{6,7},{7,6},{8,9},{9,8},{10,11... | collective-permute-start | bytes 245768 | tf_op jit(solution)/shard_map/ppermute | solution.py:418
  25.8 4.7 %collective-permute-start.9 = (bf16[4,80,128]{2,1,0:T(8,128)(2,1)S(1)}, bf16[4,80,128]{2,1,0:T(8,128)(2,1)S(1)}, u32[]{:S(2)}, u32[]{:S(2)}) collective-permute-start(bf16[4,80,128]{2,1,0:T(8,128)(2,1)S(1)} %get-tuple-element.51), channel_id=1, source_target_pairs={{1,2},{2,1},{5,6},{6,5},{9,10},{10,9},{13,14},{14,13},{17,18},{18,... | collective-permute-start | bytes 245768 | tf_op jit(solution)/shard_map/ppermute | solution.py:419
  27.8 2.7 %collective-permute-start.6 = (bf16[4,320,128]{2,1,0:T(8,128)(2,1)S(1)}, bf16[4,320,128]{2,1,0:T(8,128)(2,1)S(1)}, u32[]{:S(2)}, u32[]{:S(2)}) collective-permute-start(bf16[4,320,128]{2,1,0:T(8,128)(2,1)S(1)} %get-tuple-element.48), channel_id=1, source_target_pairs={{0,4},{4,0},{1,5},{5,1},{2,6},{6,2},{3,7},{7,3},{8,12},{12,8},{9,1... | collective-permute-start | bytes 983048 | tf_op jit(solution)/shard_map/ppermute | solution.py:421
  27.9 2.6 %collective-permute-start.7 = (bf16[4,320,128]{2,1,0:T(8,128)(2,1)S(1)}, bf16[4,320,128]{2,1,0:T(8,128)(2,1)S(1)}, u32[]{:S(2)}, u32[]{:S(2)}) collective-permute-start(bf16[4,320,128]{2,1,0:T(8,128)(2,1)S(1)} %get-tuple-element.49), channel_id=1, source_target_pairs={{0,4},{4,0},{1,5},{5,1},{2,6},{6,2},{3,7},{7,3},{8,12},{12,8},{9,1... | collective-permute-start | bytes 983048 | tf_op jit(solution)/shard_map/ppermute | solution.py:421
  32.3 1.2 %collective-permute-start.10 = (f32[1,384]{1,0:T(1,128)S(1)}, f32[1,384]{1,0:T(1,128)S(1)}, u32[]{:S(2)}, u32[]{:S(2)}) collective-permute-start(f32[1,384]{1,0:T(1,128)S(1)} %get-tuple-element.54), channel_id=1, source_target_pairs={{0,4},{4,0},{1,5},{5,1},{2,6},{6,2},{3,7},{7,3},{8,12},{12,8},{9,1... | collective-permute-start | bytes 4616 | tf_op jit(solution)/shard_map/ppermute | solution.py:458
  66.6 3.3 %collective-permute-start.11 = (f32[1,384]{1,0:T(1,128)S(1)}, f32[1,384]{1,0:T(1,128)S(1)}, u32[]{:S(2)}, u32[]{:S(2)}) collective-permute-start(f32[1,384]{1,0:T(1,128)S(1)} %reduce_sum.12.mine_ref), channel_id=1, source_target_pairs={{0,4},{4,0},{1,5},{5,1},{2,6},{6,2},{3,7},{7,3},{8,12},{12,8},{9,1... | collective-permute-start | bytes 4616 | tf_op jit(solution)/shard_map/ppermute | solution.py:464

commit v5 on v4

--- a/solution.py
+++ b/solution.py
@@ -19,6 +19,7 @@
 GROUP = 8
 SIDE_FLOPS = 100 * 10**6
 OWN_FLOPS = 4000 * 10**6
+NEAR_FLOPS = 10**6
 VMEM_LIMIT = 40 * 1024 * 1024
 
 TN = (((0,), (0,)), ((), ()))
@@ -172,7 +173,7 @@
 
 def first_kernel(
     list_hbm, count_ref, rhs_hbm, inv_hbm, face_hbm, hang_hbm,
-    rhs_ref, inv_ref, face_ref, hang_ref, tr_ref, cross_ref, ya_ref, yb_ref,
+    rhs_ref, inv_ref, face_ref, hang_ref, tr_ref, cross_ref,
     acc, app_ref, list_ref, slot_ref, sems, hang_sems,
 ):
     core, _ = core_and_row()
@@ -189,8 +190,6 @@
         bring(inv_hbm.at[pair], inv_ref.at[pair])
     late = len(copies)
     bring(face_hbm.at[core, :, :, core], face_ref.at[0])
-    bring(face_hbm.at[:, 1, :, 3], face_ref.at[1])
-    bring(face_hbm.at[:, 0, :, 2], face_ref.at[2])
     copies[0].wait()
     n = list_slots(1, 2 * core - 1, list_ref, count_ref, slot_ref)
     each_slot(n, slot_ref, hang_hbm, hang_ref, hang_sems, lambda copy: copy.start())
@@ -204,42 +203,47 @@
     fill_traces(lowered, inv_ref, tr_ref, app_ref)
     for copy in copies[late:]:
         copy.wait()
-    edge_fluxes(face_ref, tr_ref, ya_ref, yb_ref)
     each_slot(n, slot_ref, hang_hbm, hang_ref, hang_sems, lambda copy: copy.wait())
     cross_part(acc, (cross_ref,), lambda: n, core, list_ref, face_ref, hang_ref, tr_ref, slot_ref)
 
 
 def side_first_kernel(
-    list_ref, count_ref, face_hbm, hang_hbm, tr_ref, chip_ref, chip2_ref, face_ref, hang_ref, own_face_ref, own_hang_ref,
-    acc, slot_ref, own_slot_ref, sems, hang_sems, own_hang_sems,
+    list_hbm, count_ref, face_hbm, hang_hbm, tr_ref, chip_ref, chip2_ref, ya_ref, yb_ref, face_ref, hang_ref, own_face_ref, own_hang_ref,
+    acc, slot_ref, list_ref, list_sem, own_slot_ref, sems, hang_sems, own_hang_sems,
 ):
     core, _ = core_and_row()
+    listing = fetch_list(-1, 2 * core - 1, list_hbm, list_ref, count_ref, slot_ref, list_sem)
     pieces = [
         face_hbm.at[1, :, :, 0], face_hbm.at[0, :, :, 1], face_hbm.at[:, 1, :, 2],
         face_hbm.at[:, 0, :, 3], face_hbm.at[:, :, 1, 4], face_hbm.at[:, :, 0, 5],
     ]
-    copies = [pltpu.make_async_copy(face_hbm.at[1 - core, :, :, 1 - core], face_ref.at[0], sems.at[6])]
+    mine = [face_hbm.at[1 - core, :, :, 1 - core], face_hbm.at[:, 1, :, 3], face_hbm.at[:, 0, :, 2]]
+    copies = [pltpu.make_async_copy(p, face_ref.at[f], sems.at[6 + f]) for f, p in enumerate(mine)]
     copies += [pltpu.make_async_copy(p, own_face_ref.at[f], sems.at[f]) for f, p in enumerate(pieces)]
-    copies[0].start()
-    n = list_slots(-1, 2 * core - 1, list_ref, count_ref, slot_ref)
+    for copy in copies[:3]:
+        copy.start()
+    n = listing()
     each_slot(n, slot_ref, hang_hbm, hang_ref, hang_sems, lambda copy: copy.start())
-    for copy in copies[1:]:
+    for copy in copies[3:]:
         copy.start()
     own_n = list_slots(0, 1, list_ref, count_ref, own_slot_ref)
     each_slot(own_n, own_slot_ref, hang_hbm, own_hang_ref, own_hang_sems, lambda copy: copy.start())
-    copies[0].wait()
+    for copy in copies[:3]:
+        copy.wait()
+    edge_fluxes(face_ref, tr_ref, ya_ref, yb_ref)
     each_slot(n, slot_ref, hang_hbm, hang_ref, hang_sems, lambda copy: copy.wait())
     cross_part(acc, (chip_ref, chip2_ref), lambda: n, 1 - core, list_ref, face_ref, hang_ref, tr_ref, slot_ref)
-    for copy in copies[1:]:
+    for copy in copies[3:]:
         copy.wait()
     each_slot(own_n, own_slot_ref, hang_hbm, own_hang_ref, own_hang_sems, lambda copy: copy.wait())
 
 
 def side_second_kernel(
-    list_hbm, count_ref, face_ref, hang_ref, tr_ref, chip_ref, chip2_ref, acc, slot_ref, list_ref, sem
+    list_hbm, count_ref, face_ref, hang_ref, tr_ref, chip_ref, chip2_ref, ya_ref, yb_ref, acc, slot_ref, list_ref, sem
 ):
     core, _ = core_and_row()
     listing = fetch_list(-1, 2 * core - 1, list_hbm, list_ref, count_ref, slot_ref, sem)
+    edge_fluxes(face_ref, tr_ref, ya_ref, yb_ref)
     cross_part(acc, (chip_ref, chip2_ref), listing, 1 - core, list_ref, face_ref, hang_ref, tr_ref, slot_ref)
 
 
@@ -280,35 +284,39 @@
     gram_ref[...] = gram_rows((rhs_ref, rhs_ref), (rhs_ref, w1_ref), (w1_ref, w1_ref))
 
 
-def landed(e, own_ref, cross_ref, chip_refs, ya_ref, yb_ref):
+def near_kernel(own_ref, chip_ref, chip2_ref, ya_ref, yb_ref, near_ref):
     _, odd = core_and_row()
-    y = (e >> 1) & 1
-    n = 2 * (e >> 2) + (e & 1)
-    edge = swap_if(odd == 1, ya_ref[n].astype(jnp.float32), yb_ref[n].astype(jnp.float32))[1 - y]
-    came = cross_ref[e].astype(jnp.float32) + chip_refs[e // 4][e % 4].astype(jnp.float32)
-    return own_ref[e] + came + spread_b(edge, y)
+    for e in range(ELEMS):
+        y = (e >> 1) & 1
+        n = 2 * (e >> 2) + (e & 1)
+        edge = swap_if(odd == 1, ya_ref[n].astype(jnp.float32), yb_ref[n].astype(jnp.float32))[1 - y]
+        chip = (chip_ref, chip2_ref)[e // 4][e % 4].astype(jnp.float32)
+        near_ref[e] = own_ref[e] + chip + spread_b(edge, y)
+
+
+def landed(e, near_ref, cross_ref):
+    return near_ref[e] + cross_ref[e].astype(jnp.float32)
 
 
 def second_kernel(
-    list_hbm, count_ref, own_ref, in_cross, in_chip, in_chip2, in_ya, in_yb, inv_ref, face_ref, hang_ref,
-    w_ref, tr_ref, cross_ref, ya_ref, yb_ref, acc, app_ref, slot_ref, list_ref, sem,
+    list_hbm, count_ref, near_ref, in_cross, inv_ref, face_ref, hang_ref,
+    w_ref, tr_ref, cross_ref, acc, app_ref, slot_ref, list_ref, sem,
 ):
     core, _ = core_and_row()
     listing = fetch_list(1, 2 * core - 1, list_hbm, list_ref, count_ref, slot_ref, sem)
 
     def lowered(e):
-        w = landed(e, own_ref, in_cross, (in_chip, in_chip2), in_ya, in_yb)
+        w = landed(e, near_ref, in_cross)
         w_ref[e] = w
         return w.astype(jnp.bfloat16)
 
     fill_traces(lowered, inv_ref, tr_ref, app_ref)
-    edge_fluxes(face_ref, tr_ref, ya_ref, yb_ref)
     cross_part(acc, (cross_ref,), listing, core, list_ref, face_ref, hang_ref, tr_ref, slot_ref)
 
 
-def last_kernel(own_ref, in_cross, in_chip, in_chip2, in_ya, in_yb, rhs_ref, w1_ref, early_ref, w_ref, keep_ref, give_ref):
+def last_kernel(near_ref, in_cross, rhs_ref, w1_ref, early_ref, w_ref, keep_ref, give_ref):
     for e in range(ELEMS):
-        w_ref[e] = landed(e, own_ref, in_cross, (in_chip, in_chip2), in_ya, in_yb)
+        w_ref[e] = landed(e, near_ref, in_cross)
     late = gram_rows((rhs_ref, w_ref), (w1_ref, w_ref), (w_ref, w_ref))
     early = early_ref[...]
     core, _ = core_and_row()
@@ -392,7 +400,6 @@
     slots = pltpu.SMEM((HANG + 8,), jnp.int32)
     bf16 = jnp.bfloat16
     million = 10**6
-    scalars = [SMEM, SMEM]
     later = [HBM, SMEM]
     lists = [slots, pltpu.SMEM((4, HANG), jnp.int32), pltpu.SemaphoreType.DMA]
     sems = lambda n: pltpu.SemaphoreType.DMA((n,))
@@ -400,32 +407,32 @@
     hangs = stay(hang_block.reshape(HANG, FACE, BLOCK))
     packed = shape((HANG, FACE, BLOCK), bf16)
     held = lambda n: shape((n, 2, 2, FACE, FACE), bf16)
-    halves = [shape(HALF, bf16)] * 2
-    sent = [shape(TRACES, bf16), shape(FIELD, bf16), shape(SIDE, bf16), shape(SIDE, bf16)]
-
-    rhs, inv, face, hang, traces, *out = call(
-        first_kernel, [HBM, SMEM] + [HBM] * 4, [shape(FIELD, bf16), shape((ELEMS, BLOCK, BLOCK), bf16), held(3), packed] + sent,
+    sent = [shape(TRACES, bf16), shape(FIELD, bf16)]
+    beside = [shape(HALF, bf16)] * 2 + [shape(SIDE, bf16)] * 2
+
+    rhs, inv, face, hang, traces, cross = call(
+        first_kernel, [HBM, SMEM] + [HBM] * 4, [shape(FIELD, bf16), shape((ELEMS, BLOCK, BLOCK), bf16), held(1), packed] + sent,
         [
             acc, field, pltpu.SMEM((4, HANG), jnp.int32), slots,
-            sems(ELEMS + 4), sems(HANG),
+            sems(ELEMS + 2), sems(HANG),
         ],
         300 * million, 6 * million,
     )(rows, count, stay(rhs_field.reshape(FIELD)), stay(inv_block.reshape(ELEMS, BLOCK, BLOCK)), faces, hangs)
 
-    def exchange(out, side_call, own_call):
-        cross, ya, yb = out
+    def exchange(cross, side_call, own_call):
         in_cross = lax.ppermute(cross, ("z", "y", "c"), pairs["cross"])
+        low, high, ya, yb, *weights = side_call()
         in_ya = lax.ppermute(ya, "x", pairs["even"])
         in_yb = lax.ppermute(yb, "x", pairs["odd"])
-        low, high, *weights = side_call()
         in_chip = [lax.ppermute(part, "c", [(0, 1), (1, 0)]) for part in (low, high)]
         own, *rest = own_call(weights[2:])
-        return (own, in_cross, *in_chip, in_ya, in_yb), weights, rest
+        near = call(near_kernel, [VMEM] * 5, [shape(FIELD)], [], NEAR_FLOPS, 6 * million)(own, *in_chip, in_ya, in_yb)[0]
+        return (near, in_cross), weights, rest
 
     def side_first():
         return call(
-            side_first_kernel, scalars + [HBM, HBM, VMEM], halves + [held(1), packed, held(6), packed],
-            [acc, slots, slots, sems(7), sems(HANG), sems(HANG)], SIDE_FLOPS, 4 * million,
+            side_first_kernel, later + [HBM, HBM, VMEM], beside + [held(3), packed, held(6), packed],
+            [acc, *lists, slots, sems(9), sems(HANG), sems(HANG)], SIDE_FLOPS, 4 * million,
         )(rows, count, faces, hangs, traces)
 
     def own_first(weights):
@@ -433,13 +440,13 @@
             rows, count, *weights, traces
         )
 
-    arrived, weights, _ = exchange(out, side_first, own_first)
-    w1, traces, *out = call(
-        second_kernel, later + [VMEM] * 9, [shape(FIELD)] + sent, [acc, field, *lists], 300 * million, 8 * million,
+    arrived, weights, _ = exchange(cross, side_first, own_first)
+    w1, traces, cross = call(
+        second_kernel, later + [VMEM] * 5, [shape(FIELD)] + sent, [acc, field, *lists], 300 * million, 8 * million,
     )(rows, count, *arrived, inv, face, hang)
 
     def side_second():
-        return call(side_second_kernel, later + [VMEM] * 3, halves, [acc, *lists], SIDE_FLOPS, 4 * million)(
+        return call(side_second_kernel, later + [VMEM] * 3, beside, [acc, *lists], SIDE_FLOPS, 4 * million)(
             rows, count, *weights[:2], traces
         )
 
@@ -449,9 +456,9 @@
             OWN_FLOPS, 6 * million,
         )(rows, count, *weights[2:], traces, rhs, w1)
 
-    arrived, _, (early,) = exchange(out, side_second, own_second)
+    arrived, _, (early,) = exchange(cross, side_second, own_second)
     w2, keep, give = call(
-        last_kernel, [VMEM] * 9, [shape(FIELD), shape((1, 3 * RHS)), shape((1, 3 * RHS))], [], 10 * million, 8 * million
+        last_kernel, [VMEM] * 5, [shape(FIELD), shape((1, 3 * RHS)), shape((1, 3 * RHS))], [], 10 * million, 8 * million
     )(*arrived, rhs, w1, early)
 
     swap = [(0, 1), (1, 0)]

time: 72.1 us -> 71.6 us (level)
  starting transfers between devices: 17.3 us -> 16.4 us
  blocking collectives: 32.8 us -> 31.9 us
  waiting for transfers between devices: 3.39 us -> 4.28 us
    pallas_call x4 -> x6, Pallas kernels: 6.9 us -> 7.81 us  [the longest x1 3.28 us: side_first(): call(side_first_kernel, later + [HBM, HBM, VMEM], beside + [held(3), pack...]
    all_to_all x1, blocking collectives: 32.8 us -> 31.9 us  [per_device(): lax.all_to_all(jnp.broadcast_to(part, (chips, 1, 3 * RHS)), ('z', 'y', 'x...]
  transfers between devices with their start and end apart: 12 -> 12, of which waited for: 4 -> 5; matrix products, arithmetic and copies ran while one was open for 0% -> 0% of each run, Pallas kernels for 12% -> 11%
where the time goes in v5:
time: 71.6 us; the launch traced here: 71.3 us
  blocking collectives  31.9 us (45%)
  Pallas kernels  16.8 us (23%)
  starting transfers between devices  16.4 us (23%)
  waiting for transfers between devices  4.28 us (6%)
  between operations  1.61 us (2%)
    all_to_all x1, blocking collectives, per_device(): lax.all_to_all(jnp.broadcast_to(part, (chips, 1, 3 * RHS)), ('z', 'y', 'x...  31.9 us
    ppermute x2, starting transfers between devices, exchange(): in_cross = lax.ppermute(cross, ('z', 'y', 'c'), pairs['cross'])  7.63 us
    pallas_call x1, Pallas kernels, per_device(): call(first_kernel, [HBM, SMEM] + [HBM] * 4, [shape(FIELD, bf16), shape((E...  4.02 us
    ppermute x2, starting transfers between devices, exchange(): in_ya = lax.ppermute(ya, 'x', pairs['even'])  3.75 us
    pallas_call x1, Pallas kernels, side_first(): call(side_first_kernel, later + [HBM, HBM, VMEM], beside + [held(3), pack...  3.28 us
    ppermute x1, starting transfers between devices, per_device(): lax.ppermute(mine, 'c', swap)  2.47 us
    pallas_call x1, Pallas kernels, per_device(): call(second_kernel, later + [VMEM] * 5, [shape(FIELD)] + sent, [acc, fiel...  2.42 us
    ppermute x2, waiting for transfers between devices, exchange(): in_cross = lax.ppermute(cross, ('z', 'y', 'c'), pairs['cross'])  2.08 us
  transfers between devices with their start and end apart: 12, of which 5 were waited for; matrix products, arithmetic and copies ran while one was open for 0% of the time, Pallas kernels for 11%

profile of v5, /device:TPU:1, one launch (start us, length us, event | category | flops | bytes accessed | tf_op | source)
XLA Modules:
  0.0 71.3 jit_solution(4186149462016719255)
XLA Ops:
  1.3 4.0 %shard_map.77 = (bf16[8,320,128]{2,1,0:T(8,128)(2,1)S(1)}, bf16[8,320,320]{2,1,0:T(8,128)(2,1)S(1)}, bf16[1,2,2,80,80]{4,3,2,1,0:T(8,128)(2,1)S(1)}, bf16[32,80,...) custom-call(s32[4,32]{1,0:T(4,128)} %bitcast.11, ...), custom_call_target="tpu_custom_call" | custom-call | flops 300000000 | bytes 6000000 | tf_op jit(solution)/shard_map/pallas_call | solution.py:413
  5.3 4.3 %collective-permute-start.4 = (bf16[8,320,128]{2,1,0:T(8,128)(2,1)S(1)}, bf16[8,320,128]{2,1,0:T(8,128)(2,1)S(1)}, u32[]{:S(2)}, u32[]{:S(2)}) collective-permute-start(bf16[8,320,128]{2,1,0:T(8,128)(2,1)S(1)} %get-tuple-element.37), channel_id=1, source_target_pairs={{4,8},{8,4},{12,16},{16,12},{20,24},{24,20},{28,32},{32,28},{36,40... | collective-permute-start | bytes 1966088 | tf_op jit(solution)/shard_map/ppermute | solution.py:423
  9.6 3.3 %shard_map.78 = (bf16[4,320,128]{2,1,0:T(8,128)(2,1)S(1)}, bf16[4,320,128]{2,1,0:T(8,128)(2,1)S(1)}, bf16[4,80,128]{2,1,0:T(8,128)(2,1)S(1)}, bf16[4,80,128]{2,1...) custom-call(s32[4,32]{1,0:T(4,128)} %bitcast.12, ...), custom_call_target="tpu_custom_call" | custom-call | flops 100000000 | bytes 4000000 | tf_op jit(solution)/shard_map/pallas_call | solution.py:433
  12.9 1.2 %collective-permute-start.2 = (bf16[4,80,128]{2,1,0:T(8,128)(2,1)S(1)}, bf16[4,80,128]{2,1,0:T(8,128)(2,1)S(1)}, u32[]{:S(2)}, u32[]{:S(2)}) collective-permute-start(bf16[4,80,128]{2,1,0:T(8,128)(2,1)S(1)} %get-tuple-element.35), channel_id=1, source_target_pairs={{0,1},{1,0},{2,3},{3,2},{4,5},{5,4},{6,7},{7,6},{8,9},{9,8},{10,11... | collective-permute-start | bytes 245768 | tf_op jit(solution)/shard_map/ppermute | solution.py:425
  14.1 0.7 collective-permute-start.3
  14.8 0.5 collective-permute-start.1
  15.3 1.3 %shard_map.79.own_ref = f32[8,320,128]{2,1,0:T(8,128)S(1)} custom-call(s32[4,32]{1,0:T(4,128)} %bitcast.13, s32[1,1]{1,0:T(1,128)S(6)} %copy.10.count_ref, bf16[6,2,2,80,80]{4,3,2,1,0:T(8,128)(2,1)S(1)} %get-tuple-element.31.face_ref, bf16[32,80,320]{2,1,0:T(8,128)(2,1)S(1)} %get-tuple-element.32.hang_ref, bf16[48,80,128]{2,1,0:T(8,128)(2,1)S(1)} %get-tuple-element.30.tr_ref), custom_call_target="tpu_custom_call" | custom-call | flops 4000000000 | bytes 6000000 | tf_op jit(solution)/shard_map/pallas_call | solution.py:439
  16.7 0.2 collective-permute-done.1.chip2_ref
  17.1 0.7 %collective-permute-done.4.in_cross = bf16[8,320,128]{2,1,0:T(8,128)(2,1)S(1)} collective-permute-done((bf16[8,320,128]{2,1,0:T(8,128)(2,1)S(1)}, bf16[8,320,128]{2,1,0:T(8,128)(2,1)S(1)}, u32[]{:S(2)}, u32[]{:S(2)}) %collective-permute-start.4) | collective-permute-done | bytes 655392 | tf_op jit(solution)/shard_map/ppermute | solution.py:423
  17.8 2.4 %shard_map.81 = (f32[8,320,128]{2,1,0:T(8,128)S(1)}, bf16[48,80,128]{2,1,0:T(8,128)(2,1)S(1)}, bf16[8,320,128]{2,1,0:T(8,128)(2,1)S(1)}) custom-call(s32[4,32]{1,0:T(4,128)} %bitcast.14, s32[1,1]{1,0:T(1,128)S(6)} %copy.10.count_ref, f32[8,320,128]{2,1,0:T(8,128)S(1)} %shard_map.80.near_ref, bf16[8,320,128]{2,1,0:T(8,128)(2,1)S(1)} %collective-permute-done.4.in_cross, ...), custom_call_target="tpu_custom_call" | custom-call | flops 300000000 | bytes 8000000 | tf_op jit(solution)/shard_map/pallas_call | solution.py:444
  20.3 3.4 %collective-permute-start.9 = (bf16[8,320,128]{2,1,0:T(8,128)(2,1)S(1)}, bf16[8,320,128]{2,1,0:T(8,128)(2,1)S(1)}, u32[]{:S(2)}, u32[]{:S(2)}) collective-permute-start(bf16[8,320,128]{2,1,0:T(8,128)(2,1)S(1)} %get-tuple-element.51), channel_id=1, source_target_pairs={{4,8},{8,4},{12,16},{16,12},{20,24},{24,20},{28,32},{32,28},{36,40... | collective-permute-start | bytes 1966088 | tf_op jit(solution)/shard_map/ppermute | solution.py:423
  23.6 1.3 %shard_map.83 = (bf16[4,320,128]{2,1,0:T(8,128)(2,1)S(1)}, bf16[4,320,128]{2,1,0:T(8,128)(2,1)S(1)}, bf16[4,80,128]{2,1,0:T(8,128)(2,1)S(1)}, bf16[4,80,128]{2,1,0:T(8,128)(2,1)S(1)}) custom-call(s32[4,32]{1,0:T(4,128)} %bitcast.15, s32[1,1]{1,0:T(1,128)S(6)} %copy.10.count_ref, bf16[3,2,2,80,80]{4,3,2,1,0:T(8,128)(2,1)S(1)} %get-tuple-element.45.face_ref, ...), custom_call_target="tpu_custom_call" | custom-call | flops 100000000 | bytes 4000000 | tf_op jit(solution)/shard_map/pallas_call | solution.py:449
  25.0 2.6 %collective-permute-start.7 = (bf16[4,80,128]{2,1,0:T(8,128)(2,1)S(1)}, bf16[4,80,128]{2,1,0:T(8,128)(2,1)S(1)}, u32[]{:S(2)}, u32[]{:S(2)}) collective-permute-start(bf16[4,80,128]{2,1,0:T(8,128)(2,1)S(1)} %get-tuple-element.49), channel_id=1, source_target_pairs={{0,1},{1,0},{2,3},{3,2},{4,5},{5,4},{6,7},{7,6},{8,9},{9,8},{10,11... | collective-permute-start | bytes 245768 | tf_op jit(solution)/shard_map/ppermute | solution.py:425
  27.5 0.7 collective-permute-start.8
  28.3 0.5 collective-permute-start.6
  28.8 1.8 %shard_map.82 = (f32[8,320,128]{2,1,0:T(8,128)S(1)}, f32[1,384]{1,0:T(1,128)S(1)}) custom-call(s32[4,32]{1,0:T(4,128)} %bitcast.16, s32[1,1]{1,0:T(1,128)S(6)} %copy.10.count_ref, bf16[6,2,2,80,80]{4,3,2,1,0:T(8,128)(2,1)S(1)} %get-tuple-element.31.face_ref, bf16[32,80,320]{2,1,0:T(8,128)(2,1)S(1)} %get-tuple-element.32.hang_ref, ...), custom_call_target="tpu_custom_call" | custom-call | flops 4000000000 | bytes 6000000 | tf_op jit(solution)/shard_map/pallas_call | solution.py:454
  30.7 0.2 shard_map.84.near_ref
  30.9 1.3 %collective-permute-done.9.in_cross = bf16[8,320,128]{2,1,0:T(8,128)(2,1)S(1)} collective-permute-done((bf16[8,320,128]{2,1,0:T(8,128)(2,1)S(1)}, bf16[8,320,128]{2,1,0:T(8,128)(2,1)S(1)}, u32[]{:S(2)}, u32[]{:S(2)}) %collective-permute-start.9) | collective-permute-done | bytes 655392 | tf_op jit(solution)/shard_map/ppermute | solution.py:423
  32.2 0.4 shard_map.85
  32.7 1.1 %collective-permute-done.10 = f32[1,384]{1,0:T(1,128)S(1)} collective-permute-done((f32[1,384]{1,0:T(1,128)S(1)}, f32[1,384]{1,0:T(1,128)S(1)}, u32[]{:S(2)}, u32[]{:S(2)}) %collective-permute-start.10) | collective-permute-done | bytes 1568 | tf_op jit(solution)/shard_map/ppermute | solution.py:465
  34.0 31.9 %all_to_all.5 = f32[128,1,384]{2,1,0:T(1,128)S(1)} all-to-all(f32[128,1,384]{2,1,0:T(1,128)S(1)} %broadcast_in_dim.3), channel_id=1, replica_groups=mesh['z'=8,'y'=4,'c'=2,'x'=4] {'z','y','x'}, dimensions={0} | all-to-all | bytes 393216 | tf_op jit(solution)/shard_map/all_to_all | solution.py:467
  66.0 2.5 %collective-permute-start.11 = (f32[1,384]{1,0:T(1,128)S(1)}, f32[1,384]{1,0:T(1,128)S(1)}, u32[]{:S(2)}, u32[]{:S(2)}) collective-permute-start(f32[1,384]{1,0:T(1,128)S(1)} %reduce_sum.12.mine_ref), channel_id=1, source_target_pairs={{0,4},{4,0},{1,5},{5,1},{2,6},{6,2},{3,7},{7,3},{8,12},{12,8},{9,1... | collective-permute-start | bytes 4616 | tf_op jit(solution)/shard_map/ppermute | solution.py:471
  68.5 0.8 %collective-permute-done.11.other_ref = f32[1,384]{1,0:T(1,128)S(1)} collective-permute-done((f32[1,384]{1,0:T(1,128)S(1)}, f32[1,384]{1,0:T(1,128)S(1)}, u32[]{:S(2)}, u32[]{:S(2)}) %collective-permute-start.11) | collective-permute-done | bytes 1568 | tf_op jit(solution)/shard_map/ppermute | solution.py:471
  69.3 1.8 %shard_map.86 = (f32[8,320,128]{2,1,0:T(8,128)}, f32[3,2,128]{2,1,0:T(2,128)}) custom-call(f32[1,384]{1,0:T(1,128)S(1)} %reduce_sum.12.mine_ref, f32[1,384]{1,0:T(1,128)S(1)} %collective-permute-done.11.other_ref, bf16[8,320,128]{2,1,0:T(8,128)(2,1)S(1)} %get-tuple-element.42.rhs_ref, f32[8,320,128]{2,1,0:T(8,128)S(1)} %get-tuple-element.43.w1_ref, ...), custom_call_target="tpu_custom_call" | custom-call | flops 10000000 | bytes 6000000 | tf_op jit(solution)/shard_map/pallas_call | solution.py:468
  (15 shorter events, 0.8 us)
Async XLA Ops:
  5.3 12.5 %collective-permute-start.4 = (bf16[8,320,128]{2,1,0:T(8,128)(2,1)S(1)}, bf16[8,320,128]{2,1,0:T(8,128)(2,1)S(1)}, u32[]{:S(2)}, u32[]{:S(2)}) collective-permute-start(bf16[8,320,128]{2,1,0:T(8,128)(2,1)S(1)} %get-tuple-element.37), channel_id=1, source_target_pairs={{4,8},{8,4},{12,16},{16,12},{20,24},{24,20},{28,32},{32,28},{36,40... | collective-permute-start | bytes 1966088 | tf_op jit(solution)/shard_map/ppermute | solution.py:423
  12.9 3.8 %collective-permute-start.2 = (bf16[4,80,128]{2,1,0:T(8,128)(2,1)S(1)}, bf16[4,80,128]{2,1,0:T(8,128)(2,1)S(1)}, u32[]{:S(2)}, u32[]{:S(2)}) collective-permute-start(bf16[4,80,128]{2,1,0:T(8,128)(2,1)S(1)} %get-tuple-element.35), channel_id=1, source_target_pairs={{0,1},{1,0},{2,3},{3,2},{4,5},{5,4},{6,7},{7,6},{8,9},{9,8},{10,11... | collective-permute-start | bytes 245768 | tf_op jit(solution)/shard_map/ppermute | solution.py:425
  14.1 2.6 %collective-permute-start.3 = (bf16[4,80,128]{2,1,0:T(8,128)(2,1)S(1)}, bf16[4,80,128]{2,1,0:T(8,128)(2,1)S(1)}, u32[]{:S(2)}, u32[]{:S(2)}) collective-permute-start(bf16[4,80,128]{2,1,0:T(8,128)(2,1)S(1)} %get-tuple-element.36), channel_id=1, source_target_pairs={{1,2},{2,1},{5,6},{6,5},{9,10},{10,9},{13,14},{14,13},{17,18},{18,... | collective-permute-start | bytes 245768 | tf_op jit(solution)/shard_map/ppermute | solution.py:426
  14.7 2.0 %collective-permute-start = (bf16[4,320,128]{2,1,0:T(8,128)(2,1)S(1)}, bf16[4,320,128]{2,1,0:T(8,128)(2,1)S(1)}, u32[]{:S(2)}, u32[]{:S(2)}) collective-permute-start(bf16[4,320,128]{2,1,0:T(8,128)(2,1)S(1)} %get-tuple-element.33), channel_id=1, source_target_pairs={{0,4},{4,0},{1,5},{5,1},{2,6},{6,2},{3,7},{7,3},{8,12},{12,8},{9,1... | collective-permute-start | bytes 983048 | tf_op jit(solution)/shard_map/ppermute | solution.py:427
  14.8 2.1 %collective-permute-start.1 = (bf16[4,320,128]{2,1,0:T(8,128)(2,1)S(1)}, bf16[4,320,128]{2,1,0:T(8,128)(2,1)S(1)}, u32[]{:S(2)}, u32[]{:S(2)}) collective-permute-start(bf16[4,320,128]{2,1,0:T(8,128)(2,1)S(1)} %get-tuple-element.34), channel_id=1, source_target_pairs={{0,4},{4,0},{1,5},{5,1},{2,6},{6,2},{3,7},{7,3},{8,12},{12,8},{9,1... | collective-permute-start | bytes 983048 | tf_op jit(solution)/shard_map/ppermute | solution.py:427
  20.3 11.9 %collective-permute-start.9 = (bf16[8,320,128]{2,1,0:T(8,128)(2,1)S(1)}, bf16[8,320,128]{2,1,0:T(8,128)(2,1)S(1)}, u32[]{:S(2)}, u32[]{:S(2)}) collective-permute-start(bf16[8,320,128]{2,1,0:T(8,128)(2,1)S(1)} %get-tuple-element.51), channel_id=1, source_target_pairs={{4,8},{8,4},{12,16},{16,12},{20,24},{24,20},{28,32},{32,28},{36,40... | collective-permute-start | bytes 1966088 | tf_op jit(solution)/shard_map/ppermute | solution.py:423
  25.0 5.6 %collective-permute-start.7 = (bf16[4,80,128]{2,1,0:T(8,128)(2,1)S(1)}, bf16[4,80,128]{2,1,0:T(8,128)(2,1)S(1)}, u32[]{:S(2)}, u32[]{:S(2)}) collective-permute-start(bf16[4,80,128]{2,1,0:T(8,128)(2,1)S(1)} %get-tuple-element.49), channel_id=1, source_target_pairs={{0,1},{1,0},{2,3},{3,2},{4,5},{5,4},{6,7},{7,6},{8,9},{9,8},{10,11... | collective-permute-start | bytes 245768 | tf_op jit(solution)/shard_map/ppermute | solution.py:425
  27.5 3.1 %collective-permute-start.8 = (bf16[4,80,128]{2,1,0:T(8,128)(2,1)S(1)}, bf16[4,80,128]{2,1,0:T(8,128)(2,1)S(1)}, u32[]{:S(2)}, u32[]{:S(2)}) collective-permute-start(bf16[4,80,128]{2,1,0:T(8,128)(2,1)S(1)} %get-tuple-element.50), channel_id=1, source_target_pairs={{1,2},{2,1},{5,6},{6,5},{9,10},{10,9},{13,14},{14,13},{17,18},{18,... | collective-permute-start | bytes 245768 | tf_op jit(solution)/shard_map/ppermute | solution.py:426
  28.2 2.5 %collective-permute-start.5 = (bf16[4,320,128]{2,1,0:T(8,128)(2,1)S(1)}, bf16[4,320,128]{2,1,0:T(8,128)(2,1)S(1)}, u32[]{:S(2)}, u32[]{:S(2)}) collective-permute-start(bf16[4,320,128]{2,1,0:T(8,128)(2,1)S(1)} %get-tuple-element.47), channel_id=1, source_target_pairs={{0,4},{4,0},{1,5},{5,1},{2,6},{6,2},{3,7},{7,3},{8,12},{12,8},{9,1... | collective-permute-start | bytes 983048 | tf_op jit(solution)/shard_map/ppermute | solution.py:427
  28.3 2.4 %collective-permute-start.6 = (bf16[4,320,128]{2,1,0:T(8,128)(2,1)S(1)}, bf16[4,320,128]{2,1,0:T(8,128)(2,1)S(1)}, u32[]{:S(2)}, u32[]{:S(2)}) collective-permute-start(bf16[4,320,128]{2,1,0:T(8,128)(2,1)S(1)} %get-tuple-element.48), channel_id=1, source_target_pairs={{0,4},{4,0},{1,5},{5,1},{2,6},{6,2},{3,7},{7,3},{8,12},{12,8},{9,1... | collective-permute-start | bytes 983048 | tf_op jit(solution)/shard_map/ppermute | solution.py:427
  32.6 1.2 %collective-permute-start.10 = (f32[1,384]{1,0:T(1,128)S(1)}, f32[1,384]{1,0:T(1,128)S(1)}, u32[]{:S(2)}, u32[]{:S(2)}) collective-permute-start(f32[1,384]{1,0:T(1,128)S(1)} %get-tuple-element.54), channel_id=1, source_target_pairs={{0,4},{4,0},{1,5},{5,1},{2,6},{6,2},{3,7},{7,3},{8,12},{12,8},{9,1... | collective-permute-start | bytes 4616 | tf_op jit(solution)/shard_map/ppermute | solution.py:465
  66.0 3.3 %collective-permute-start.11 = (f32[1,384]{1,0:T(1,128)S(1)}, f32[1,384]{1,0:T(1,128)S(1)}, u32[]{:S(2)}, u32[]{:S(2)}) collective-permute-start(f32[1,384]{1,0:T(1,128)S(1)} %reduce_sum.12.mine_ref), channel_id=1, source_target_pairs={{0,4},{4,0},{1,5},{5,1},{2,6},{6,2},{3,7},{7,3},{8,12},{12,8},{9,1... | collective-permute-start | bytes 4616 | tf_op jit(solution)/shard_map/ppermute | solution.py:471

commit v6 on v5

--- a/solution.py
+++ b/solution.py
@@ -284,6 +284,15 @@
     gram_ref[...] = gram_rows((rhs_ref, rhs_ref), (rhs_ref, w1_ref), (w1_ref, w1_ref))
 
 
+def landed(e, own_ref, cross_ref, chip_refs, ya_ref, yb_ref):
+    _, odd = core_and_row()
+    y = (e >> 1) & 1
+    n = 2 * (e >> 2) + (e & 1)
+    edge = swap_if(odd == 1, ya_ref[n].astype(jnp.float32), yb_ref[n].astype(jnp.float32))[1 - y]
+    came = cross_ref[e].astype(jnp.float32) + chip_refs[e // 4][e % 4].astype(jnp.float32)
+    return own_ref[e] + came + spread_b(edge, y)
+
+
 def near_kernel(own_ref, chip_ref, chip2_ref, ya_ref, yb_ref, near_ref):
     _, odd = core_and_row()
     for e in range(ELEMS):
@@ -294,19 +303,15 @@
         near_ref[e] = own_ref[e] + chip + spread_b(edge, y)
 
 
-def landed(e, near_ref, cross_ref):
-    return near_ref[e] + cross_ref[e].astype(jnp.float32)
-
-
 def second_kernel(
-    list_hbm, count_ref, near_ref, in_cross, inv_ref, face_ref, hang_ref,
+    list_hbm, count_ref, own_ref, in_cross, in_chip, in_chip2, in_ya, in_yb, inv_ref, face_ref, hang_ref,
     w_ref, tr_ref, cross_ref, acc, app_ref, slot_ref, list_ref, sem,
 ):
     core, _ = core_and_row()
     listing = fetch_list(1, 2 * core - 1, list_hbm, list_ref, count_ref, slot_ref, sem)
 
     def lowered(e):
-        w = landed(e, near_ref, in_cross)
+        w = landed(e, own_ref, in_cross, (in_chip, in_chip2), in_ya, in_yb)
         w_ref[e] = w
         return w.astype(jnp.bfloat16)
 
@@ -316,7 +321,7 @@
 
 def last_kernel(near_ref, in_cross, rhs_ref, w1_ref, early_ref, w_ref, keep_ref, give_ref):
     for e in range(ELEMS):
-        w_ref[e] = landed(e, near_ref, in_cross)
+        w_ref[e] = near_ref[e] + in_cross[e].astype(jnp.float32)
     late = gram_rows((rhs_ref, w_ref), (w1_ref, w_ref), (w_ref, w_ref))
     early = early_ref[...]
     core, _ = core_and_row()
@@ -426,8 +431,7 @@
         in_yb = lax.ppermute(yb, "x", pairs["odd"])
         in_chip = [lax.ppermute(part, "c", [(0, 1), (1, 0)]) for part in (low, high)]
         own, *rest = own_call(weights[2:])
-        near = call(near_kernel, [VMEM] * 5, [shape(FIELD)], [], NEAR_FLOPS, 6 * million)(own, *in_chip, in_ya, in_yb)[0]
-        return (near, in_cross), weights, rest
+        return (own, in_cross, *in_chip, in_ya, in_yb), weights, rest
 
     def side_first():
         return call(
@@ -442,7 +446,7 @@
 
     arrived, weights, _ = exchange(cross, side_first, own_first)
     w1, traces, cross = call(
-        second_kernel, later + [VMEM] * 5, [shape(FIELD)] + sent, [acc, field, *lists], 300 * million, 8 * million,
+        second_kernel, later + [VMEM] * 9, [shape(FIELD)] + sent, [acc, field, *lists], 300 * million, 8 * million,
     )(rows, count, *arrived, inv, face, hang)
 
     def side_second():
@@ -456,10 +460,11 @@
             OWN_FLOPS, 6 * million,
         )(rows, count, *weights[2:], traces, rhs, w1)
 
-    arrived, _, (early,) = exchange(cross, side_second, own_second)
+    (own, in_cross, *others), _, (early,) = exchange(cross, side_second, own_second)
+    near = call(near_kernel, [VMEM] * 5, [shape(FIELD)], [], NEAR_FLOPS, 6 * million)(own, *others)[0]
     w2, keep, give = call(
         last_kernel, [VMEM] * 5, [shape(FIELD), shape((1, 3 * RHS)), shape((1, 3 * RHS))], [], 10 * million, 8 * million
-    )(*arrived, rhs, w1, early)
+    )(near, in_cross, rhs, w1, early)
 
     swap = [(0, 1), (1, 0)]
     part = keep + lax.ppermute(give, "c", swap)

time: 71.6 us -> 70.9 us (level)
  starting transfers between devices: 16.4 us -> 19.3 us
  waiting for transfers between devices: 4.28 us -> 2.16 us
  Pallas kernels: 16.8 us -> 15.1 us
    ppermute x2, starting transfers between devices: 3.75 us -> 5.73 us  [exchange(): in_ya = lax.ppermute(ya, 'x', pairs['even'])]
    ppermute x2, waiting for transfers between devices: 2.08 us -> 0.28 us  [exchange(): in_cross = lax.ppermute(cross, ('z', 'y', 'c'), pairs['cross'])]
    pallas_call x3 -> x2, Pallas kernels: 2.78 us -> 1.79 us  [the longest x1 1.61 us: per_device(): call(second_kernel, later + [VMEM] * 9, [shape(FIELD)] + sent, [acc, fiel...]
where the time goes in v6:
time: 70.9 us; the launch traced here: 70.6 us
  blocking collectives  32.1 us (45%)
  starting transfers between devices  19.3 us (27%)
  Pallas kernels  15.1 us (21%)
  waiting for transfers between devices  2.16 us (3%)
  between operations  1.6 us (2%)
    all_to_all x1, blocking collectives, per_device(): lax.all_to_all(jnp.broadcast_to(part, (chips, 1, 3 * RHS)), ('z', 'y', 'x...  32.1 us
    ppermute x2, starting transfers between devices, exchange(): in_cross = lax.ppermute(cross, ('z', 'y', 'c'), pairs['cross'])  8.23 us
    ppermute x2, starting transfers between devices, exchange(): in_ya = lax.ppermute(ya, 'x', pairs['even'])  5.73 us
    pallas_call x1, Pallas kernels, per_device(): call(first_kernel, [HBM, SMEM] + [HBM] * 4, [shape(FIELD, bf16), shape((E...  3.6 us
    pallas_call x1, Pallas kernels, side_first(): call(side_first_kernel, later + [HBM, HBM, VMEM], beside + [held(3), pack...  3.07 us
    ppermute x1, starting transfers between devices, per_device(): lax.ppermute(mine, 'c', swap)  2.42 us
    pallas_call x1, Pallas kernels, own_second(): call(own_gram_kernel, later + [VMEM] * 5, [shape(FIELD), shape((1, 3 * RH...  1.82 us
    pallas_call x1, Pallas kernels, per_device(): call(functools.partial(combine_kernel, entries), [VMEM] * 5, [shape(FIELD...  1.79 us
  transfers between devices with their start and end apart: 12, of which 5 were waited for; matrix products, arithmetic and copies ran while one was open for 0% of the time, Pallas kernels for 11%

profile of v6, /device:TPU:1, one launch (start us, length us, event | category | flops | bytes accessed | tf_op | source)
XLA Modules:
  0.0 70.6 jit_solution(10768606657917762080)
XLA Ops:
  1.3 3.6 %shard_map.77 = (bf16[8,320,128]{2,1,0:T(8,128)(2,1)S(1)}, bf16[8,320,320]{2,1,0:T(8,128)(2,1)S(1)}, bf16[1,2,2,80,80]{4,3,2,1,0:T(8,128)(2,1)S(1)}, bf16[32,80,...) custom-call(s32[4,32]{1,0:T(4,128)} %bitcast.11, ...), custom_call_target="tpu_custom_call" | custom-call | flops 300000000 | bytes 6000000 | tf_op jit(solution)/shard_map/pallas_call | solution.py:418
  4.9 4.6 %collective-permute-start = (bf16[8,320,128]{2,1,0:T(8,128)(2,1)S(1)}, bf16[8,320,128]{2,1,0:T(8,128)(2,1)S(1)}, u32[]{:S(2)}, u32[]{:S(2)}) collective-permute-start(bf16[8,320,128]{2,1,0:T(8,128)(2,1)S(1)} %get-tuple-element.33), channel_id=1, source_target_pairs={{4,8},{8,4},{12,16},{16,12},{20,24},{24,20},{28,32},{32,28},{36,40... | collective-permute-start | bytes 1966088 | tf_op jit(solution)/shard_map/ppermute | solution.py:428
  9.5 3.1 %shard_map.78 = (bf16[4,320,128]{2,1,0:T(8,128)(2,1)S(1)}, bf16[4,320,128]{2,1,0:T(8,128)(2,1)S(1)}, bf16[4,80,128]{2,1,0:T(8,128)(2,1)S(1)}, bf16[4,80,128]{2,1...) custom-call(s32[4,32]{1,0:T(4,128)} %bitcast.12, ...), custom_call_target="tpu_custom_call" | custom-call | flops 100000000 | bytes 4000000 | tf_op jit(solution)/shard_map/pallas_call | solution.py:437
  12.6 2.1 %collective-permute-start.3 = (bf16[4,80,128]{2,1,0:T(8,128)(2,1)S(1)}, bf16[4,80,128]{2,1,0:T(8,128)(2,1)S(1)}, u32[]{:S(2)}, u32[]{:S(2)}) collective-permute-start(bf16[4,80,128]{2,1,0:T(8,128)(2,1)S(1)} %get-tuple-element.36), channel_id=1, source_target_pairs={{0,1},{1,0},{2,3},{3,2},{4,5},{5,4},{6,7},{7,6},{8,9},{9,8},{10,11... | collective-permute-start | bytes 245768 | tf_op jit(solution)/shard_map/ppermute | solution.py:430
  14.7 0.7 collective-permute-start.4
  15.5 0.5 collective-permute-start.2
  16.0 1.3 %shard_map.79.own_ref = f32[8,320,128]{2,1,0:T(8,128)S(1)} custom-call(s32[4,32]{1,0:T(4,128)} %bitcast.13, s32[1,1]{1,0:T(1,128)S(6)} %copy.10.count_ref, bf16[6,2,2,80,80]{4,3,2,1,0:T(8,128)(2,1)S(1)} %get-tuple-element.31.face_ref, bf16[32,80,320]{2,1,0:T(8,128)(2,1)S(1)} %get-tuple-element.32.hang_ref, bf16[48,80,128]{2,1,0:T(8,128)(2,1)S(1)} %get-tuple-element.30.tr_ref), custom_call_target="tpu_custom_call" | custom-call | flops 4000000000 | bytes 6000000 | tf_op jit(solution)/shard_map/pallas_call | solution.py:443
  17.3 0.2 collective-permute-done.2.in_chip2
  17.5 0.2 collective-permute-done.in_cross
  17.7 1.6 %shard_map.80 = (f32[8,320,128]{2,1,0:T(8,128)S(1)}, bf16[48,80,128]{2,1,0:T(8,128)(2,1)S(1)}, bf16[8,320,128]{2,1,0:T(8,128)(2,1)S(1)}) custom-call(s32[4,32]{1,0:T(4,128)} %bitcast.14, s32[1,1]{1,0:T(1,128)S(6)} %copy.10.count_ref, f32[8,320,128]{2,1,0:T(8,128)S(1)} %shard_map.79.own_ref, bf16[8,320,128]{2,1,0:T(8,128)(2,1)S(1)} %collective-permute-done.in_cross, ...), custom_call_target="tpu_custom_call" | custom-call | flops 300000000 | bytes 8000000 | tf_op jit(solution)/shard_map/pallas_call | solution.py:448
  19.3 3.6 %collective-permute-start.9 = (bf16[8,320,128]{2,1,0:T(8,128)(2,1)S(1)}, bf16[8,320,128]{2,1,0:T(8,128)(2,1)S(1)}, u32[]{:S(2)}, u32[]{:S(2)}) collective-permute-start(bf16[8,320,128]{2,1,0:T(8,128)(2,1)S(1)} %get-tuple-element.51), channel_id=1, source_target_pairs={{4,8},{8,4},{12,16},{16,12},{20,24},{24,20},{28,32},{32,28},{36,40... | collective-permute-start | bytes 1966088 | tf_op jit(solution)/shard_map/ppermute | solution.py:428
  23.0 1.2 %shard_map.82 = (bf16[4,320,128]{2,1,0:T(8,128)(2,1)S(1)}, bf16[4,320,128]{2,1,0:T(8,128)(2,1)S(1)}, bf16[4,80,128]{2,1,0:T(8,128)(2,1)S(1)}, bf16[4,80,128]{2,1,0:T(8,128)(2,1)S(1)}) custom-call(s32[4,32]{1,0:T(4,128)} %bitcast.15, s32[1,1]{1,0:T(1,128)S(6)} %copy.10.count_ref, bf16[3,2,2,80,80]{4,3,2,1,0:T(8,128)(2,1)S(1)} %get-tuple-element.45.face_ref, ...), custom_call_target="tpu_custom_call" | custom-call | flops 100000000 | bytes 4000000 | tf_op jit(solution)/shard_map/pallas_call | solution.py:453
  24.3 3.6 %collective-permute-start.7 = (bf16[4,80,128]{2,1,0:T(8,128)(2,1)S(1)}, bf16[4,80,128]{2,1,0:T(8,128)(2,1)S(1)}, u32[]{:S(2)}, u32[]{:S(2)}) collective-permute-start(bf16[4,80,128]{2,1,0:T(8,128)(2,1)S(1)} %get-tuple-element.49), channel_id=1, source_target_pairs={{0,1},{1,0},{2,3},{3,2},{4,5},{5,4},{6,7},{7,6},{8,9},{9,8},{10,11... | collective-permute-start | bytes 245768 | tf_op jit(solution)/shard_map/ppermute | solution.py:430
  27.8 0.7 collective-permute-start.8
  28.6 0.5 collective-permute-start.6
  29.1 1.8 %shard_map.81 = (f32[8,320,128]{2,1,0:T(8,128)S(1)}, f32[1,384]{1,0:T(1,128)S(1)}) custom-call(s32[4,32]{1,0:T(4,128)} %bitcast.16, s32[1,1]{1,0:T(1,128)S(6)} %copy.10.count_ref, bf16[6,2,2,80,80]{4,3,2,1,0:T(8,128)(2,1)S(1)} %get-tuple-element.31.face_ref, bf16[32,80,320]{2,1,0:T(8,128)(2,1)S(1)} %get-tuple-element.32.hang_ref, ...), custom_call_target="tpu_custom_call" | custom-call | flops 4000000000 | bytes 6000000 | tf_op jit(solution)/shard_map/pallas_call | solution.py:458
  31.0 0.2 shard_map.83.near_ref
  31.3 0.4 shard_map.84
  31.7 0.5 collective-permute-start.10
  32.2 0.8 %collective-permute-done.10 = f32[1,384]{1,0:T(1,128)S(1)} collective-permute-done((f32[1,384]{1,0:T(1,128)S(1)}, f32[1,384]{1,0:T(1,128)S(1)}, u32[]{:S(2)}, u32[]{:S(2)}) %collective-permute-start.10) | collective-permute-done | bytes 1568 | tf_op jit(solution)/shard_map/ppermute | solution.py:470
  33.1 32.1 %all_to_all.5 = f32[128,1,384]{2,1,0:T(1,128)S(1)} all-to-all(f32[128,1,384]{2,1,0:T(1,128)S(1)} %broadcast_in_dim.3), channel_id=1, replica_groups=mesh['z'=8,'y'=4,'c'=2,'x'=4] {'z','y','x'}, dimensions={0} | all-to-all | bytes 393216 | tf_op jit(solution)/shard_map/all_to_all | solution.py:472
  65.4 2.4 %collective-permute-start.11 = (f32[1,384]{1,0:T(1,128)S(1)}, f32[1,384]{1,0:T(1,128)S(1)}, u32[]{:S(2)}, u32[]{:S(2)}) collective-permute-start(f32[1,384]{1,0:T(1,128)S(1)} %reduce_sum.12.mine_ref), channel_id=1, source_target_pairs={{0,4},{4,0},{1,5},{5,1},{2,6},{6,2},{3,7},{7,3},{8,12},{12,8},{9,1... | collective-permute-start | bytes 4616 | tf_op jit(solution)/shard_map/ppermute | solution.py:476
  67.8 0.8 %collective-permute-done.11.other_ref = f32[1,384]{1,0:T(1,128)S(1)} collective-permute-done((f32[1,384]{1,0:T(1,128)S(1)}, f32[1,384]{1,0:T(1,128)S(1)}, u32[]{:S(2)}, u32[]{:S(2)}) %collective-permute-start.11) | collective-permute-done | bytes 1568 | tf_op jit(solution)/shard_map/ppermute | solution.py:476
  68.6 1.8 %shard_map.85 = (f32[8,320,128]{2,1,0:T(8,128)}, f32[3,2,128]{2,1,0:T(2,128)}) custom-call(f32[1,384]{1,0:T(1,128)S(1)} %reduce_sum.12.mine_ref, f32[1,384]{1,0:T(1,128)S(1)} %collective-permute-done.11.other_ref, bf16[8,320,128]{2,1,0:T(8,128)(2,1)S(1)} %get-tuple-element.42.rhs_ref, f32[8,320,128]{2,1,0:T(8,128)S(1)} %get-tuple-element.43.w1_ref, ...), custom_call_target="tpu_custom_call" | custom-call | flops 10000000 | bytes 6000000 | tf_op jit(solution)/shard_map/pallas_call | solution.py:473
  (14 shorter events, 0.6 us)
Async XLA Ops:
  4.9 12.8 %collective-permute-start = (bf16[8,320,128]{2,1,0:T(8,128)(2,1)S(1)}, bf16[8,320,128]{2,1,0:T(8,128)(2,1)S(1)}, u32[]{:S(2)}, u32[]{:S(2)}) collective-permute-start(bf16[8,320,128]{2,1,0:T(8,128)(2,1)S(1)} %get-tuple-element.33), channel_id=1, source_target_pairs={{4,8},{8,4},{12,16},{16,12},{20,24},{24,20},{28,32},{32,28},{36,40... | collective-permute-start | bytes 1966088 | tf_op jit(solution)/shard_map/ppermute | solution.py:428
  12.6 4.7 %collective-permute-start.3 = (bf16[4,80,128]{2,1,0:T(8,128)(2,1)S(1)}, bf16[4,80,128]{2,1,0:T(8,128)(2,1)S(1)}, u32[]{:S(2)}, u32[]{:S(2)}) collective-permute-start(bf16[4,80,128]{2,1,0:T(8,128)(2,1)S(1)} %get-tuple-element.36), channel_id=1, source_target_pairs={{0,1},{1,0},{2,3},{3,2},{4,5},{5,4},{6,7},{7,6},{8,9},{9,8},{10,11... | collective-permute-start | bytes 245768 | tf_op jit(solution)/shard_map/ppermute | solution.py:430
  14.7 2.6 %collective-permute-start.4 = (bf16[4,80,128]{2,1,0:T(8,128)(2,1)S(1)}, bf16[4,80,128]{2,1,0:T(8,128)(2,1)S(1)}, u32[]{:S(2)}, u32[]{:S(2)}) collective-permute-start(bf16[4,80,128]{2,1,0:T(8,128)(2,1)S(1)} %get-tuple-element.37), channel_id=1, source_target_pairs={{1,2},{2,1},{5,6},{6,5},{9,10},{10,9},{13,14},{14,13},{17,18},{18,... | collective-permute-start | bytes 245768 | tf_op jit(solution)/shard_map/ppermute | solution.py:431
  15.4 2.0 %collective-permute-start.1 = (bf16[4,320,128]{2,1,0:T(8,128)(2,1)S(1)}, bf16[4,320,128]{2,1,0:T(8,128)(2,1)S(1)}, u32[]{:S(2)}, u32[]{:S(2)}) collective-permute-start(bf16[4,320,128]{2,1,0:T(8,128)(2,1)S(1)} %get-tuple-element.34), channel_id=1, source_target_pairs={{0,4},{4,0},{1,5},{5,1},{2,6},{6,2},{3,7},{7,3},{8,12},{12,8},{9,1... | collective-permute-start | bytes 983048 | tf_op jit(solution)/shard_map/ppermute | solution.py:432
  15.5 2.1 %collective-permute-start.2 = (bf16[4,320,128]{2,1,0:T(8,128)(2,1)S(1)}, bf16[4,320,128]{2,1,0:T(8,128)(2,1)S(1)}, u32[]{:S(2)}, u32[]{:S(2)}) collective-permute-start(bf16[4,320,128]{2,1,0:T(8,128)(2,1)S(1)} %get-tuple-element.35), channel_id=1, source_target_pairs={{0,4},{4,0},{1,5},{5,1},{2,6},{6,2},{3,7},{7,3},{8,12},{12,8},{9,1... | collective-permute-start | bytes 983048 | tf_op jit(solution)/shard_map/ppermute | solution.py:432
  19.3 11.9 %collective-permute-start.9 = (bf16[8,320,128]{2,1,0:T(8,128)(2,1)S(1)}, bf16[8,320,128]{2,1,0:T(8,128)(2,1)S(1)}, u32[]{:S(2)}, u32[]{:S(2)}) collective-permute-start(bf16[8,320,128]{2,1,0:T(8,128)(2,1)S(1)} %get-tuple-element.51), channel_id=1, source_target_pairs={{4,8},{8,4},{12,16},{16,12},{20,24},{24,20},{28,32},{32,28},{36,40... | collective-permute-start | bytes 1966088 | tf_op jit(solution)/shard_map/ppermute | solution.py:428
  24.3 6.7 %collective-permute-start.7 = (bf16[4,80,128]{2,1,0:T(8,128)(2,1)S(1)}, bf16[4,80,128]{2,1,0:T(8,128)(2,1)S(1)}, u32[]{:S(2)}, u32[]{:S(2)}) collective-permute-start(bf16[4,80,128]{2,1,0:T(8,128)(2,1)S(1)} %get-tuple-element.49), channel_id=1, source_target_pairs={{0,1},{1,0},{2,3},{3,2},{4,5},{5,4},{6,7},{7,6},{8,9},{9,8},{10,11... | collective-permute-start | bytes 245768 | tf_op jit(solution)/shard_map/ppermute | solution.py:430
  27.8 3.1 %collective-permute-start.8 = (bf16[4,80,128]{2,1,0:T(8,128)(2,1)S(1)}, bf16[4,80,128]{2,1,0:T(8,128)(2,1)S(1)}, u32[]{:S(2)}, u32[]{:S(2)}) collective-permute-start(bf16[4,80,128]{2,1,0:T(8,128)(2,1)S(1)} %get-tuple-element.50), channel_id=1, source_target_pairs={{1,2},{2,1},{5,6},{6,5},{9,10},{10,9},{13,14},{14,13},{17,18},{18,... | collective-permute-start | bytes 245768 | tf_op jit(solution)/shard_map/ppermute | solution.py:431
  28.5 2.5 %collective-permute-start.5 = (bf16[4,320,128]{2,1,0:T(8,128)(2,1)S(1)}, bf16[4,320,128]{2,1,0:T(8,128)(2,1)S(1)}, u32[]{:S(2)}, u32[]{:S(2)}) collective-permute-start(bf16[4,320,128]{2,1,0:T(8,128)(2,1)S(1)} %get-tuple-element.47), channel_id=1, source_target_pairs={{0,4},{4,0},{1,5},{5,1},{2,6},{6,2},{3,7},{7,3},{8,12},{12,8},{9,1... | collective-permute-start | bytes 983048 | tf_op jit(solution)/shard_map/ppermute | solution.py:432
  28.6 2.4 %collective-permute-start.6 = (bf16[4,320,128]{2,1,0:T(8,128)(2,1)S(1)}, bf16[4,320,128]{2,1,0:T(8,128)(2,1)S(1)}, u32[]{:S(2)}, u32[]{:S(2)}) collective-permute-start(bf16[4,320,128]{2,1,0:T(8,128)(2,1)S(1)} %get-tuple-element.48), channel_id=1, source_target_pairs={{0,4},{4,0},{1,5},{5,1},{2,6},{6,2},{3,7},{7,3},{8,12},{12,8},{9,1... | collective-permute-start | bytes 983048 | tf_op jit(solution)/shard_map/ppermute | solution.py:432
  31.7 1.3 %collective-permute-start.10 = (f32[1,384]{1,0:T(1,128)S(1)}, f32[1,384]{1,0:T(1,128)S(1)}, u32[]{:S(2)}, u32[]{:S(2)}) collective-permute-start(f32[1,384]{1,0:T(1,128)S(1)} %get-tuple-element.54), channel_id=1, source_target_pairs={{0,4},{4,0},{1,5},{5,1},{2,6},{6,2},{3,7},{7,3},{8,12},{12,8},{9,1... | collective-permute-start | bytes 4616 | tf_op jit(solution)/shard_map/ppermute | solution.py:470
  65.4 3.2 %collective-permute-start.11 = (f32[1,384]{1,0:T(1,128)S(1)}, f32[1,384]{1,0:T(1,128)S(1)}, u32[]{:S(2)}, u32[]{:S(2)}) collective-permute-start(f32[1,384]{1,0:T(1,128)S(1)} %reduce_sum.12.mine_ref), channel_id=1, source_target_pairs={{0,4},{4,0},{1,5},{5,1},{2,6},{6,2},{3,7},{7,3},{8,12},{12,8},{9,1... | collective-permute-start | bytes 4616 | tf_op jit(solution)/shard_map/ppermute | solution.py:476

commit v7 on v6

--- a/solution.py
+++ b/solution.py
@@ -208,34 +208,22 @@
 
 
 def side_first_kernel(
-    list_hbm, count_ref, face_hbm, hang_hbm, tr_ref, chip_ref, chip2_ref, ya_ref, yb_ref, face_ref, hang_ref, own_face_ref, own_hang_ref,
-    acc, slot_ref, list_ref, list_sem, own_slot_ref, sems, hang_sems, own_hang_sems,
+    list_hbm, count_ref, face_hbm, hang_hbm, tr_ref, chip_ref, chip2_ref, ya_ref, yb_ref, face_ref, hang_ref,
+    acc, slot_ref, list_ref, list_sem, sems, hang_sems,
 ):
     core, _ = core_and_row()
     listing = fetch_list(-1, 2 * core - 1, list_hbm, list_ref, count_ref, slot_ref, list_sem)
-    pieces = [
-        face_hbm.at[1, :, :, 0], face_hbm.at[0, :, :, 1], face_hbm.at[:, 1, :, 2],
-        face_hbm.at[:, 0, :, 3], face_hbm.at[:, :, 1, 4], face_hbm.at[:, :, 0, 5],
-    ]
     mine = [face_hbm.at[1 - core, :, :, 1 - core], face_hbm.at[:, 1, :, 3], face_hbm.at[:, 0, :, 2]]
-    copies = [pltpu.make_async_copy(p, face_ref.at[f], sems.at[6 + f]) for f, p in enumerate(mine)]
-    copies += [pltpu.make_async_copy(p, own_face_ref.at[f], sems.at[f]) for f, p in enumerate(pieces)]
-    for copy in copies[:3]:
+    copies = [pltpu.make_async_copy(p, face_ref.at[f], sems.at[f]) for f, p in enumerate(mine)]
+    for copy in copies:
         copy.start()
     n = listing()
     each_slot(n, slot_ref, hang_hbm, hang_ref, hang_sems, lambda copy: copy.start())
-    for copy in copies[3:]:
-        copy.start()
-    own_n = list_slots(0, 1, list_ref, count_ref, own_slot_ref)
-    each_slot(own_n, own_slot_ref, hang_hbm, own_hang_ref, own_hang_sems, lambda copy: copy.start())
-    for copy in copies[:3]:
+    for copy in copies:
         copy.wait()
     edge_fluxes(face_ref, tr_ref, ya_ref, yb_ref)
     each_slot(n, slot_ref, hang_hbm, hang_ref, hang_sems, lambda copy: copy.wait())
     cross_part(acc, (chip_ref, chip2_ref), lambda: n, 1 - core, list_ref, face_ref, hang_ref, tr_ref, slot_ref)
-    for copy in copies[3:]:
-        copy.wait()
-    each_slot(own_n, own_slot_ref, hang_hbm, own_hang_ref, own_hang_sems, lambda copy: copy.wait())
 
 
 def side_second_kernel(
@@ -259,9 +247,28 @@
     own_ref[...] = acc[0:ELEMS]
 
 
-def own_kernel(list_hbm, count_ref, face_ref, hang_ref, tr_ref, own_ref, acc, slot_ref, list_ref, sem):
-    listing = fetch_list(0, 1, list_hbm, list_ref, count_ref, slot_ref, sem)
-    own_part(listing, list_ref, face_ref, hang_ref, tr_ref, own_ref, acc, slot_ref)
+def own_kernel(
+    list_hbm, count_ref, face_hbm, hang_hbm, tr_ref, own_ref, face_ref, hang_ref,
+    acc, slot_ref, list_ref, list_sem, sems, hang_sems,
+):
+    listing = fetch_list(0, 1, list_hbm, list_ref, count_ref, slot_ref, list_sem)
+    pieces = [
+        face_hbm.at[1, :, :, 0], face_hbm.at[0, :, :, 1], face_hbm.at[:, 1, :, 2],
+        face_hbm.at[:, 0, :, 3], face_hbm.at[:, :, 1, 4], face_hbm.at[:, :, 0, 5],
+    ]
+    copies = [pltpu.make_async_copy(p, face_ref.at[f], sems.at[f]) for f, p in enumerate(pieces)]
+    for copy in copies:
+        copy.start()
+    n = listing()
+    each_slot(n, slot_ref, hang_hbm, hang_ref, hang_sems, lambda copy: copy.start())
+    for copy in copies:
+        copy.wait()
+
+    def brought():
+        each_slot(n, slot_ref, hang_hbm, hang_ref, hang_sems, lambda copy: copy.wait())
+        return n
+
+    own_part(brought, list_ref, face_ref, hang_ref, tr_ref, own_ref, acc, slot_ref)
 
 
 def inner(e, *pairs):
@@ -430,35 +437,36 @@
         in_ya = lax.ppermute(ya, "x", pairs["even"])
         in_yb = lax.ppermute(yb, "x", pairs["odd"])
         in_chip = [lax.ppermute(part, "c", [(0, 1), (1, 0)]) for part in (low, high)]
-        own, *rest = own_call(weights[2:])
+        own, *rest = own_call()
         return (own, in_cross, *in_chip, in_ya, in_yb), weights, rest
 
     def side_first():
         return call(
-            side_first_kernel, later + [HBM, HBM, VMEM], beside + [held(3), packed, held(6), packed],
-            [acc, *lists, slots, sems(9), sems(HANG), sems(HANG)], SIDE_FLOPS, 4 * million,
+            side_first_kernel, later + [HBM, HBM, VMEM], beside + [held(3), packed],
+            [acc, *lists, sems(3), sems(HANG)], SIDE_FLOPS, 4 * million,
         )(rows, count, faces, hangs, traces)
 
-    def own_first(weights):
-        return call(own_kernel, later + [VMEM] * 3, [shape(FIELD)], [acc, *lists], OWN_FLOPS, 6 * million)(
-            rows, count, *weights, traces
-        )
-
-    arrived, weights, _ = exchange(cross, side_first, own_first)
+    def own_first():
+        return call(
+            own_kernel, later + [HBM, HBM, VMEM], [shape(FIELD), held(6), packed],
+            [acc, *lists, sems(6), sems(HANG)], OWN_FLOPS, 6 * million,
+        )(rows, count, faces, hangs, traces)
+
+    arrived, weights, own_weights = exchange(cross, side_first, own_first)
     w1, traces, cross = call(
         second_kernel, later + [VMEM] * 9, [shape(FIELD)] + sent, [acc, field, *lists], 300 * million, 8 * million,
     )(rows, count, *arrived, inv, face, hang)
 
     def side_second():
         return call(side_second_kernel, later + [VMEM] * 3, beside, [acc, *lists], SIDE_FLOPS, 4 * million)(
-            rows, count, *weights[:2], traces
+            rows, count, *weights, traces
         )
 
-    def own_second(_):
+    def own_second():
         return call(
             own_gram_kernel, later + [VMEM] * 5, [shape(FIELD), shape((1, 3 * RHS))], [acc, *lists],
             OWN_FLOPS, 6 * million,
-        )(rows, count, *weights[2:], traces, rhs, w1)
+        )(rows, count, *own_weights, traces, rhs, w1)
 
     (own, in_cross, *others), _, (early,) = exchange(cross, side_second, own_second)
     near = call(near_kernel, [VMEM] * 5, [shape(FIELD)], [], NEAR_FLOPS, 6 * million)(own, *others)[0]

time: 70.9 us -> 71.6 us (level)
  starting transfers between devices: 19.3 us -> 17.6 us
  waiting for transfers between devices: 2.16 us -> 3.04 us
  Pallas kernels: 15.1 us -> 15.9 us
    ppermute x2, starting transfers between devices: 5.73 us -> 4.36 us  [exchange(): in_ya = lax.ppermute(ya, 'x', pairs['even'])]
    pallas_call x1, Pallas kernels: 1.32 us -> 2.64 us  [own_first(): call(own_kernel, later + [HBM, HBM, VMEM], [shape(FIELD), held(6), packed...]
    ppermute x2, waiting for transfers between devices: 0.28 us -> 1.06 us  [exchange(): in_cross = lax.ppermute(cross, ('z', 'y', 'c'), pairs['cross'])]
  transfers between devices with their start and end apart: 12 -> 12, of which waited for: 5 -> 4; matrix products, arithmetic and copies ran while one was open for 0% -> 0% of each run, Pallas kernels for 11% -> 12%
where the time goes in v7:
time: 71.6 us; the launch traced here: 71.1 us
  blocking collectives  32.7 us (46%)
  starting transfers between devices  17.6 us (25%)
  Pallas kernels  15.9 us (22%)
  waiting for transfers between devices  3.04 us (4%)
  between operations  1.62 us (2%)
    all_to_all x1, blocking collectives, per_device(): lax.all_to_all(jnp.broadcast_to(part, (chips, 1, 3 * RHS)), ('z', 'y', 'x...  32.7 us
    ppermute x2, starting transfers between devices, exchange(): in_cross = lax.ppermute(cross, ('z', 'y', 'c'), pairs['cross'])  8.23 us
    ppermute x2, starting transfers between devices, exchange(): in_ya = lax.ppermute(ya, 'x', pairs['even'])  4.36 us
    pallas_call x1, Pallas kernels, per_device(): call(first_kernel, [HBM, SMEM] + [HBM] * 4, [shape(FIELD, bf16), shape((E...  3.59 us
    pallas_call x1, Pallas kernels, side_first(): call(side_first_kernel, later + [HBM, HBM, VMEM], beside + [held(3), pack...  2.65 us
    pallas_call x1, Pallas kernels, own_first(): call(own_kernel, later + [HBM, HBM, VMEM], [shape(FIELD), held(6), packed...  2.64 us
    ppermute x1, starting transfers between devices, per_device(): lax.ppermute(mine, 'c', swap)  2.47 us
    pallas_call x1, Pallas kernels, per_device(): call(functools.partial(combine_kernel, entries), [VMEM] * 5, [shape(FIELD...  1.79 us
  transfers between devices with their start and end apart: 12, of which 4 were waited for; matrix products, arithmetic and copies ran while one was open for 0% of the time, Pallas kernels for 12%

profile of v7, /device:TPU:1, one launch (start us, length us, event | category | flops | bytes accessed | tf_op | source)
XLA Modules:
  0.0 71.1 jit_solution(18357034746187182599)
XLA Ops:
  1.3 3.6 %shard_map.77 = (bf16[8,320,128]{2,1,0:T(8,128)(2,1)S(1)}, bf16[8,320,320]{2,1,0:T(8,128)(2,1)S(1)}, bf16[1,2,2,80,80]{4,3,2,1,0:T(8,128)(2,1)S(1)}, bf16[32,80,...) custom-call(s32[4,32]{1,0:T(4,128)} %bitcast.12, ...), custom_call_target="tpu_custom_call" | custom-call | flops 300000000 | bytes 6000000 | tf_op jit(solution)/shard_map/pallas_call | solution.py:425
  4.9 4.6 %collective-permute-start = (bf16[8,320,128]{2,1,0:T(8,128)(2,1)S(1)}, bf16[8,320,128]{2,1,0:T(8,128)(2,1)S(1)}, u32[]{:S(2)}, u32[]{:S(2)}) collective-permute-start(bf16[8,320,128]{2,1,0:T(8,128)(2,1)S(1)} %get-tuple-element.35), channel_id=1, source_target_pairs={{4,8},{8,4},{12,16},{16,12},{20,24},{24,20},{28,32},{32,28},{36,40... | collective-permute-start | bytes 1966088 | tf_op jit(solution)/shard_map/ppermute | solution.py:435
  9.5 2.7 %shard_map.79 = (bf16[4,320,128]{2,1,0:T(8,128)(2,1)S(1)}, bf16[4,320,128]{2,1,0:T(8,128)(2,1)S(1)}, bf16[4,80,128]{2,1,0:T(8,128)(2,1)S(1)}, bf16[4,80,128]{2,1...) custom-call(s32[4,32]{1,0:T(4,128)} %bitcast.13, ...), custom_call_target="tpu_custom_call" | custom-call | flops 100000000 | bytes 4000000 | tf_op jit(solution)/shard_map/pallas_call | solution.py:444
  12.1 1.5 %collective-permute-start.3 = (bf16[4,80,128]{2,1,0:T(8,128)(2,1)S(1)}, bf16[4,80,128]{2,1,0:T(8,128)(2,1)S(1)}, u32[]{:S(2)}, u32[]{:S(2)}) collective-permute-start(bf16[4,80,128]{2,1,0:T(8,128)(2,1)S(1)} %get-tuple-element.38), channel_id=1, source_target_pairs={{0,1},{1,0},{2,3},{3,2},{4,5},{5,4},{6,7},{7,6},{8,9},{9,8},{10,11... | collective-permute-start | bytes 245768 | tf_op jit(solution)/shard_map/ppermute | solution.py:437
  13.6 0.7 collective-permute-start.4
  14.4 0.5 collective-permute-start.2
  14.9 2.6 %shard_map.78 = (f32[8,320,128]{2,1,0:T(8,128)S(1)}, bf16[6,2,2,80,80]{4,3,2,1,0:T(8,128)(2,1)S(1)}, bf16[32,80,320]{2,1,0:T(8,128)(2,1)S(1)}) custom-call(s32[4,32]{1,0:T(4,128)} %bitcast.14, s32[1,1]{1,0:T(1,128)S(6)} %copy.10.count_ref, bf16[2,2,2,6,80,80]{5,4,3,2,1,0:T(8,128)(2,1)} %face_hbm.5, bf16[32,80,320]{2,1,0:T(8,128)(2,1)} %bitcast.9, ...), custom_call_target="tpu_custom_call" | custom-call | flops 4000000000 | bytes 6000000 | tf_op jit(solution)/shard_map/pallas_call | solution.py:450
  17.6 0.2 collective-permute-done.in_cross
  17.7 1.6 %shard_map.80 = (f32[8,320,128]{2,1,0:T(8,128)S(1)}, bf16[48,80,128]{2,1,0:T(8,128)(2,1)S(1)}, bf16[8,320,128]{2,1,0:T(8,128)(2,1)S(1)}) custom-call(s32[4,32]{1,0:T(4,128)} %bitcast.15, s32[1,1]{1,0:T(1,128)S(6)} %copy.10.count_ref, f32[8,320,128]{2,1,0:T(8,128)S(1)} %get-tuple-element.34.own_ref, bf16[8,320,128]{2,1,0:T(8,128)(2,1)S(1)} %collective-permute-done.in_cross, ...), custom_call_target="tpu_custom_call" | custom-call | flops 300000000 | bytes 8000000 | tf_op jit(solution)/shard_map/pallas_call | solution.py:456
  19.3 3.6 %collective-permute-start.9 = (bf16[8,320,128]{2,1,0:T(8,128)(2,1)S(1)}, bf16[8,320,128]{2,1,0:T(8,128)(2,1)S(1)}, u32[]{:S(2)}, u32[]{:S(2)}) collective-permute-start(bf16[8,320,128]{2,1,0:T(8,128)(2,1)S(1)} %get-tuple-element.53), channel_id=1, source_target_pairs={{4,8},{8,4},{12,16},{16,12},{20,24},{24,20},{28,32},{32,28},{36,40... | collective-permute-start | bytes 1966088 | tf_op jit(solution)/shard_map/ppermute | solution.py:435
  23.0 1.2 %shard_map.82 = (bf16[4,320,128]{2,1,0:T(8,128)(2,1)S(1)}, bf16[4,320,128]{2,1,0:T(8,128)(2,1)S(1)}, bf16[4,80,128]{2,1,0:T(8,128)(2,1)S(1)}, bf16[4,80,128]{2,1,0:T(8,128)(2,1)S(1)}) custom-call(s32[4,32]{1,0:T(4,128)} %bitcast.16, s32[1,1]{1,0:T(1,128)S(6)} %copy.10.count_ref, bf16[3,2,2,80,80]{4,3,2,1,0:T(8,128)(2,1)S(1)} %get-tuple-element.47.face_ref, ...), custom_call_target="tpu_custom_call" | custom-call | flops 100000000 | bytes 4000000 | tf_op jit(solution)/shard_map/pallas_call | solution.py:461
  24.3 2.9 %collective-permute-start.7 = (bf16[4,80,128]{2,1,0:T(8,128)(2,1)S(1)}, bf16[4,80,128]{2,1,0:T(8,128)(2,1)S(1)}, u32[]{:S(2)}, u32[]{:S(2)}) collective-permute-start(bf16[4,80,128]{2,1,0:T(8,128)(2,1)S(1)} %get-tuple-element.51), channel_id=1, source_target_pairs={{0,1},{1,0},{2,3},{3,2},{4,5},{5,4},{6,7},{7,6},{8,9},{9,8},{10,11... | collective-permute-start | bytes 245768 | tf_op jit(solution)/shard_map/ppermute | solution.py:437
  27.1 0.7 collective-permute-start.8
  27.9 0.5 collective-permute-start.6
  28.4 1.7 %shard_map.81 = (f32[8,320,128]{2,1,0:T(8,128)S(1)}, f32[1,384]{1,0:T(1,128)S(1)}) custom-call(s32[4,32]{1,0:T(4,128)} %bitcast.17, s32[1,1]{1,0:T(1,128)S(6)} %copy.10.count_ref, bf16[6,2,2,80,80]{4,3,2,1,0:T(8,128)(2,1)S(1)} %get-tuple-element.32.face_ref, bf16[32,80,320]{2,1,0:T(8,128)(2,1)S(1)} %get-tuple-element.33.hang_ref, ...), custom_call_target="tpu_custom_call" | custom-call | flops 4000000000 | bytes 6000000 | tf_op jit(solution)/shard_map/pallas_call | solution.py:466
  30.2 0.2 shard_map.83.near_ref
  30.4 0.9 %collective-permute-done.9.in_cross = bf16[8,320,128]{2,1,0:T(8,128)(2,1)S(1)} collective-permute-done((bf16[8,320,128]{2,1,0:T(8,128)(2,1)S(1)}, bf16[8,320,128]{2,1,0:T(8,128)(2,1)S(1)}, u32[]{:S(2)}, u32[]{:S(2)}) %collective-permute-start.9) | collective-permute-done | bytes 655392 | tf_op jit(solution)/shard_map/ppermute | solution.py:435
  31.3 0.4 shard_map.84
  31.8 1.1 %collective-permute-done.10 = f32[1,384]{1,0:T(1,128)S(1)} collective-permute-done((f32[1,384]{1,0:T(1,128)S(1)}, f32[1,384]{1,0:T(1,128)S(1)}, u32[]{:S(2)}, u32[]{:S(2)}) %collective-permute-start.10) | collective-permute-done | bytes 1568 | tf_op jit(solution)/shard_map/ppermute | solution.py:478
  33.0 32.7 %all_to_all.5 = f32[128,1,384]{2,1,0:T(1,128)S(1)} all-to-all(f32[128,1,384]{2,1,0:T(1,128)S(1)} %broadcast_in_dim.3), channel_id=1, replica_groups=mesh['z'=8,'y'=4,'c'=2,'x'=4] {'z','y','x'}, dimensions={0} | all-to-all | bytes 393216 | tf_op jit(solution)/shard_map/all_to_all | solution.py:480
  65.7 0.2 reduce_sum.11
  65.9 2.5 %collective-permute-start.11 = (f32[1,384]{1,0:T(1,128)S(1)}, f32[1,384]{1,0:T(1,128)S(1)}, u32[]{:S(2)}, u32[]{:S(2)}) collective-permute-start(f32[1,384]{1,0:T(1,128)S(1)} %reduce_sum.12.mine_ref), channel_id=1, source_target_pairs={{0,4},{4,0},{1,5},{5,1},{2,6},{6,2},{3,7},{7,3},{8,12},{12,8},{9,1... | collective-permute-start | bytes 4616 | tf_op jit(solution)/shard_map/ppermute | solution.py:484
  68.4 0.8 %collective-permute-done.11.other_ref = f32[1,384]{1,0:T(1,128)S(1)} collective-permute-done((f32[1,384]{1,0:T(1,128)S(1)}, f32[1,384]{1,0:T(1,128)S(1)}, u32[]{:S(2)}, u32[]{:S(2)}) %collective-permute-start.11) | collective-permute-done | bytes 1568 | tf_op jit(solution)/shard_map/ppermute | solution.py:484
  69.2 1.8 %shard_map.85 = (f32[8,320,128]{2,1,0:T(8,128)}, f32[3,2,128]{2,1,0:T(2,128)}) custom-call(f32[1,384]{1,0:T(1,128)S(1)} %reduce_sum.12.mine_ref, f32[1,384]{1,0:T(1,128)S(1)} %collective-permute-done.11.other_ref, bf16[8,320,128]{2,1,0:T(8,128)(2,1)S(1)} %get-tuple-element.44.rhs_ref, f32[8,320,128]{2,1,0:T(8,128)S(1)} %get-tuple-element.45.w1_ref, ...), custom_call_target="tpu_custom_call" | custom-call | flops 10000000 | bytes 6000000 | tf_op jit(solution)/shard_map/pallas_call | solution.py:481
  (14 shorter events, 0.4 us)
Async XLA Ops:
  4.9 12.9 %collective-permute-start = (bf16[8,320,128]{2,1,0:T(8,128)(2,1)S(1)}, bf16[8,320,128]{2,1,0:T(8,128)(2,1)S(1)}, u32[]{:S(2)}, u32[]{:S(2)}) collective-permute-start(bf16[8,320,128]{2,1,0:T(8,128)(2,1)S(1)} %get-tuple-element.35), channel_id=1, source_target_pairs={{4,8},{8,4},{12,16},{16,12},{20,24},{24,20},{28,32},{32,28},{36,40... | collective-permute-start | bytes 1966088 | tf_op jit(solution)/shard_map/ppermute | solution.py:435
  12.1 5.4 %collective-permute-start.3 = (bf16[4,80,128]{2,1,0:T(8,128)(2,1)S(1)}, bf16[4,80,128]{2,1,0:T(8,128)(2,1)S(1)}, u32[]{:S(2)}, u32[]{:S(2)}) collective-permute-start(bf16[4,80,128]{2,1,0:T(8,128)(2,1)S(1)} %get-tuple-element.38), channel_id=1, source_target_pairs={{0,1},{1,0},{2,3},{3,2},{4,5},{5,4},{6,7},{7,6},{8,9},{9,8},{10,11... | collective-permute-start | bytes 245768 | tf_op jit(solution)/shard_map/ppermute | solution.py:437
  13.6 3.9 %collective-permute-start.4 = (bf16[4,80,128]{2,1,0:T(8,128)(2,1)S(1)}, bf16[4,80,128]{2,1,0:T(8,128)(2,1)S(1)}, u32[]{:S(2)}, u32[]{:S(2)}) collective-permute-start(bf16[4,80,128]{2,1,0:T(8,128)(2,1)S(1)} %get-tuple-element.39), channel_id=1, source_target_pairs={{1,2},{2,1},{5,6},{6,5},{9,10},{10,9},{13,14},{14,13},{17,18},{18,... | collective-permute-start | bytes 245768 | tf_op jit(solution)/shard_map/ppermute | solution.py:438
  14.3 3.3 %collective-permute-start.1 = (bf16[4,320,128]{2,1,0:T(8,128)(2,1)S(1)}, bf16[4,320,128]{2,1,0:T(8,128)(2,1)S(1)}, u32[]{:S(2)}, u32[]{:S(2)}) collective-permute-start(bf16[4,320,128]{2,1,0:T(8,128)(2,1)S(1)} %get-tuple-element.36), channel_id=1, source_target_pairs={{0,4},{4,0},{1,5},{5,1},{2,6},{6,2},{3,7},{7,3},{8,12},{12,8},{9,1... | collective-permute-start | bytes 983048 | tf_op jit(solution)/shard_map/ppermute | solution.py:439
  14.4 3.2 %collective-permute-start.2 = (bf16[4,320,128]{2,1,0:T(8,128)(2,1)S(1)}, bf16[4,320,128]{2,1,0:T(8,128)(2,1)S(1)}, u32[]{:S(2)}, u32[]{:S(2)}) collective-permute-start(bf16[4,320,128]{2,1,0:T(8,128)(2,1)S(1)} %get-tuple-element.37), channel_id=1, source_target_pairs={{0,4},{4,0},{1,5},{5,1},{2,6},{6,2},{3,7},{7,3},{8,12},{12,8},{9,1... | collective-permute-start | bytes 983048 | tf_op jit(solution)/shard_map/ppermute | solution.py:439
  19.3 11.9 %collective-permute-start.9 = (bf16[8,320,128]{2,1,0:T(8,128)(2,1)S(1)}, bf16[8,320,128]{2,1,0:T(8,128)(2,1)S(1)}, u32[]{:S(2)}, u32[]{:S(2)}) collective-permute-start(bf16[8,320,128]{2,1,0:T(8,128)(2,1)S(1)} %get-tuple-element.53), channel_id=1, source_target_pairs={{4,8},{8,4},{12,16},{16,12},{20,24},{24,20},{28,32},{32,28},{36,40... | collective-permute-start | bytes 1966088 | tf_op jit(solution)/shard_map/ppermute | solution.py:435
  24.3 5.9 %collective-permute-start.7 = (bf16[4,80,128]{2,1,0:T(8,128)(2,1)S(1)}, bf16[4,80,128]{2,1,0:T(8,128)(2,1)S(1)}, u32[]{:S(2)}, u32[]{:S(2)}) collective-permute-start(bf16[4,80,128]{2,1,0:T(8,128)(2,1)S(1)} %get-tuple-element.51), channel_id=1, source_target_pairs={{0,1},{1,0},{2,3},{3,2},{4,5},{5,4},{6,7},{7,6},{8,9},{9,8},{10,11... | collective-permute-start | bytes 245768 | tf_op jit(solution)/shard_map/ppermute | solution.py:437
  27.1 3.0 %collective-permute-start.8 = (bf16[4,80,128]{2,1,0:T(8,128)(2,1)S(1)}, bf16[4,80,128]{2,1,0:T(8,128)(2,1)S(1)}, u32[]{:S(2)}, u32[]{:S(2)}) collective-permute-start(bf16[4,80,128]{2,1,0:T(8,128)(2,1)S(1)} %get-tuple-element.52), channel_id=1, source_target_pairs={{1,2},{2,1},{5,6},{6,5},{9,10},{10,9},{13,14},{14,13},{17,18},{18,... | collective-permute-start | bytes 245768 | tf_op jit(solution)/shard_map/ppermute | solution.py:438
  27.8 2.4 %collective-permute-start.5 = (bf16[4,320,128]{2,1,0:T(8,128)(2,1)S(1)}, bf16[4,320,128]{2,1,0:T(8,128)(2,1)S(1)}, u32[]{:S(2)}, u32[]{:S(2)}) collective-permute-start(bf16[4,320,128]{2,1,0:T(8,128)(2,1)S(1)} %get-tuple-element.49), channel_id=1, source_target_pairs={{0,4},{4,0},{1,5},{5,1},{2,6},{6,2},{3,7},{7,3},{8,12},{12,8},{9,1... | collective-permute-start | bytes 983048 | tf_op jit(solution)/shard_map/ppermute | solution.py:439
  27.9 2.3 %collective-permute-start.6 = (bf16[4,320,128]{2,1,0:T(8,128)(2,1)S(1)}, bf16[4,320,128]{2,1,0:T(8,128)(2,1)S(1)}, u32[]{:S(2)}, u32[]{:S(2)}) collective-permute-start(bf16[4,320,128]{2,1,0:T(8,128)(2,1)S(1)} %get-tuple-element.50), channel_id=1, source_target_pairs={{0,4},{4,0},{1,5},{5,1},{2,6},{6,2},{3,7},{7,3},{8,12},{12,8},{9,1... | collective-permute-start | bytes 983048 | tf_op jit(solution)/shard_map/ppermute | solution.py:439
  31.7 1.2 %collective-permute-start.10 = (f32[1,384]{1,0:T(1,128)S(1)}, f32[1,384]{1,0:T(1,128)S(1)}, u32[]{:S(2)}, u32[]{:S(2)}) collective-permute-start(f32[1,384]{1,0:T(1,128)S(1)} %get-tuple-element.56), channel_id=1, source_target_pairs={{0,4},{4,0},{1,5},{5,1},{2,6},{6,2},{3,7},{7,3},{8,12},{12,8},{9,1... | collective-permute-start | bytes 4616 | tf_op jit(solution)/shard_map/ppermute | solution.py:478
  65.9 3.3 %collective-permute-start.11 = (f32[1,384]{1,0:T(1,128)S(1)}, f32[1,384]{1,0:T(1,128)S(1)}, u32[]{:S(2)}, u32[]{:S(2)}) collective-permute-start(f32[1,384]{1,0:T(1,128)S(1)} %reduce_sum.12.mine_ref), channel_id=1, source_target_pairs={{0,4},{4,0},{1,5},{5,1},{2,6},{6,2},{3,7},{7,3},{8,12},{12,8},{9,1... | collective-permute-start | bytes 4616 | tf_op jit(solution)/shard_map/ppermute | solution.py:484
